TPU v7x, 32 devices: a whole 2x2x4 slice. The times are simulated.
32 devices in a mesh: expert: 8 (over z, y), tensor: 4 (over x, core).
Axes of the slice: x: 2, y: 2, z: 4, core: 2. Of those that a mesh axis runs over, the one named last changes fastest.
Arguments:
- tokens: bfloat16 [1024, 8192], P('expert', 'tensor'), may hold values from -25 to 25, as said below
- routes: int32 [1024, 2], P('expert'), may hold values from 0 to 7, all different within a row; in each aligned block of 128 rows (0 to 127, 128 to 255, ...) at most 48 rows name the same one
- norm_gain: float32 [2, 8192], P(None, 'tensor'), may hold values from 0.5 to 1.5
- router_weight: bfloat16 [2, 8192, 8], P(None, 'tensor'), may hold values from -0.0625 to 0.0625
- gate_codes: int32 [2, 8, 4096, 1024], P(None, 'expert', None, 'tensor'), may hold values from 0 to 255
- gate_scales: int32 [2, 8, 64, 1024], P(None, 'expert', None, 'tensor'), may hold values from 8 to 10
- up_codes: int32 [2, 8, 4096, 1024], P(None, 'expert', None, 'tensor'), may hold values from 0 to 255
- up_scales: int32 [2, 8, 64, 1024], P(None, 'expert', None, 'tensor'), may hold values from 8 to 10
- down_codes: int32 [2, 8, 512, 8192], P(None, 'expert', 'tensor'), may hold values from 0 to 255
- down_scales: int32 [2, 8, 8, 8192], P(None, 'expert', 'tensor'), may hold values from 6 to 8
Outputs:
- hidden_out: bfloat16 [1024, 8192], P('expert', 'tensor')
Inputs may be any that keep to these rules, and one draw needn't show every extreme that they name: `routes`: in the rows of one index of expert (128 aligned rows) no expert is named by more than 48 rows, a bound that some block reaches; the two experts of a row differ. `tokens`: token activations.
All inputs are finite; a program needn't handle non-finite values.
Results may differ from a plain program's by a relative error of at most 0.029.
Values may be sent and summed in bfloat16 or wider, within the bound.
No kernel may reach another device: no remote copies, remote signals or barrier semaphores. Data moves between devices by JAX's collectives and lax.ppermute only.
A program may use at most 192 MiB of HBM per device.

v0:
```python
import functools
import math

import jax
import jax.numpy as jnp
import numpy as np
from jax import lax
from jax.experimental import pallas as pl
from jax.experimental.pallas import tpu as pltpu
from jax.sharding import PartitionSpec as P

LAYERS = 2
ORDERS = (
    (
        ("Ra", 0), ("G", 1), ("Wg0", 1), ("Rb", 0), ("V0", 1), ("Wd0", 1), ("Wu0", 1),
        ("Rc", 1), ("Ca", 0), ("Ea", 1), ("Cb", 0), ("Cc", 0), ("Ec", 0), ("Xa", 1), ("Xc", 0),
        ("Eb", 0), ("Xb", 0), ("S", 0), ("Wg1", 1), ("Pc", 0), ("Pa", 1), ("Wu1", 0), ("Pb", 1),
        ("V1", 1),
    ),
    (
        ("Nc", 1), ("Na", 0), ("Ra", 1), ("Nb", 1), ("Rb", 1), ("Ca", 1), ("Ea", 1), ("Xa", 1),
        ("v", 0), ("Rc", 0), ("Wd1", 1), ("Cb", 1), ("Pa", 1), ("Eb", 0), ("S", 1), ("Xb", 1),
        ("Cc", 1), ("Ec", 0), ("Pb", 1), ("Xc", 1), ("Pc", 1),
    ),
)
GROUPS = (
    (("a", (0, 1, 2, 3)), ("b", (4, 5)), ("c", (6, 7))),
    (("a", (0, 1, 2, 3)), ("b", (4, 5)), ("c", (6, 7))),
)
GROUP = 128
BLOCK = 256
MIB = 1 << 20
FIRST = 8
SECOND = 64
NT = (((1,), (1,)), ((), ()))
TN = (((0,), (0,)), ((), ()))


def exchange(shard, axis, mask):
    return lax.ppermute(shard, axis, [(i, i ^ mask) for i in range(lax.axis_size(axis))])


def block_table():
    index = np.arange(BLOCK)
    order = np.concatenate([index[0::2], index[1::2]])
    common = index[:, None] & order[None, :]
    ones = np.array([bin(v).count("1") for v in range(BLOCK)])[common]
    return np.where(ones % 2 == 1, -1.0, 1.0).astype(np.float32)


def split_table(width):
    table = np.zeros((width, width), np.float32)
    for unit in range(width):
        table[unit, unit % 2 * (width // 2) + unit // 2] = 1.0
    return table


def power(exponents):
    return (1 << (16 - exponents)).astype(jnp.float32) * (1.0 / 65536.0)


SHORT = pl.CostEstimate(flops=1000, bytes_accessed=1000, transcendentals=0)


def butterfly(rows, start):
    stride = start
    while stride < len(rows):
        for b in range(len(rows)):
            if b & stride == 0:
                low, high = rows[b], rows[b + stride]
                rows[b], rows[b + stride] = low + high, low - high
        stride *= 2


def in_weights_kernel(first_steps, words_ref, scales_ref, table_ref, out_ref, sums_ref):
    half = BLOCK // 2
    words_group = GROUP // 2
    groups_block = BLOCK // GROUP
    step = pl.program_id(0)
    width = words_ref.shape[3]
    block_count = out_ref.shape[0]

    @pl.when(step < first_steps)
    def _():
        sums = []
        for q in range(FIRST):
            words = words_ref[0, 0, q * half : (q + 1) * half, :]
            pieces = []
            for shift in (0, 4):
                codes = ((words >> shift) & 15).astype(jnp.float32) - 8.0
                for g in range(groups_block):
                    at = q * groups_block + g
                    factor = power(scales_ref[0, 0, at : at + 1, :])
                    pieces.append(codes[g * words_group : (g + 1) * words_group] * factor)
            block = jnp.concatenate(pieces, axis=0).astype(jnp.bfloat16)
            sums.append(jnp.dot(table_ref[...], block, preferred_element_type=jnp.float32))
        butterfly(sums, 1)
        for q in range(FIRST):
            sums_ref[step * FIRST + q] = sums[q]

    @pl.when(step >= first_steps)
    def _():
        base = (step - first_steps) * SECOND
        for r in range(0, SECOND, 16):
            for c in range(0, width, 128):
                for q in range(FIRST):
                    rows = [
                        sums_ref[b * FIRST + q, pl.ds(pl.multiple_of(base + r, 16), 16), c : c + 128]
                        for b in range(block_count // FIRST)
                    ]
                    butterfly(rows, 1)
                    for b, row in enumerate(rows):
                        out_ref[b * FIRST + q, r : r + 16, c : c + 128] = row.astype(jnp.bfloat16)


def in_weights(words, scales, table, layer_idx):
    _, _, word_rows, width = words.shape
    full = 2 * word_rows
    block_count = full // BLOCK
    first_steps = block_count // FIRST
    word_tile = FIRST * BLOCK // 2
    group_tile = FIRST * BLOCK // GROUP
    out = pl.pallas_call(
        functools.partial(in_weights_kernel, first_steps),
        grid=(first_steps + BLOCK // SECOND,),
        in_specs=[
            pl.BlockSpec(
                (1, 1, word_tile, width),
                lambda i: (layer_idx, 0, jnp.minimum(i, first_steps - 1), 0),
            ),
            pl.BlockSpec(
                (1, 1, group_tile, width),
                lambda i: (layer_idx, 0, jnp.minimum(i, first_steps - 1), 0),
            ),
            pl.BlockSpec((BLOCK, BLOCK), lambda i: (0, 0)),
        ],
        out_specs=pl.BlockSpec(
            (block_count, SECOND, width), lambda i: (0, jnp.maximum(i - first_steps, 0), 0)
        ),
        out_shape=jax.ShapeDtypeStruct((block_count, BLOCK, width), jnp.bfloat16),
        scratch_shapes=[pltpu.VMEM((block_count, BLOCK, width), jnp.float32)],
        compiler_params=pltpu.CompilerParams(vmem_limit_bytes=54 * MIB),
        cost_estimate=SHORT,
        name="in_weights",
    )(words, scales, table)
    return out.reshape(full, width)


def down_rows_kernel(words_ref, scales_ref, out_ref):
    words = words_ref[0, 0]
    word_rows = words.shape[0]
    words_group = GROUP // 2
    for part, shift in enumerate((0, 4)):
        codes = ((words >> shift) & 15).astype(jnp.float32) - 8.0
        for g in range(word_rows // words_group):
            factor = power(scales_ref[0, 0, pl.ds(g, 1), :])
            out_ref[pl.ds(part * word_rows + g * words_group, words_group), :] = (
                codes[g * words_group : (g + 1) * words_group] * factor
            ).astype(jnp.bfloat16)


def down_rows(words, scales, layer_idx):
    _, _, word_rows, width = words.shape
    groups = scales.shape[2]
    tile = width // 2
    return pl.pallas_call(
        down_rows_kernel,
        grid=(width // tile,),
        in_specs=[
            pl.BlockSpec((1, 1, word_rows, tile), lambda c: (layer_idx, 0, 0, c)),
            pl.BlockSpec((1, 1, groups, tile), lambda c: (layer_idx, 0, 0, c)),
        ],
        out_specs=pl.BlockSpec((2 * word_rows, tile), lambda c: (0, c)),
        out_shape=jax.ShapeDtypeStruct((2 * word_rows, width), jnp.bfloat16),
        compiler_params=pltpu.CompilerParams(vmem_limit_bytes=54 * MIB),
        cost_estimate=SHORT,
        name="out_weights_rows",
    )(words, scales)


def expert_kernel(part_count, full_width, index_ref, *refs):
    x_refs, refs = refs[:part_count], refs[part_count:]
    gain_refs, refs = refs[:part_count], refs[part_count:]
    split_ref, gate_hbm, up_hbm, down_hbm = refs[:4]
    out_refs, refs = refs[4:6], refs[6:]
    gate_ref, up_ref, down_ref, gate_sem, up_sem, down_sem = refs
    width = x_refs[0].shape[1]
    copies = [[], [], []]
    for j in range(part_count):
        at = pl.ds(pl.multiple_of((index_ref[0] ^ j) * width, width), width)
        copies[0].append(
            pltpu.make_async_copy(gate_hbm.at[at, :], gate_ref.at[j], gate_sem.at[j])
        )
        copies[1].append(pltpu.make_async_copy(up_hbm.at[at, :], up_ref.at[j], up_sem.at[j]))
        copies[2].append(
            pltpu.make_async_copy(down_hbm.at[:, at], down_ref.at[j], down_sem.at[j])
        )
    for j in range(part_count):
        copies[0][j].start()
        copies[1][j].start()
    for j in range(part_count):
        copies[2][j].start()
    gate = up = square = None
    for j in range(part_count):
        wide = x_refs[j][...].astype(jnp.float32)
        rows = (wide * gain_refs[j][...]).astype(jnp.bfloat16)
        part = jnp.sum(wide * wide, axis=1, keepdims=True)
        square = part if j == 0 else square + part
        copies[0][j].wait()
        part = jnp.dot(rows, gate_ref[j], preferred_element_type=jnp.float32)
        gate = part if j == 0 else gate + part
        copies[1][j].wait()
        part = jnp.dot(rows, up_ref[j], preferred_element_type=jnp.float32)
        up = part if j == 0 else up + part
    scale = lax.rsqrt(square / full_width + 1e-05) * (1.0 / math.sqrt(full_width))
    gate = gate * scale
    act = (gate / (1.0 + jnp.exp(-gate))) * (up * scale)
    act = jnp.dot(
        act.astype(jnp.bfloat16), split_ref[...], preferred_element_type=jnp.float32
    ).astype(jnp.bfloat16)
    for j in range(part_count):
        copies[2][j].wait()
        out_refs[j % 2][j // 2] = jnp.dot(
            act, down_ref[j], preferred_element_type=jnp.float32
        ).astype(jnp.bfloat16)


def expert_parts(index, parts, gains, gate_w, up_w, down_w, split):
    part_count = len(parts)
    row_count, width = parts[0].shape
    full_width, hidden = gate_w.shape
    vmem = pl.BlockSpec(memory_space=pltpu.VMEM)
    hbm = pl.BlockSpec(memory_space=pltpu.HBM)
    return pl.pallas_call(
        functools.partial(expert_kernel, part_count, full_width),
        in_specs=[pl.BlockSpec(memory_space=pltpu.SMEM)]
        + [vmem] * (2 * part_count + 1)
        + [hbm] * 3,
        out_specs=[vmem] * 2,
        out_shape=[jax.ShapeDtypeStruct((part_count // 2, row_count, width), jnp.bfloat16)] * 2,
        scratch_shapes=[
            pltpu.VMEM((part_count, width, hidden), jnp.bfloat16),
            pltpu.VMEM((part_count, width, hidden), jnp.bfloat16),
            pltpu.VMEM((part_count, hidden, width), jnp.bfloat16),
            pltpu.SemaphoreType.DMA((part_count,)),
            pltpu.SemaphoreType.DMA((part_count,)),
            pltpu.SemaphoreType.DMA((part_count,)),
        ],
        compiler_params=pltpu.CompilerParams(vmem_limit_bytes=36 * MIB),
        cost_estimate=SHORT,
        name="expert_parts",
    )(index, *parts, *gains, split, gate_w, up_w, down_w)


def add_split_kernel(term_count, *refs):
    total = refs[0][0].astype(jnp.float32)
    for term in refs[1:term_count]:
        total = total + term[0].astype(jnp.float32)
    at = 0
    for out in refs[term_count:]:
        rows = out.shape[0]
        out[...] = total[at : at + rows].astype(jnp.bfloat16)
        at += rows


def add_split(terms, piece_rows):
    _, row_count, width = terms[0].shape
    vmem = pl.BlockSpec(memory_space=pltpu.VMEM)
    count = row_count // piece_rows
    return pl.pallas_call(
        functools.partial(add_split_kernel, len(terms)),
        in_specs=[vmem] * len(terms),
        out_specs=[vmem] * count,
        out_shape=[jax.ShapeDtypeStruct((piece_rows, width), jnp.bfloat16)] * count,
        compiler_params=pltpu.CompilerParams(vmem_limit_bytes=32 * MIB),
        cost_estimate=SHORT,
        name="add_split",
    )(*terms)


def out_weights_kernel(word_rows, *refs):
    out_ref = refs[-1]
    words_group = GROUP // 2
    for source, ref in enumerate(refs[:-1]):
        for g in range(word_rows // words_group):
            words = ref[g * words_group : (g + 1) * words_group, :]
            factor = power(ref[word_rows + g : word_rows + g + 1, :])
            for part, shift in enumerate((0, 4)):
                codes = ((words >> shift) & 15).astype(jnp.float32) - 8.0
                at = part * word_rows + g * words_group
                out_ref[source, at : at + words_group, :] = (codes * factor).astype(jnp.bfloat16)


def out_weights(blocks, word_rows):
    width = blocks[0].shape[1]
    vmem = pl.BlockSpec(memory_space=pltpu.VMEM)
    return pl.pallas_call(
        functools.partial(out_weights_kernel, word_rows),
        in_specs=[vmem] * len(blocks),
        out_specs=vmem,
        out_shape=jax.ShapeDtypeStruct((len(blocks), 2 * word_rows, width), jnp.bfloat16),
        compiler_params=pltpu.CompilerParams(vmem_limit_bytes=24 * MIB),
        cost_estimate=SHORT,
        name="out_weights",
    )(*blocks)


def hidden_kernel(part_count, full_width, index_ref, *refs):
    x_refs, refs = refs[:part_count], refs[part_count:]
    gain_refs, refs = refs[:part_count], refs[part_count:]
    split_ref, gate_hbm, up_hbm, out_ref, gate_ref, up_ref, gate_sem, up_sem = refs
    width = x_refs[0].shape[1]
    copies = []
    for j in range(part_count):
        at = pl.ds(pl.multiple_of((index_ref[0] ^ j) * width, width), width)
        copies.append(
            (
                pltpu.make_async_copy(gate_hbm.at[at, :], gate_ref.at[j], gate_sem.at[j]),
                pltpu.make_async_copy(up_hbm.at[at, :], up_ref.at[j], up_sem.at[j]),
            )
        )
        copies[j][0].start()
        copies[j][1].start()
    gate = up = square = None
    for j in range(part_count):
        wide = x_refs[j][...].astype(jnp.float32)
        rows = (wide * gain_refs[j][...]).astype(jnp.bfloat16)
        part = jnp.sum(wide * wide, axis=1, keepdims=True)
        square = part if j == 0 else square + part
        copies[j][0].wait()
        part = jnp.dot(rows, gate_ref[j], preferred_element_type=jnp.float32)
        gate = part if j == 0 else gate + part
        copies[j][1].wait()
        part = jnp.dot(rows, up_ref[j], preferred_element_type=jnp.float32)
        up = part if j == 0 else up + part
    scale = lax.rsqrt(square / full_width + 1e-05) * (1.0 / math.sqrt(full_width))
    gate = gate * scale
    act = (gate / (1.0 + jnp.exp(-gate))) * (up * scale)
    out_ref[...] = jnp.dot(
        act.astype(jnp.bfloat16), split_ref[...], preferred_element_type=jnp.float32
    ).astype(jnp.bfloat16)


def hidden_units(index, parts, gains, gate_w, up_w, split):
    part_count = len(parts)
    row_count, width = parts[0].shape
    full_width, hidden = gate_w.shape
    vmem = pl.BlockSpec(memory_space=pltpu.VMEM)
    hbm = pl.BlockSpec(memory_space=pltpu.HBM)
    return pl.pallas_call(
        functools.partial(hidden_kernel, part_count, full_width),
        in_specs=[pl.BlockSpec(memory_space=pltpu.SMEM)]
        + [vmem] * (2 * part_count + 1)
        + [hbm] * 2,
        out_specs=vmem,
        out_shape=jax.ShapeDtypeStruct((row_count, hidden), jnp.bfloat16),
        scratch_shapes=[
            pltpu.VMEM((part_count, width, hidden), jnp.bfloat16),
            pltpu.VMEM((part_count, width, hidden), jnp.bfloat16),
            pltpu.SemaphoreType.DMA((part_count,)),
            pltpu.SemaphoreType.DMA((part_count,)),
        ],
        compiler_params=pltpu.CompilerParams(vmem_limit_bytes=24 * MIB),
        cost_estimate=SHORT,
        name="hidden_units",
    )(index, *parts, *gains, split, gate_w, up_w)


def columns_kernel(array_count, *refs):
    act_refs, down_ref, out_refs = refs[:array_count], refs[array_count], refs[array_count + 1 :]
    total = None
    source = 0
    for acts in act_refs:
        for i in range(acts.shape[0]):
            part = jnp.dot(acts[i], down_ref[source], preferred_element_type=jnp.float32)
            total = part if source == 0 else total + part
            source += 1
    at = 0
    for out in out_refs:
        rows = out.shape[0]
        out[...] = total[at : at + rows].astype(jnp.bfloat16)
        at += rows


def columns(acts, down_w, piece_rows):
    row_count = acts[0].shape[1]
    width = down_w.shape[2]
    vmem = pl.BlockSpec(memory_space=pltpu.VMEM)
    count = row_count // piece_rows
    return pl.pallas_call(
        functools.partial(columns_kernel, len(acts)),
        in_specs=[vmem] * (len(acts) + 1),
        out_specs=[vmem] * count,
        out_shape=[jax.ShapeDtypeStruct((piece_rows, width), jnp.bfloat16)] * count,
        compiler_params=pltpu.CompilerParams(vmem_limit_bytes=24 * MIB),
        cost_estimate=SHORT,
        name="columns",
    )(*acts, down_w)


def make_stats(stream, gain, router):
    scaled = (stream * gain).astype(jnp.bfloat16)
    logits = lax.dot_general(router, scaled, NT, preferred_element_type=jnp.float32)
    squares = stream * stream
    high = squares.astype(jnp.bfloat16)
    low = (squares - high.astype(jnp.float32)).astype(jnp.bfloat16)
    ones = jnp.ones((8, stream.shape[1]), jnp.bfloat16)
    square = lax.dot_general(ones, high, NT, preferred_element_type=jnp.float32) + lax.dot_general(
        ones, low, NT, preferred_element_type=jnp.float32
    )
    return logits, square


def fill_slots(picks, rows, slot_refs):
    gathered = jnp.dot(picks, rows, preferred_element_type=jnp.float32)
    capacity = slot_refs[0].shape[0]
    for k, out in enumerate(slot_refs):
        out[...] = gathered[k * capacity : (k + 1) * capacity].astype(jnp.bfloat16)


def enter_kernel(expert_count, me_ref, routes_ref, tokens_ref, gain_ref, router_ref, *refs):
    picks_ref, stats_ref = refs[:2]
    slot_refs = refs[2:]
    token_count = tokens_ref.shape[0]
    capacity = slot_refs[0].shape[0]
    relative = lax.broadcasted_iota(jnp.int32, (expert_count, token_count), 0) ^ me_ref[0]
    first, second = routes_ref[0:1, :], routes_ref[1:2, :]
    member = ((relative == first) | (relative == second)).astype(jnp.float32)
    before = lax.broadcasted_iota(jnp.int32, (token_count, token_count), 0)
    after = lax.broadcasted_iota(jnp.int32, (token_count, token_count), 1)
    earlier = (before < after).astype(jnp.bfloat16)
    ranks = jnp.dot(member.astype(jnp.bfloat16), earlier, preferred_element_type=jnp.float32)
    position = lax.broadcasted_iota(jnp.int32, (capacity, token_count), 0).astype(jnp.float32)
    pieces = [
        jnp.where(position == ranks[k : k + 1, :], member[k : k + 1, :], 0.0)
        for k in range(expert_count)
    ]
    picks = jnp.concatenate(pieces, axis=0).astype(jnp.bfloat16)
    picks_ref[...] = picks
    tokens = tokens_ref[...]
    fill_slots(picks, tokens, slot_refs)
    logits, square = make_stats(tokens.astype(jnp.float32), gain_ref[...], router_ref[...])
    stats_ref[0:expert_count, :] = logits
    stats_ref[expert_count:, :] = square


def enter(me, routes, tokens, gain, router, capacity):
    token_count, width = tokens.shape
    expert_count = router.shape[0]
    vmem = pl.BlockSpec(memory_space=pltpu.VMEM)
    return pl.pallas_call(
        functools.partial(enter_kernel, expert_count),
        in_specs=[pl.BlockSpec(memory_space=pltpu.SMEM)] + [vmem] * 4,
        out_shape=[
            jax.ShapeDtypeStruct((expert_count * capacity, token_count), jnp.bfloat16),
            jax.ShapeDtypeStruct((expert_count + 8, token_count), jnp.float32),
        ]
        + [jax.ShapeDtypeStruct((capacity, width), jnp.bfloat16)] * expert_count,
        compiler_params=pltpu.CompilerParams(vmem_limit_bytes=32 * MIB),
        cost_estimate=SHORT,
        name="enter",
    )(me, routes, tokens, gain, router)


def combine_kernel(expert_count, piece_count, full_width, last, me_ref, *refs):
    routes_ref, picks_ref, stats_ref, stream_ref = refs[:4]
    piece_refs = refs[4 : 4 + piece_count]
    rest = refs[4 + piece_count :]
    token_count = stream_ref.shape[0]
    capacity = picks_ref.shape[0] // expert_count
    first, second = routes_ref[0:1, :], routes_ref[1:2, :]
    logits = stats_ref[0:expert_count, :]
    scale = lax.rsqrt(stats_ref[expert_count : expert_count + 1, :] / full_width + 1e-05)
    expert = lax.broadcasted_iota(jnp.int32, (expert_count, token_count), 0)
    first_logit = jnp.sum(jnp.where(expert == first, logits, 0.0), axis=0, keepdims=True)
    second_logit = jnp.sum(jnp.where(expert == second, logits, 0.0), axis=0, keepdims=True)
    first_weight = 1.0 / (1.0 + jnp.exp((second_logit - first_logit) * scale))
    second_weight = 1.0 - first_weight
    relative = expert ^ me_ref[0]
    weight = jnp.where(relative == first, first_weight, 0.0) + jnp.where(
        relative == second, second_weight, 0.0
    )
    picks = picks_ref[...]
    wide_picks = picks.astype(jnp.float32)
    weighted = jnp.concatenate(
        [
            wide_picks[k * capacity : (k + 1) * capacity] * weight[k : k + 1, :]
            for k in range(expert_count)
        ],
        axis=0,
    )
    high = weighted.astype(jnp.bfloat16)
    low = (weighted - high.astype(jnp.float32)).astype(jnp.bfloat16)
    outs = [piece[...] for piece in piece_refs]
    outs = outs[0] if len(outs) == 1 else jnp.concatenate(outs, axis=0)
    added = lax.dot_general(high, outs, TN, preferred_element_type=jnp.float32)
    added = added + lax.dot_general(low, outs, TN, preferred_element_type=jnp.float32)
    stream = stream_ref[...].astype(jnp.float32) + added
    if last:
        rest[0][...] = stream.astype(jnp.bfloat16)
        return
    gain_ref, router_ref, next_ref, next_stats_ref = rest[:4]
    next_ref[...] = stream
    fill_slots(picks, stream.astype(jnp.bfloat16), rest[4:])
    logits, square = make_stats(stream, gain_ref[...], router_ref[...])
    next_stats_ref[0:expert_count, :] = logits
    next_stats_ref[expert_count:, :] = square


def combine(me, routes, picks, stats, stream, pieces, full_width, following):
    token_count, width = stream.shape
    expert_count = stats.shape[0] - 8
    capacity = picks.shape[0] // expert_count
    if capacity % 16:
        pieces = [jnp.concatenate(pieces, axis=0)]
    vmem = pl.BlockSpec(memory_space=pltpu.VMEM)
    operands = [routes, picks, stats, stream, *pieces]
    if following is None:
        out_shape = [jax.ShapeDtypeStruct((token_count, width), jnp.bfloat16)]
    else:
        operands += following
        out_shape = [
            jax.ShapeDtypeStruct((token_count, width), jnp.float32),
            jax.ShapeDtypeStruct(stats.shape, jnp.float32),
        ] + [jax.ShapeDtypeStruct((capacity, width), jnp.bfloat16)] * expert_count
    return pl.pallas_call(
        functools.partial(
            combine_kernel, expert_count, len(pieces), full_width, following is None
        ),
        in_specs=[pl.BlockSpec(memory_space=pltpu.SMEM)] + [vmem] * len(operands),
        out_shape=out_shape,
        compiler_params=pltpu.CompilerParams(vmem_limit_bytes=32 * MIB),
        cost_estimate=SHORT,
        name="combine",
    )(me, *operands)


def ordered(value, *earlier):
    return lax.optimization_barrier((value, earlier))[0]


def gather_parts(parts, bits):
    parts = dict(parts)
    for bit in bits:
        for j in sorted(parts):
            parts[j ^ 1 << bit] = exchange(parts[j], "tensor", 1 << bit)
    return parts


def per_device(
    tokens,
    routes,
    norm_gain,
    router_weight,
    gate_codes,
    gate_scales,
    up_codes,
    up_scales,
    down_codes,
    down_scales,
):
    part_count = lax.axis_size("tensor")
    expert_count = lax.axis_size("expert")
    bits = part_count.bit_length() - 1
    token_count, width = tokens.shape
    full_width = width * part_count
    hidden = gate_codes.shape[3]
    capacity = 3 * token_count // expert_count
    me = lax.axis_index("expert").astype(jnp.int32).reshape(1)
    index = lax.axis_index("tensor").astype(jnp.int32).reshape(1)
    table = jnp.asarray(block_table(), jnp.bfloat16)
    split = jnp.asarray(split_table(hidden), jnp.bfloat16)
    routes_rows = routes.T
    router_rows = jnp.swapaxes(router_weight, 1, 2)

    picks, stats, *slots = enter(
        me, routes_rows, tokens, norm_gain[0:1], router_rows[0], capacity
    )
    first_bits, core_bits = list(reversed(range(1, bits))), [0]
    stream = tokens

    def cores_added(outs):
        kept, away = outs
        return [(kept, 1), (exchange(away, "tensor", 1), 1)]

    def leaving_of(terms):
        total = sum(array[step :: 2 * step].astype(jnp.float32) for array, step in terms)
        return total.astype(jnp.bfloat16)

    def rest_added(terms, leaving):
        for bit in range(1, bits):
            if bit > 1:
                leaving = leaving_of(terms)
            terms = [(array, 2 * step) for array, step in terms]
            terms.append((exchange(leaving, "tensor", 1 << bit), 1))
        return [array for array, _ in terms]

    def give_back(terms, chunk, returned):
        pieces = add_split(terms, capacity)
        for k, piece in zip(chunk, pieces):
            returned[k] = piece if k == 0 else exchange(piece, "expert", k)
        return pieces

    word_rows = down_codes.shape[2]
    scale_rows = down_scales.shape[2]

    def word_block(layer_idx, j):
        at = (index[0] ^ j) * width
        words = lax.dynamic_slice_in_dim(down_codes[layer_idx, 0], at, width, 1)
        scales = lax.dynamic_slice_in_dim(down_scales[layer_idx, 0], at, width, 1)
        spare = jnp.zeros((8 - scale_rows % 8, width), jnp.int32)
        return jnp.concatenate([words, scales, spare], axis=0)

    top = 1 << bits - 1
    moved = {}

    def swap_first(part, wait):
        going = [j for j in range(part_count) if j & top]
        going = going[part * len(going) // 2 : (part + 1) * len(going) // 2]
        payload = wait(jnp.stack([word_block(LAYERS - 1, j) for j in going]))
        arrived = exchange(payload, "tensor", top)
        for i, j in enumerate(going):
            moved[j ^ top] = [(0, word_block(LAYERS - 1, j ^ top)), (top, arrived[i])]
        return payload

    def swap_rest(wait):
        held, payload = dict(moved), None
        for bit in reversed(range(bits - 1)):
            going = [(j, *item) for j in sorted(held) if j >> bit & 1 for item in held[j]]
            payload = wait(jnp.stack([block for _, _, block in going]))
            arrived = exchange(payload, "tensor", 1 << bit)
            held = {j: list(items) for j, items in held.items() if not j >> bit & 1}
            for i, (j, source, _) in enumerate(going):
                held[j ^ 1 << bit].append((source ^ 1 << bit, arrived[i]))
        return payload, [block for _, block in sorted(held[0], key=lambda item: item[0])]

    final = None
    prepared = {}
    whole_gain = None
    for layer_idx in range(LAYERS):
        unit = max(1, expert_count // 8)
        groups = {
            name: [k for u in units for k in range(u * unit, (u + 1) * unit)]
            for name, units in GROUPS[layer_idx]
        }
        arrived = {0: slots[0]}

        def sent(name, slots=slots):
            for k in groups[name]:
                if k not in arrived:
                    arrived[k] = exchange(slots[k], "expert", k)
            return [arrived[k] for k in groups[name]]

        returned = [None] * expert_count
        rows, parts, outs, terms, acts = {}, {}, {}, {}, {}
        by_words = layer_idx == LAYERS - 1
        token = None
        for step, chained in ORDERS[layer_idx]:
            kind, name = step[0], step[1:]

            def wait(value):
                if not chained or token is None:
                    return value
                return ordered(value, token)

            if kind == "R":
                if name not in rows:
                    rows[name] = jnp.concatenate(wait(sent(name)), axis=0)
                else:
                    rows[name] = wait(rows[name])
                parts[name] = gather_parts({0: rows[name]}, first_bits)
                token = rows[name]
            elif kind == "C":
                held = dict(wait(parts[name]))
                token = [held[j] for j in sorted(held) if j > 0]
                held[0] = ordered(held[0], token)
                parts[name] = gather_parts(held, core_bits)
            elif kind == "E" and by_words:
                token = hidden_units(
                    wait(index),
                    [parts[name][j] for j in range(part_count)],
                    [whole_gain[j][layer_idx : layer_idx + 1] for j in range(part_count)],
                    prepared["g", layer_idx],
                    prepared["u", layer_idx],
                    split,
                )
                acts[name] = [token[None], exchange(token, "tensor", 1)[None]]
            elif kind == "X" and by_words:
                for bit in range(1, bits):
                    held = jnp.concatenate(wait(acts[name]), axis=0)
                    token = held
                    acts[name] = [held, exchange(held, "tensor", 1 << bit)]
            elif kind == "P" and by_words:
                token = columns(wait(acts[name]), prepared["d", layer_idx], capacity)
                for k, piece in zip(groups[name], token):
                    returned[k] = piece if k == 0 else exchange(piece, "expert", k)
            elif kind == "V":
                token = swap_first(int(name), wait)
            elif kind == "v":
                token, final = swap_rest(wait)
            elif kind == "E":
                outs[name] = expert_parts(
                    wait(index),
                    [parts[name][j] for j in range(part_count)],
                    [whole_gain[j][layer_idx : layer_idx + 1] for j in range(part_count)],
                    *[prepared[w, layer_idx] for w in "gud"],
                    split,
                )
                token = outs[name]
                terms[name] = cores_added(outs[name])
            elif kind == "X":
                leaving = wait(leaving_of(terms[name]))
                terms[name] = rest_added(terms[name], leaving)
                token = leaving
            elif kind == "P":
                token = give_back(wait(terms[name]), groups[name], returned)
            elif kind == "Z":
                sent(name, wait(slots))
            elif kind == "N":
                rows[name] = jnp.concatenate(wait(sent(name)), axis=0)
                token = rows[name]
            elif kind == "W":
                at = int(name[1:])
                if name[0] == "d" and at == LAYERS - 1:
                    prepared["d", at] = out_weights(wait(final), word_rows)
                elif name[0] == "d":
                    prepared["d", at] = down_rows(down_codes, wait(down_scales), at)
                else:
                    codes, scales = {"g": (gate_codes, gate_scales), "u": (up_codes, up_scales)}[name[0]]
                    prepared[name[0], at] = in_weights(codes, scales, wait(table), at)
                token = prepared[name[0], at]
            elif kind == "S":
                stats = wait(stats)
                for bit in range(bits):
                    stats = stats + exchange(stats, "tensor", 1 << bit)
                token = stats
            elif kind == "G":
                whole_gain = gather_parts({0: wait(norm_gain)}, first_bits + core_bits)
                token = whole_gain
        following = None
        if layer_idx + 1 < LAYERS:
            following = [norm_gain[layer_idx + 1 : layer_idx + 2], router_rows[layer_idx + 1]]
            ready = [value for (_, at), value in prepared.items() if at > layer_idx]
            me = ordered(me, ready)
        results = combine(
            me, routes_rows, picks, stats, stream, returned, full_width, following
        )
        if following is None:
            return results[0]
        stream, stats, *slots = results


def solution(mesh):
    in_specs = (
        P("expert", "tensor"),
        P("expert", None),
        P(None, "tensor"),
        P(None, "tensor", None),
        P(None, "expert", None, "tensor"),
        P(None, "expert", None, "tensor"),
        P(None, "expert", None, "tensor"),
        P(None, "expert", None, "tensor"),
        P(None, "expert", "tensor", None),
        P(None, "expert", "tensor", None),
    )
    out_specs = P("expert", "tensor")
    return jax.shard_map(
        per_device, mesh=mesh, in_specs=in_specs, out_specs=out_specs, check_vma=False
    )
```

profile of v0, /device:TPU:0, one launch (start us, length us, event | category | flops | bytes accessed | tf_op | source)
XLA Modules:
  0.0 343.4 jit_solution(17729805930429652211)
XLA Ops:
  4.5 1.6 enter.1
  7.3 4.0 %collective-permute-start.11 = (bf16[48,2048]{1,0:T(8,128)(2,1)S(1)}, bf16[48,2048]{1,0:T(8,128)(2,1)S(1)}, u32[]{:S(2)}, u32[]{:S(2)}) collective-permute-start(bf16[48,2048]{1,0:T(8,128)(2,1)S(1)} %get-tuple-element.109), channel_id=1, source_target_pairs={{0,16},{4,20},{8,24},{12,28},{16,0},{20,4},{24,8},{28,12},{1,17},{... | collective-permute-start | bytes 589832 | tf_op jit(solution)/shard_map/ppermute | solution.py:40
  12.9 1.9 collective-permute-start.3
  16.1 4.6 %slice.100 = s32[1,1,128,8192]{3,2,1,0:T(8,128)} slice(s32[2,1,128,8192]{3,2,1,0:T(8,128)} %words_ref.8), slice={[1:2], [0:1], [0:128], [0:8192]} | slice | bytes 8388608 | tf_op jit(solution)/shard_map/slice | solution.py:609
  20.8 2.7 dynamic-slice_bitcast_fusion.1
  23.6 2.0 add_bitcast_fusion.1
  27.7 3.8 %collective-permute-done.4 = bf16[48,2048]{1,0:T(8,128)(2,1)S(1)} collective-permute-done((bf16[48,2048]{1,0:T(8,128)(2,1)S(1)}, bf16[48,2048]{1,0:T(8,128)(2,1)S(1)}, u32[]{:S(2)}, u32[]{:S(2)}) %collective-permute-start.4) | collective-permute-done | bytes 196640 | tf_op jit(solution)/shard_map/ppermute | solution.py:40
  36.4 4.9 %out_weights_rows.1.refs_11_ = bf16[256,8192]{1,0:T(8,128)(2,1)} custom-call(s32[2,1,128,8192]{3,2,1,0:T(8,128)} %words_ref.8, s32[2,1,2,8192]{3,2,1,0:T(2,128)} %scales_ref.7), custom_call_target="tpu_custom_call" | custom-call | flops 1000 | bytes 1000 | tf_op jit(solution)/shard_map/out_weights_rows/pallas_call | solution.py:166
  41.2 7.8 %in_weights.7 = bf16[32,256,256]{2,1,0:T(8,128)(2,1)} custom-call(s32[2,1,4096,256]{3,2,1,0:T(8,128)} %words_ref.9, s32[2,1,64,256]{3,2,1,0:T(8,128)} %scales_ref.8, bf16[256,256]{1,0:T(8,128)(2,1)} %constant.34.clone.table_ref), custom_call_target="tpu_custom_call" | custom-call | flops 1000 | bytes 1000 | tf_op jit(solution)/shard_map/in_weights/pallas_call | solution.py:123
  50.3 8.6 %in_weights.6 = bf16[32,256,256]{2,1,0:T(8,128)(2,1)} custom-call(s32[2,1,4096,256]{3,2,1,0:T(8,128)} %words_ref.7, s32[2,1,64,256]{3,2,1,0:T(8,128)} %scales_ref.6, bf16[256,256]{1,0:T(8,128)(2,1)} %constant.34.clone.table_ref), custom_call_target="tpu_custom_call" | custom-call | flops 1000 | bytes 1000 | tf_op jit(solution)/shard_map/in_weights/pallas_call | solution.py:123
  58.9 3.9 %collective-permute-done.25.refs_2_ = bf16[96,2048]{1,0:T(8,128)(2,1)S(1)} collective-permute-done((bf16[96,2048]{1,0:T(8,128)(2,1)S(1)}, bf16[96,2048]{1,0:T(8,128)(2,1)S(1)}, u32[]{:S(2)}, u32[]{:S(2)}) %collective-permute-start.25) | collective-permute-done | bytes 393248 | tf_op jit(solution)/shard_map/ppermute | solution.py:40
  65.5 2.2 copy-done.5
  71.8 5.7 %expert_parts.5 = (bf16[2,96,2048]{2,1,0:T(8,128)(2,1)S(1)}, bf16[2,96,2048]{2,1,0:T(8,128)(2,1)S(1)}) custom-call(s32[1]{0:T(128)} %bitcast.6.index_ref, bf16[96,2048]{1,0:T(8,128)(2,1)S(1)} %copy-done.15, bf16[96,2048]{1,0:T(8,128)(2,1)S(1)} %collective-permute-done.26.refs_1_, bf16[96,2048]{1,0:T(8,128)(2,1)S(1)} %copy-done.17, ...), custom_call_target="tpu_custom_call" | custom-call | flops 1000 | bytes 1000 | tf_op jit(solution)/shard_map/expert_parts/pallas_call | solution.py:234
  78.2 1.9 collective-permute-done.28.refs_1_
  81.6 4.6 %collective-permute-start.14 = (bf16[48,2048]{1,0:T(8,128)(2,1)}, bf16[48,2048]{1,0:T(8,128)(2,1)}, u32[]{:S(2)}, u32[]{:S(2)}) collective-permute-start(bf16[48,2048]{1,0:T(8,128)(2,1)} %get-tuple-element.116), channel_id=1, source_target_pairs={{0,24},{4,28},{8,16},{12,20},{16,8},{20,12},{24,0},{28,4},{1,25},{... | collective-permute-start | bytes 589832 | tf_op jit(solution)/shard_map/ppermute | solution.py:40
  86.3 9.7 %expert_parts.3 = (bf16[2,192,2048]{2,1,0:T(8,128)(2,1)S(1)}, bf16[2,192,2048]{2,1,0:T(8,128)(2,1)}) custom-call(s32[1]{0:T(128)} %bitcast.6.index_ref, bf16[192,2048]{1,0:T(8,128)(2,1)} %constant_dynamic-update-slice_fusion.refs_0_, bf16[192,2048]{1,0:T(8,128)(2,1)S(1)} %collective-permute-done.6.refs_1_, bf16[192,2048]{1,0:T(8,128)(2,1)} %collective-permute-done.5.refs_2_, ...), custom_call_target="tpu_custom_call" | custom-call | flops 1000 | bytes 1000 | tf_op jit(solution)/shard_map/expert_parts/pallas_call | solution.py:234
  97.2 8.1 %in_weights.5 = bf16[32,256,256]{2,1,0:T(8,128)(2,1)} custom-call(s32[2,1,4096,256]{3,2,1,0:T(8,128)} %words_ref.9, s32[2,1,64,256]{3,2,1,0:T(8,128)} %scales_ref.8, bf16[256,256]{1,0:T(8,128)(2,1)} %constant.34.clone.table_ref), custom_call_target="tpu_custom_call" | custom-call | flops 1000 | bytes 1000 | tf_op jit(solution)/shard_map/in_weights/pallas_call | solution.py:123
  111.8 31.4 %collective-permute-done.16.refs_2_ = bf16[96,2048]{1,0:T(8,128)(2,1)S(1)} collective-permute-done((bf16[96,2048]{1,0:T(8,128)(2,1)S(1)}, bf16[96,2048]{1,0:T(8,128)(2,1)S(1)}, u32[]{:S(2)}, u32[]{:S(2)}) %collective-permute-start.16) | collective-permute-done | bytes 393248 | tf_op jit(solution)/shard_map/ppermute | solution.py:40
  145.5 2.2 copy-done.6
  147.7 5.7 %expert_parts.4 = (bf16[2,96,2048]{2,1,0:T(8,128)(2,1)S(1)}, bf16[2,96,2048]{2,1,0:T(8,128)(2,1)S(1)}) custom-call(s32[1]{0:T(128)} %bitcast.6.index_ref, bf16[96,2048]{1,0:T(8,128)(2,1)S(1)} %constant_dynamic-update-slice_fusion.6.refs_0_, bf16[96,2048]{1,0:T(8,128)(2,1)S(1)} %collective-permute-done.17.refs_1_, ...), custom_call_target="tpu_custom_call" | custom-call | flops 1000 | bytes 1000 | tf_op jit(solution)/shard_map/expert_parts/pallas_call | solution.py:234
  153.6 1.6 pad_add_fusion
  159.5 25.9 %collective-permute-done.21.refs_2_ = bf16[1,96,2048]{2,1,0:T(8,128)(2,1)S(1)} collective-permute-done((bf16[1,96,2048]{2,1,0:T(8,128)(2,1)S(1)}, bf16[1,96,2048]{2,1,0:T(8,128)(2,1)S(1)}, u32[]{:S(2)}, u32[]{:S(2)}) %collective-permute-start.21) | collective-permute-done | bytes 393248 | tf_op jit(solution)/shard_map/ppermute | solution.py:40
  185.6 3.8 %collective-permute-start.32 = (bf16[48,2048]{1,0:T(8,128)(2,1)S(1)}, bf16[48,2048]{1,0:T(8,128)(2,1)S(1)}, u32[]{:S(2)}, u32[]{:S(2)}) collective-permute-start(bf16[48,2048]{1,0:T(8,128)(2,1)S(1)} %get-tuple-element.124), channel_id=1, source_target_pairs={{0,24},{4,28},{8,16},{12,20},{16,8},{20,12},{24,0},{28,4},{1,25},{... | collective-permute-start | bytes 589832 | tf_op jit(solution)/shard_map/ppermute | solution.py:40
  190.8 1.7 add_split.4
  194.6 12.9 %collective-permute-done.31.refs_9_ = bf16[48,2048]{1,0:T(8,128)(2,1)S(1)} collective-permute-done((bf16[48,2048]{1,0:T(8,128)(2,1)S(1)}, bf16[48,2048]{1,0:T(8,128)(2,1)S(1)}, u32[]{:S(2)}, u32[]{:S(2)}) %collective-permute-start.31) | collective-permute-done | bytes 196640 | tf_op jit(solution)/shard_map/ppermute | solution.py:40
  207.5 4.8 %collective-permute-start.24 = (bf16[48,2048]{1,0:T(8,128)(2,1)S(1)}, bf16[48,2048]{1,0:T(8,128)(2,1)S(1)}, u32[]{:S(2)}, u32[]{:S(2)}) collective-permute-start(bf16[48,2048]{1,0:T(8,128)(2,1)S(1)} %get-tuple-element.132), channel_id=1, source_target_pairs={{0,12},{4,8},{8,4},{12,0},{16,28},{20,24},{24,20},{28,16},{1,13},{... | collective-permute-start | bytes 589832 | tf_op jit(solution)/shard_map/ppermute | solution.py:40
  212.3 8.1 %in_weights.4 = bf16[32,256,256]{2,1,0:T(8,128)(2,1)} custom-call(s32[2,1,4096,256]{3,2,1,0:T(8,128)} %words_ref.7, s32[2,1,64,256]{3,2,1,0:T(8,128)} %scales_ref.6, bf16[256,256]{1,0:T(8,128)(2,1)} %constant.34.clone.table_ref), custom_call_target="tpu_custom_call" | custom-call | flops 1000 | bytes 1000 | tf_op jit(solution)/shard_map/in_weights/pallas_call | solution.py:123
  220.4 1.6 combine.2
  222.6 2.9 collective-permute-start.38
  227.0 2.8 collective-permute-done.36
  229.8 3.0 collective-permute-done.37
  232.8 4.3 %collective-permute-done.38 = bf16[48,2048]{1,0:T(8,128)(2,1)S(1)} collective-permute-done((bf16[48,2048]{1,0:T(8,128)(2,1)S(1)}, bf16[48,2048]{1,0:T(8,128)(2,1)S(1)}, u32[]{:S(2)}, u32[]{:S(2)}) %collective-permute-start.38) | collective-permute-done | bytes 196640 | tf_op jit(solution)/shard_map/ppermute | solution.py:40
  237.2 16.4 %collective-permute-done.34 = bf16[48,2048]{1,0:T(8,128)(2,1)S(1)} collective-permute-done((bf16[48,2048]{1,0:T(8,128)(2,1)S(1)}, bf16[48,2048]{1,0:T(8,128)(2,1)S(1)}, u32[]{:S(2)}, u32[]{:S(2)}) %collective-permute-start.34) | collective-permute-done | bytes 196640 | tf_op jit(solution)/shard_map/ppermute | solution.py:40
  255.1 2.3 collective-permute-done.35
  259.6 2.4 collective-permute-done.44
  263.6 14.4 %collective-permute-done.39.refs_2_ = bf16[96,2048]{1,0:T(8,128)(2,1)S(1)} collective-permute-done((bf16[96,2048]{1,0:T(8,128)(2,1)S(1)}, bf16[96,2048]{1,0:T(8,128)(2,1)S(1)}, u32[]{:S(2)}, u32[]{:S(2)}) %collective-permute-start.39) | collective-permute-done | bytes 393248 | tf_op jit(solution)/shard_map/ppermute | solution.py:40
  280.5 4.0 %hidden_units.3 = bf16[96,256]{1,0:T(8,128)(2,1)S(1)} custom-call(s32[1]{0:T(128)} %bitcast.6.index_ref, bf16[96,2048]{1,0:T(8,128)(2,1)S(1)} %pad_maximum_fusion.1.refs_0_, bf16[96,2048]{1,0:T(8,128)(2,1)S(1)} %collective-permute-done.45.refs_1_, bf16[96,2048]{1,0:T(8,128)(2,1)S(1)} %collective-permute-done.39.refs_2_, ...), custom_call_target="tpu_custom_call" | custom-call | flops 1000 | bytes 1000 | tf_op jit(solution)/shard_map/hidden_units/pallas_call | solution.py:350
  287.2 3.0 collective-permute-done.48
  290.8 5.6 %hidden_units.4 = bf16[192,256]{1,0:T(8,128)(2,1)S(1)} custom-call(s32[1]{0:T(128)} %bitcast.6.index_ref, bf16[192,2048]{1,0:T(8,128)(2,1)S(1)} %pad_maximum_fusion.refs_0_, bf16[192,2048]{1,0:T(8,128)(2,1)S(1)} %collective-permute-done.50.refs_1_, bf16[192,2048]{1,0:T(8,128)(2,1)S(1)} %collective-permute-done.49.refs_2_, ...), custom_call_target="tpu_custom_call" | custom-call | flops 1000 | bytes 1000 | tf_op jit(solution)/shard_map/hidden_units/pallas_call | solution.py:350
  298.0 4.2 %hidden_units.5 = bf16[96,256]{1,0:T(8,128)(2,1)S(1)} custom-call(s32[1]{0:T(128)} %bitcast.6.index_ref, bf16[96,2048]{1,0:T(8,128)(2,1)S(1)} %constant_dynamic-update-slice_fusion.8.refs_0_, bf16[96,2048]{1,0:T(8,128)(2,1)S(1)} %collective-permute-done.60.refs_1_, bf16[96,2048]{1,0:T(8,128)(2,1)S(1)} %collective-permute-done.59.refs_2_, ...), custom_call_target="tpu_custom_call" | custom-call | flops 1000 | bytes 1000 | tf_op jit(solution)/shard_map/hidden_units/pallas_call | solution.py:350
  304.8 6.2 %collective-permute-start.63 = (bf16[48,2048]{1,0:T(8,128)(2,1)S(1)}, bf16[48,2048]{1,0:T(8,128)(2,1)S(1)}, u32[]{:S(2)}, u32[]{:S(2)}) collective-permute-start(bf16[48,2048]{1,0:T(8,128)(2,1)S(1)} %get-tuple-element.182), channel_id=1, source_target_pairs={{0,20},{4,16},{8,28},{12,24},{16,4},{20,0},{24,12},{28,8},{1,21},{... | collective-permute-start | bytes 589832 | tf_op jit(solution)/shard_map/ppermute | solution.py:40
  312.9 2.4 collective-permute-start.54
  317.7 4.0 %collective-permute-done.62.refs_8_ = bf16[48,2048]{1,0:T(8,128)(2,1)S(1)} collective-permute-done((bf16[48,2048]{1,0:T(8,128)(2,1)S(1)}, bf16[48,2048]{1,0:T(8,128)(2,1)S(1)}, u32[]{:S(2)}, u32[]{:S(2)}) %collective-permute-start.62) | collective-permute-done | bytes 196640 | tf_op jit(solution)/shard_map/ppermute | solution.py:40
  321.7 1.9 collective-permute-start.66
  323.6 4.2 %collective-permute-done.63.refs_9_ = bf16[48,2048]{1,0:T(8,128)(2,1)S(1)} collective-permute-done((bf16[48,2048]{1,0:T(8,128)(2,1)S(1)}, bf16[48,2048]{1,0:T(8,128)(2,1)S(1)}, u32[]{:S(2)}, u32[]{:S(2)}) %collective-permute-start.63) | collective-permute-done | bytes 196640 | tf_op jit(solution)/shard_map/ppermute | solution.py:40
  327.8 2.0 collective-permute-start.67
  329.8 11.8 %collective-permute-done.56.refs_7_ = bf16[48,2048]{1,0:T(8,128)(2,1)S(1)} collective-permute-done((bf16[48,2048]{1,0:T(8,128)(2,1)S(1)}, bf16[48,2048]{1,0:T(8,128)(2,1)S(1)}, u32[]{:S(2)}, u32[]{:S(2)}) %collective-permute-start.56) | collective-permute-done | bytes 196640 | tf_op jit(solution)/shard_map/ppermute | solution.py:40
  341.6 1.6 combine.3
  (240 shorter events, 65.7 us)
Async XLA Ops:
  7.3 27.4 %collective-permute-start.11 = (bf16[48,2048]{1,0:T(8,128)(2,1)S(1)}, bf16[48,2048]{1,0:T(8,128)(2,1)S(1)}, u32[]{:S(2)}, u32[]{:S(2)}) collective-permute-start(bf16[48,2048]{1,0:T(8,128)(2,1)S(1)} %get-tuple-element.109), channel_id=1, source_target_pairs={{0,16},{4,20},{8,24},{12,28},{16,0},{20,4},{24,8},{28,12},{1,17},{... | collective-permute-start | bytes 589832 | tf_op jit(solution)/shard_map/ppermute | solution.py:40
  11.4 23.4 %collective-permute-start.12 = (bf16[48,2048]{1,0:T(8,128)(2,1)S(1)}, bf16[48,2048]{1,0:T(8,128)(2,1)S(1)}, u32[]{:S(2)}, u32[]{:S(2)}) collective-permute-start(bf16[48,2048]{1,0:T(8,128)(2,1)S(1)} %get-tuple-element.110), channel_id=1, source_target_pairs={{0,20},{4,16},{8,28},{12,24},{16,4},{20,0},{24,12},{28,8},{1,21},{... | collective-permute-start | bytes 589832 | tf_op jit(solution)/shard_map/ppermute | solution.py:40
  12.6 13.6 %collective-permute-start.2 = (bf16[48,2048]{1,0:T(8,128)(2,1)S(1)}, bf16[48,2048]{1,0:T(8,128)(2,1)S(1)}, u32[]{:S(2)}, u32[]{:S(2)}) collective-permute-start(bf16[48,2048]{1,0:T(8,128)(2,1)S(1)} %get-tuple-element.102), channel_id=1, source_target_pairs={{0,4},{4,0},{8,12},{12,8},{16,20},{20,16},{24,28},{28,24},{1,5},{5... | collective-permute-start | bytes 589832 | tf_op jit(solution)/shard_map/ppermute | solution.py:40
  12.9 14.1 %collective-permute-start.3 = (bf16[48,2048]{1,0:T(8,128)(2,1)S(1)}, bf16[48,2048]{1,0:T(8,128)(2,1)S(1)}, u32[]{:S(2)}, u32[]{:S(2)}) collective-permute-start(bf16[48,2048]{1,0:T(8,128)(2,1)S(1)} %get-tuple-element.103), channel_id=1, source_target_pairs={{0,8},{4,12},{8,0},{12,4},{16,24},{20,28},{24,16},{28,20},{1,9},{5... | collective-permute-start | bytes 589832 | tf_op jit(solution)/shard_map/ppermute | solution.py:40
  14.7 16.7 %collective-permute-start.4 = (bf16[48,2048]{1,0:T(8,128)(2,1)S(1)}, bf16[48,2048]{1,0:T(8,128)(2,1)S(1)}, u32[]{:S(2)}, u32[]{:S(2)}) collective-permute-start(bf16[48,2048]{1,0:T(8,128)(2,1)S(1)} %get-tuple-element.104), channel_id=1, source_target_pairs={{0,12},{4,8},{8,4},{12,0},{16,28},{20,24},{24,20},{28,16},{1,13},{... | collective-permute-start | bytes 589832 | tf_op jit(solution)/shard_map/ppermute | solution.py:40
  32.1 16.9 %collective-permute-start.9 = (f32[2,2048]{1,0:T(2,128)S(1)}, f32[2,2048]{1,0:T(2,128)S(1)}, u32[]{:S(2)}, u32[]{:S(2)}) collective-permute-start(f32[2,2048]{1,0:T(2,128)S(1)} %copy-done.44), channel_id=1, source_target_pairs={{0,2},{1,3},{2,0},{3,1},{4,6},{5,7},{6,4},{7,5},{8,10},{9,11},{10,... | collective-permute-start | bytes 49160 | tf_op jit(solution)/shard_map/ppermute | solution.py:40
  33.6 16.0 %collective-permute-start.8 = (f32[2,2048]{1,0:T(2,128)S(1)}, f32[2,2048]{1,0:T(2,128)S(1)}, u32[]{:S(2)}, u32[]{:S(2)}) collective-permute-start(f32[2,2048]{1,0:T(2,128)S(1)} %copy-done.44), channel_id=1, source_target_pairs={{0,1},{1,0},{2,3},{3,2},{4,5},{5,4},{6,7},{7,6},{8,9},{9,8},{10,11... | collective-permute-start | bytes 49160 | tf_op jit(solution)/shard_map/ppermute | solution.py:40
  34.2 43.4 %collective-permute-start.5 = (bf16[192,2048]{1,0:T(8,128)(2,1)}, bf16[192,2048]{1,0:T(8,128)(2,1)}, u32[]{:S(2)}, u32[]{:S(2)}) collective-permute-start(bf16[192,2048]{1,0:T(8,128)(2,1)} %constant_dynamic-update-slice_fusion.refs_0_), channel_id=1, source_target_pairs={{0,2},{1,3},{2,0},{3,1},{4,6},{5,7},{6,4},{7,5},{8,10},{9,11},{10,... | collective-permute-start | bytes 2359304 | tf_op jit(solution)/shard_map/ppermute | solution.py:40
  34.8 28.0 %collective-permute-start.25 = (bf16[96,2048]{1,0:T(8,128)(2,1)S(1)}, bf16[96,2048]{1,0:T(8,128)(2,1)S(1)}, u32[]{:S(2)}, u32[]{:S(2)}) collective-permute-start(bf16[96,2048]{1,0:T(8,128)(2,1)S(1)} %constant_dynamic-update-slice_fusion.4.refs_0_), channel_id=1, source_target_pairs={{0,2},{1,3},{2,0},{3,1},{4,6},{5,7},{6,4},{7,5},{8,10},{9,11},{10,... | collective-permute-start | bytes 1179656 | tf_op jit(solution)/shard_map/ppermute | solution.py:40
  77.6 8.6 %collective-permute-start.6 = (bf16[192,2048]{1,0:T(8,128)(2,1)}, bf16[192,2048]{1,0:T(8,128)(2,1)S(1)}, u32[]{:S(2)}, u32[]{:S(2)}) collective-permute-start(bf16[192,2048]{1,0:T(8,128)(2,1)} %constant_dynamic-update-slice_fusion.refs_0_), channel_id=1, source_target_pairs={{0,1},{1,0},{2,3},{3,2},{4,5},{5,4},{6,7},{7,6},{8,9},{9,8},{10,11... | collective-permute-start | bytes 2359304 | tf_op jit(solution)/shard_map/ppermute | solution.py:40
  81.1 24.2 %collective-permute-start.29 = (bf16[1,96,2048]{2,1,0:T(8,128)(2,1)}, bf16[1,96,2048]{2,1,0:T(8,128)(2,1)}, u32[]{:S(2)}, u32[]{:S(2)}) collective-permute-start(bf16[1,96,2048]{2,1,0:T(8,128)(2,1)} %add_convert_fusion.1), channel_id=1, source_target_pairs={{0,2},{1,3},{2,0},{3,1},{4,6},{5,7},{6,4},{7,5},{8,10},{9,11},{10,... | collective-permute-start | bytes 1179656 | tf_op jit(solution)/shard_map/ppermute | solution.py:40
  81.6 23.7 %collective-permute-start.14 = (bf16[48,2048]{1,0:T(8,128)(2,1)}, bf16[48,2048]{1,0:T(8,128)(2,1)}, u32[]{:S(2)}, u32[]{:S(2)}) collective-permute-start(bf16[48,2048]{1,0:T(8,128)(2,1)} %get-tuple-element.116), channel_id=1, source_target_pairs={{0,24},{4,28},{8,16},{12,20},{16,8},{20,12},{24,0},{28,4},{1,25},{... | collective-permute-start | bytes 589832 | tf_op jit(solution)/shard_map/ppermute | solution.py:40
  86.2 19.1 %collective-permute-start.15 = (bf16[48,2048]{1,0:T(8,128)(2,1)}, bf16[48,2048]{1,0:T(8,128)(2,1)}, u32[]{:S(2)}, u32[]{:S(2)}) collective-permute-start(bf16[48,2048]{1,0:T(8,128)(2,1)} %get-tuple-element.117), channel_id=1, source_target_pairs={{0,28},{4,24},{8,20},{12,16},{16,12},{20,8},{24,4},{28,0},{1,29},{... | collective-permute-start | bytes 589832 | tf_op jit(solution)/shard_map/ppermute | solution.py:40
  97.2 58.4 %collective-permute-start.13 = (bf16[2,192,2048]{2,1,0:T(8,128)(2,1)}, bf16[2,192,2048]{2,1,0:T(8,128)(2,1)}, u32[]{:S(2)}, u32[]{:S(2)}) collective-permute-start(bf16[2,192,2048]{2,1,0:T(8,128)(2,1)} %get-tuple-element.115), channel_id=1, source_target_pairs={{0,1},{1,0},{2,3},{3,2},{4,5},{5,4},{6,7},{7,6},{8,9},{9,8},{10,11... | collective-permute-start | bytes 4718600 | tf_op jit(solution)/shard_map/ppermute | solution.py:40
  107.8 45.8 %collective-permute-start.40 = (s32[1,136,2048]{2,1,0:T(8,128)S(1)}, s32[1,136,2048]{2,1,0:T(8,128)S(1)}, u32[]{:S(2)}, u32[]{:S(2)}) collective-permute-start(s32[1,136,2048]{2,1,0:T(8,128)S(1)} %copy-done.43), channel_id=1, source_target_pairs={{0,2},{1,3},{2,0},{3,1},{4,6},{5,7},{6,4},{7,5},{8,10},{9,11},{10,... | collective-permute-start | bytes 3342344 | tf_op jit(solution)/shard_map/ppermute | solution.py:40
  111.2 32.0 %collective-permute-start.16 = (bf16[96,2048]{1,0:T(8,128)(2,1)S(1)}, bf16[96,2048]{1,0:T(8,128)(2,1)S(1)}, u32[]{:S(2)}, u32[]{:S(2)}) collective-permute-start(bf16[96,2048]{1,0:T(8,128)(2,1)S(1)} %constant_dynamic-update-slice_fusion.6.refs_0_), channel_id=1, source_target_pairs={{0,2},{1,3},{2,0},{3,1},{4,6},{5,7},{6,4},{7,5},{8,10},{9,11},{10,... | collective-permute-start | bytes 1179656 | tf_op jit(solution)/shard_map/ppermute | solution.py:40
  155.2 106.7 %collective-permute-start.41 = (s32[2,136,2048]{2,1,0:T(8,128)}, s32[2,136,2048]{2,1,0:T(8,128)S(1)}, u32[]{:S(2)}, u32[]{:S(2)}) collective-permute-start(s32[2,136,2048]{2,1,0:T(8,128)} %pad_add_fusion), channel_id=1, source_target_pairs={{0,1},{1,0},{2,3},{3,2},{4,5},{5,4},{6,7},{7,6},{8,9},{9,8},{10,11... | collective-permute-start | bytes 6684680 | tf_op jit(solution)/shard_map/ppermute | solution.py:40
  157.1 32.3 %collective-permute-start.19 = (bf16[1,192,2048]{2,1,0:T(8,128)(2,1)S(1)}, bf16[1,192,2048]{2,1,0:T(8,128)(2,1)S(1)}, u32[]{:S(2)}, u32[]{:S(2)}) collective-permute-start(bf16[1,192,2048]{2,1,0:T(8,128)(2,1)S(1)} %add_convert_fusion), channel_id=1, source_target_pairs={{0,2},{1,3},{2,0},{3,1},{4,6},{5,7},{6,4},{7,5},{8,10},{9,11},{10,... | collective-permute-start | bytes 2359304 | tf_op jit(solution)/shard_map/ppermute | solution.py:40
  158.8 26.6 %collective-permute-start.21 = (bf16[1,96,2048]{2,1,0:T(8,128)(2,1)S(1)}, bf16[1,96,2048]{2,1,0:T(8,128)(2,1)S(1)}, u32[]{:S(2)}, u32[]{:S(2)}) collective-permute-start(bf16[1,96,2048]{2,1,0:T(8,128)(2,1)S(1)} %add_convert_fusion.2), channel_id=1, source_target_pairs={{0,2},{1,3},{2,0},{3,1},{4,6},{5,7},{6,4},{7,5},{8,10},{9,11},{10,... | collective-permute-start | bytes 1179656 | tf_op jit(solution)/shard_map/ppermute | solution.py:40
  159.4 26.2 %collective-permute-start = (f32[16,128]{1,0:T(8,128)S(1)}, f32[16,128]{1,0:T(8,128)S(1)}, u32[]{:S(2)}, u32[]{:S(2)}) collective-permute-start(f32[16,128]{1,0:T(8,128)S(1)} %copy-done.40), channel_id=1, source_target_pairs={{0,1},{1,0},{2,3},{3,2},{4,5},{5,4},{6,7},{7,6},{8,9},{9,8},{10,11... | collective-permute-start | bytes 24584 | tf_op jit(solution)/shard_map/ppermute | solution.py:40
  159.4 34.7 %collective-permute-start.30 = (bf16[48,2048]{1,0:T(8,128)(2,1)S(1)}, bf16[48,2048]{1,0:T(8,128)(2,1)S(1)}, u32[]{:S(2)}, u32[]{:S(2)}) collective-permute-start(bf16[48,2048]{1,0:T(8,128)(2,1)S(1)} %get-tuple-element.139), channel_id=1, source_target_pairs={{0,16},{4,20},{8,24},{12,28},{16,0},{20,4},{24,8},{28,12},{1,17},{... | collective-permute-start | bytes 589832 | tf_op jit(solution)/shard_map/ppermute | solution.py:40
  185.4 22.1 %collective-permute-start.31 = (bf16[48,2048]{1,0:T(8,128)(2,1)S(1)}, bf16[48,2048]{1,0:T(8,128)(2,1)S(1)}, u32[]{:S(2)}, u32[]{:S(2)}) collective-permute-start(bf16[48,2048]{1,0:T(8,128)(2,1)S(1)} %get-tuple-element.140), channel_id=1, source_target_pairs={{0,20},{4,16},{8,28},{12,24},{16,4},{20,0},{24,12},{28,8},{1,21},{... | collective-permute-start | bytes 589832 | tf_op jit(solution)/shard_map/ppermute | solution.py:40
  185.6 21.9 %collective-permute-start.32 = (bf16[48,2048]{1,0:T(8,128)(2,1)S(1)}, bf16[48,2048]{1,0:T(8,128)(2,1)S(1)}, u32[]{:S(2)}, u32[]{:S(2)}) collective-permute-start(bf16[48,2048]{1,0:T(8,128)(2,1)S(1)} %get-tuple-element.124), channel_id=1, source_target_pairs={{0,24},{4,28},{8,16},{12,20},{16,8},{20,12},{24,0},{28,4},{1,25},{... | collective-permute-start | bytes 589832 | tf_op jit(solution)/shard_map/ppermute | solution.py:40
  193.0 27.3 %collective-permute-start.33 = (bf16[48,2048]{1,0:T(8,128)(2,1)S(1)}, bf16[48,2048]{1,0:T(8,128)(2,1)S(1)}, u32[]{:S(2)}, u32[]{:S(2)}) collective-permute-start(bf16[48,2048]{1,0:T(8,128)(2,1)S(1)} %get-tuple-element.125), channel_id=1, source_target_pairs={{0,28},{4,24},{8,20},{12,16},{16,12},{20,8},{24,4},{28,0},{1,29},{... | collective-permute-start | bytes 589832 | tf_op jit(solution)/shard_map/ppermute | solution.py:40
  194.1 26.3 %collective-permute-start.22 = (bf16[48,2048]{1,0:T(8,128)(2,1)S(1)}, bf16[48,2048]{1,0:T(8,128)(2,1)S(1)}, u32[]{:S(2)}, u32[]{:S(2)}) collective-permute-start(bf16[48,2048]{1,0:T(8,128)(2,1)S(1)} %get-tuple-element.130), channel_id=1, source_target_pairs={{0,4},{4,0},{8,12},{12,8},{16,20},{20,16},{24,28},{28,24},{1,5},{5... | collective-permute-start | bytes 589832 | tf_op jit(solution)/shard_map/ppermute | solution.py:40
  207.5 12.9 %collective-permute-start.23 = (bf16[48,2048]{1,0:T(8,128)(2,1)S(1)}, bf16[48,2048]{1,0:T(8,128)(2,1)S(1)}, u32[]{:S(2)}, u32[]{:S(2)}) collective-permute-start(bf16[48,2048]{1,0:T(8,128)(2,1)S(1)} %get-tuple-element.131), channel_id=1, source_target_pairs={{0,8},{4,12},{8,0},{12,4},{16,24},{20,28},{24,16},{28,20},{1,9},{5... | collective-permute-start | bytes 589832 | tf_op jit(solution)/shard_map/ppermute | solution.py:40
  207.5 12.9 %collective-permute-start.24 = (bf16[48,2048]{1,0:T(8,128)(2,1)S(1)}, bf16[48,2048]{1,0:T(8,128)(2,1)S(1)}, u32[]{:S(2)}, u32[]{:S(2)}) collective-permute-start(bf16[48,2048]{1,0:T(8,128)(2,1)S(1)} %get-tuple-element.132), channel_id=1, source_target_pairs={{0,12},{4,8},{8,4},{12,0},{16,28},{20,24},{24,20},{28,16},{1,13},{... | collective-permute-start | bytes 589832 | tf_op jit(solution)/shard_map/ppermute | solution.py:40
  222.5 10.3 %collective-permute-start.37 = (bf16[48,2048]{1,0:T(8,128)(2,1)S(1)}, bf16[48,2048]{1,0:T(8,128)(2,1)S(1)}, u32[]{:S(2)}, u32[]{:S(2)}) collective-permute-start(bf16[48,2048]{1,0:T(8,128)(2,1)S(1)} %get-tuple-element.146), channel_id=1, source_target_pairs={{0,8},{4,12},{8,0},{12,4},{16,24},{20,28},{24,16},{28,20},{1,9},{5... | collective-permute-start | bytes 589832 | tf_op jit(solution)/shard_map/ppermute | solution.py:40
  222.6 14.5 %collective-permute-start.38 = (bf16[48,2048]{1,0:T(8,128)(2,1)S(1)}, bf16[48,2048]{1,0:T(8,128)(2,1)S(1)}, u32[]{:S(2)}, u32[]{:S(2)}) collective-permute-start(bf16[48,2048]{1,0:T(8,128)(2,1)S(1)} %get-tuple-element.147), channel_id=1, source_target_pairs={{0,12},{4,8},{8,4},{12,0},{16,28},{20,24},{24,20},{28,16},{1,13},{... | collective-permute-start | bytes 589832 | tf_op jit(solution)/shard_map/ppermute | solution.py:40
  225.5 36.6 %collective-permute-start.42 = (s32[1,136,2048]{2,1,0:T(8,128)S(1)}, s32[1,136,2048]{2,1,0:T(8,128)S(1)}, u32[]{:S(2)}, u32[]{:S(2)}) collective-permute-start(s32[1,136,2048]{2,1,0:T(8,128)S(1)} %copy-done.42), channel_id=1, source_target_pairs={{0,2},{1,3},{2,0},{3,1},{4,6},{5,7},{6,4},{7,5},{8,10},{9,11},{10,... | collective-permute-start | bytes 3342344 | tf_op jit(solution)/shard_map/ppermute | solution.py:40
  229.8 29.1 %collective-permute-start.43 = (bf16[48,2048]{1,0:T(8,128)(2,1)S(1)}, bf16[48,2048]{1,0:T(8,128)(2,1)S(1)}, u32[]{:S(2)}, u32[]{:S(2)}) collective-permute-start(bf16[48,2048]{1,0:T(8,128)(2,1)S(1)} %get-tuple-element.151), channel_id=1, source_target_pairs={{0,24},{4,28},{8,16},{12,20},{16,8},{20,12},{24,0},{28,4},{1,25},{... | collective-permute-start | bytes 589832 | tf_op jit(solution)/shard_map/ppermute | solution.py:40
  232.8 20.8 %collective-permute-start.34 = (bf16[48,2048]{1,0:T(8,128)(2,1)S(1)}, bf16[48,2048]{1,0:T(8,128)(2,1)S(1)}, u32[]{:S(2)}, u32[]{:S(2)}) collective-permute-start(bf16[48,2048]{1,0:T(8,128)(2,1)S(1)} %get-tuple-element.142), channel_id=1, source_target_pairs={{0,16},{4,20},{8,24},{12,28},{16,0},{20,4},{24,8},{28,12},{1,17},{... | collective-permute-start | bytes 589832 | tf_op jit(solution)/shard_map/ppermute | solution.py:40
  237.1 20.3 %collective-permute-start.35 = (bf16[48,2048]{1,0:T(8,128)(2,1)S(1)}, bf16[48,2048]{1,0:T(8,128)(2,1)S(1)}, u32[]{:S(2)}, u32[]{:S(2)}) collective-permute-start(bf16[48,2048]{1,0:T(8,128)(2,1)S(1)} %get-tuple-element.143), channel_id=1, source_target_pairs={{0,20},{4,16},{8,28},{12,24},{16,4},{20,0},{24,12},{28,8},{1,21},{... | collective-permute-start | bytes 589832 | tf_op jit(solution)/shard_map/ppermute | solution.py:40
  253.6 8.4 %collective-permute-start.44 = (bf16[48,2048]{1,0:T(8,128)(2,1)S(1)}, bf16[48,2048]{1,0:T(8,128)(2,1)S(1)}, u32[]{:S(2)}, u32[]{:S(2)}) collective-permute-start(bf16[48,2048]{1,0:T(8,128)(2,1)S(1)} %get-tuple-element.152), channel_id=1, source_target_pairs={{0,28},{4,24},{8,20},{12,16},{16,12},{20,8},{24,4},{28,0},{1,29},{... | collective-permute-start | bytes 589832 | tf_op jit(solution)/shard_map/ppermute | solution.py:40
  257.4 21.1 %collective-permute-start.49 = (bf16[192,2048]{1,0:T(8,128)(2,1)S(1)}, bf16[192,2048]{1,0:T(8,128)(2,1)S(1)}, u32[]{:S(2)}, u32[]{:S(2)}) collective-permute-start(bf16[192,2048]{1,0:T(8,128)(2,1)S(1)} %pad_maximum_fusion.refs_0_), channel_id=1, source_target_pairs={{0,2},{1,3},{2,0},{3,1},{4,6},{5,7},{6,4},{7,5},{8,10},{9,11},{10,... | collective-permute-start | bytes 2359304 | tf_op jit(solution)/shard_map/ppermute | solution.py:40
  258.9 19.0 %collective-permute-start.39 = (bf16[96,2048]{1,0:T(8,128)(2,1)S(1)}, bf16[96,2048]{1,0:T(8,128)(2,1)S(1)}, u32[]{:S(2)}, u32[]{:S(2)}) collective-permute-start(bf16[96,2048]{1,0:T(8,128)(2,1)S(1)} %pad_maximum_fusion.1.refs_0_), channel_id=1, source_target_pairs={{0,2},{1,3},{2,0},{3,1},{4,6},{5,7},{6,4},{7,5},{8,10},{9,11},{10,... | collective-permute-start | bytes 1179656 | tf_op jit(solution)/shard_map/ppermute | solution.py:40
  278.5 12.3 %collective-permute-start.50 = (bf16[192,2048]{1,0:T(8,128)(2,1)S(1)}, bf16[192,2048]{1,0:T(8,128)(2,1)S(1)}, u32[]{:S(2)}, u32[]{:S(2)}) collective-permute-start(bf16[192,2048]{1,0:T(8,128)(2,1)S(1)} %pad_maximum_fusion.refs_0_), channel_id=1, source_target_pairs={{0,1},{1,0},{2,3},{3,2},{4,5},{5,4},{6,7},{7,6},{8,9},{9,8},{10,11... | collective-permute-start | bytes 2359304 | tf_op jit(solution)/shard_map/ppermute | solution.py:40
  278.5 12.3 %collective-permute-start.51 = (bf16[192,2048]{1,0:T(8,128)(2,1)S(1)}, bf16[192,2048]{1,0:T(8,128)(2,1)S(1)}, u32[]{:S(2)}, u32[]{:S(2)}) collective-permute-start(bf16[192,2048]{1,0:T(8,128)(2,1)S(1)} %collective-permute-done.49.refs_2_), channel_id=1, source_target_pairs={{0,1},{1,0},{2,3},{3,2},{4,5},{5,4},{6,7},{7,6},{8,9},{9,8},{10,11... | collective-permute-start | bytes 2359304 | tf_op jit(solution)/shard_map/ppermute | solution.py:40
  279.0 11.2 %collective-permute-start.59 = (bf16[96,2048]{1,0:T(8,128)(2,1)S(1)}, bf16[96,2048]{1,0:T(8,128)(2,1)S(1)}, u32[]{:S(2)}, u32[]{:S(2)}) collective-permute-start(bf16[96,2048]{1,0:T(8,128)(2,1)S(1)} %constant_dynamic-update-slice_fusion.8.refs_0_), channel_id=1, source_target_pairs={{0,2},{1,3},{2,0},{3,1},{4,6},{5,7},{6,4},{7,5},{8,10},{9,11},{10,... | collective-permute-start | bytes 1179656 | tf_op jit(solution)/shard_map/ppermute | solution.py:40
  302.3 8.8 %collective-permute-start.64 = (bf16[96,256]{1,0:T(8,128)(2,1)S(1)}, bf16[96,256]{1,0:T(8,128)(2,1)S(1)}, u32[]{:S(2)}, u32[]{:S(2)}) collective-permute-start(bf16[96,256]{1,0:T(8,128)(2,1)S(1)} %hidden_units.5), channel_id=1, source_target_pairs={{0,1},{1,0},{2,3},{3,2},{4,5},{5,4},{6,7},{7,6},{8,9},{9,8},{10,11... | collective-permute-start | bytes 147464 | tf_op jit(solution)/shard_map/ppermute | solution.py:40
  302.5 9.4 %collective-permute-start.53 = (bf16[2,192,256]{2,1,0:T(8,128)(2,1)S(1)}, bf16[2,192,256]{2,1,0:T(8,128)(2,1)S(1)}, u32[]{:S(2)}, u32[]{:S(2)}) collective-permute-start(bf16[2,192,256]{2,1,0:T(8,128)(2,1)S(1)} %constant_dynamic-update-slice_fusion.10.refs_0_), channel_id=1, source_target_pairs={{0,2},{1,3},{2,0},{3,1},{4,6},{5,7},{6,4},{7,5},{8,10},{9,11},{10,... | collective-permute-start | bytes 589832 | tf_op jit(solution)/shard_map/ppermute | solution.py:40
  304.6 17.1 %collective-permute-start.62 = (bf16[48,2048]{1,0:T(8,128)(2,1)S(1)}, bf16[48,2048]{1,0:T(8,128)(2,1)S(1)}, u32[]{:S(2)}, u32[]{:S(2)}) collective-permute-start(bf16[48,2048]{1,0:T(8,128)(2,1)S(1)} %get-tuple-element.181), channel_id=1, source_target_pairs={{0,16},{4,20},{8,24},{12,28},{16,0},{20,4},{24,8},{28,12},{1,17},{... | collective-permute-start | bytes 589832 | tf_op jit(solution)/shard_map/ppermute | solution.py:40
  304.8 23.0 %collective-permute-start.63 = (bf16[48,2048]{1,0:T(8,128)(2,1)S(1)}, bf16[48,2048]{1,0:T(8,128)(2,1)S(1)}, u32[]{:S(2)}, u32[]{:S(2)}) collective-permute-start(bf16[48,2048]{1,0:T(8,128)(2,1)S(1)} %get-tuple-element.182), channel_id=1, source_target_pairs={{0,20},{4,16},{8,28},{12,24},{16,4},{20,0},{24,12},{28,8},{1,21},{... | collective-permute-start | bytes 589832 | tf_op jit(solution)/shard_map/ppermute | solution.py:40
  312.9 16.9 %collective-permute-start.54 = (bf16[48,2048]{1,0:T(8,128)(2,1)S(1)}, bf16[48,2048]{1,0:T(8,128)(2,1)S(1)}, u32[]{:S(2)}, u32[]{:S(2)}) collective-permute-start(bf16[48,2048]{1,0:T(8,128)(2,1)S(1)} %get-tuple-element.171), channel_id=1, source_target_pairs={{0,4},{4,0},{8,12},{12,8},{16,20},{20,16},{24,28},{28,24},{1,5},{5... | collective-permute-start | bytes 589832 | tf_op jit(solution)/shard_map/ppermute | solution.py:40
  315.4 14.5 %collective-permute-start.55 = (bf16[48,2048]{1,0:T(8,128)(2,1)S(1)}, bf16[48,2048]{1,0:T(8,128)(2,1)S(1)}, u32[]{:S(2)}, u32[]{:S(2)}) collective-permute-start(bf16[48,2048]{1,0:T(8,128)(2,1)S(1)} %get-tuple-element.172), channel_id=1, source_target_pairs={{0,8},{4,12},{8,0},{12,4},{16,24},{20,28},{24,16},{28,20},{1,9},{5... | collective-permute-start | bytes 589832 | tf_op jit(solution)/shard_map/ppermute | solution.py:40
  315.7 25.9 %collective-permute-start.56 = (bf16[48,2048]{1,0:T(8,128)(2,1)S(1)}, bf16[48,2048]{1,0:T(8,128)(2,1)S(1)}, u32[]{:S(2)}, u32[]{:S(2)}) collective-permute-start(bf16[48,2048]{1,0:T(8,128)(2,1)S(1)} %get-tuple-element.173), channel_id=1, source_target_pairs={{0,12},{4,8},{8,4},{12,0},{16,28},{20,24},{24,20},{28,16},{1,13},{... | collective-permute-start | bytes 589832 | tf_op jit(solution)/shard_map/ppermute | solution.py:40
  321.7 19.9 %collective-permute-start.66 = (bf16[48,2048]{1,0:T(8,128)(2,1)S(1)}, bf16[48,2048]{1,0:T(8,128)(2,1)S(1)}, u32[]{:S(2)}, u32[]{:S(2)}) collective-permute-start(bf16[48,2048]{1,0:T(8,128)(2,1)S(1)} %get-tuple-element.187), channel_id=1, source_target_pairs={{0,24},{4,28},{8,16},{12,20},{16,8},{20,12},{24,0},{28,4},{1,25},{... | collective-permute-start | bytes 589832 | tf_op jit(solution)/shard_map/ppermute | solution.py:40
  327.8 13.8 %collective-permute-start.67 = (bf16[48,2048]{1,0:T(8,128)(2,1)S(1)}, bf16[48,2048]{1,0:T(8,128)(2,1)S(1)}, u32[]{:S(2)}, u32[]{:S(2)}) collective-permute-start(bf16[48,2048]{1,0:T(8,128)(2,1)S(1)} %get-tuple-element.188), channel_id=1, source_target_pairs={{0,28},{4,24},{8,20},{12,16},{16,12},{20,8},{24,4},{28,0},{1,29},{... | collective-permute-start | bytes 589832 | tf_op jit(solution)/shard_map/ppermute | solution.py:40
  (66 other events, 634.2 us)
where the time goes:
time: 348 us; the launch traced here: 343 us
  waiting for transfers between devices  152 us (44%)
  Pallas kernels  84 us (24%)
  starting transfers between devices  67.3 us (19%)
  local copies, waits for them, and re-layouts  33 us (9%)
  other arithmetic  6.28 us (2%)
    ppermute x68, waiting for transfers between devices, exchange(): lax.ppermute(shard, axis, [(i, i ^ mask) for i in range(lax.axis_size(axi...  152 us
    ppermute x68, starting transfers between devices, exchange(): lax.ppermute(shard, axis, [(i, i ^ mask) for i in range(lax.axis_size(axi...  67.3 us
    pallas_call x4, Pallas kernels, in_weights(): pl.pallas_call(functools.partial(in_weights_kernel, first_steps), grid=(f...  32.5 us
    pallas_call x3, Pallas kernels, expert_parts(): pl.pallas_call(functools.partial(expert_kernel, part_count, full_width),...  21.1 us
    unnamed x99, local copies, waits for them, and re-layouts  17.7 us
    pallas_call x3, Pallas kernels, hidden_units(): pl.pallas_call(functools.partial(hidden_kernel, part_count, full_width),...  13.8 us
  transfers between devices with their start and end apart: 68, of which 23 were waited for; matrix products, arithmetic and copies ran while one was open for 6% of the time, Pallas kernels for 24%

commit v1 on v0

--- a/solution.py
+++ b/solution.py
@@ -12,20 +12,18 @@
 LAYERS = 2
 ORDERS = (
     (
-        ("Ra", 0), ("G", 1), ("Wg0", 1), ("Rb", 0), ("V0", 1), ("Wd0", 1), ("Wu0", 1),
-        ("Rc", 1), ("Ca", 0), ("Ea", 1), ("Cb", 0), ("Cc", 0), ("Ec", 0), ("Xa", 1), ("Xc", 0),
-        ("Eb", 0), ("Xb", 0), ("S", 0), ("Wg1", 1), ("Pc", 0), ("Pa", 1), ("Wu1", 0), ("Pb", 1),
-        ("V1", 1),
+        ("Wg0", 1), ("G", 0), ("S", 0), ("Ra", 1), ("Wu0", 1), ("Wd0", 1), ("Rb", 1),
+        ("Ca", 0), ("Cb", 1), ("Ea", 0), ("Xa", 1), ("Eb", 0), ("Xb", 1), ("Pb", 1),
+        ("Wd1", 1), ("Wu1", 1), ("Pa", 1), ("Wg1", 1),
     ),
     (
-        ("Nc", 1), ("Na", 0), ("Ra", 1), ("Nb", 1), ("Rb", 1), ("Ca", 1), ("Ea", 1), ("Xa", 1),
-        ("v", 0), ("Rc", 0), ("Wd1", 1), ("Cb", 1), ("Pa", 1), ("Eb", 0), ("S", 1), ("Xb", 1),
-        ("Cc", 1), ("Ec", 0), ("Pb", 1), ("Xc", 1), ("Pc", 1),
+        ("S", 1), ("Ra", 0), ("Rb", 0), ("Ca", 1), ("Ea", 1), ("Cb", 1), ("Eb", 0), ("Xb", 1),
+        ("Xa", 1), ("Pb", 1), ("Pa", 0),
     ),
 )
 GROUPS = (
-    (("a", (0, 1, 2, 3)), ("b", (4, 5)), ("c", (6, 7))),
-    (("a", (0, 1, 2, 3)), ("b", (4, 5)), ("c", (6, 7))),
+    ("a", (0, 1, 2, 3)),
+    ("b", (4, 5, 6, 7)),
 )
 GROUP = 128
 BLOCK = 256
@@ -146,7 +144,7 @@
     return out.reshape(full, width)
 
 
-def down_rows_kernel(words_ref, scales_ref, out_ref):
+def out_weights_kernel(words_ref, scales_ref, out_ref):
     words = words_ref[0, 0]
     word_rows = words.shape[0]
     words_group = GROUP // 2
@@ -159,12 +157,12 @@
             ).astype(jnp.bfloat16)
 
 
-def down_rows(words, scales, layer_idx):
+def out_weights(words, scales, layer_idx):
     _, _, word_rows, width = words.shape
     groups = scales.shape[2]
     tile = width // 2
     return pl.pallas_call(
-        down_rows_kernel,
+        out_weights_kernel,
         grid=(width // tile,),
         in_specs=[
             pl.BlockSpec((1, 1, word_rows, tile), lambda c: (layer_idx, 0, 0, c)),
@@ -174,7 +172,7 @@
         out_shape=jax.ShapeDtypeStruct((2 * word_rows, width), jnp.bfloat16),
         compiler_params=pltpu.CompilerParams(vmem_limit_bytes=54 * MIB),
         cost_estimate=SHORT,
-        name="out_weights_rows",
+        name="out_weights",
     )(words, scales)
 
 
@@ -278,126 +276,6 @@
     )(*terms)
 
 
-def out_weights_kernel(word_rows, *refs):
-    out_ref = refs[-1]
-    words_group = GROUP // 2
-    for source, ref in enumerate(refs[:-1]):
-        for g in range(word_rows // words_group):
-            words = ref[g * words_group : (g + 1) * words_group, :]
-            factor = power(ref[word_rows + g : word_rows + g + 1, :])
-            for part, shift in enumerate((0, 4)):
-                codes = ((words >> shift) & 15).astype(jnp.float32) - 8.0
-                at = part * word_rows + g * words_group
-                out_ref[source, at : at + words_group, :] = (codes * factor).astype(jnp.bfloat16)
-
-
-def out_weights(blocks, word_rows):
-    width = blocks[0].shape[1]
-    vmem = pl.BlockSpec(memory_space=pltpu.VMEM)
-    return pl.pallas_call(
-        functools.partial(out_weights_kernel, word_rows),
-        in_specs=[vmem] * len(blocks),
-        out_specs=vmem,
-        out_shape=jax.ShapeDtypeStruct((len(blocks), 2 * word_rows, width), jnp.bfloat16),
-        compiler_params=pltpu.CompilerParams(vmem_limit_bytes=24 * MIB),
-        cost_estimate=SHORT,
-        name="out_weights",
-    )(*blocks)
-
-
-def hidden_kernel(part_count, full_width, index_ref, *refs):
-    x_refs, refs = refs[:part_count], refs[part_count:]
-    gain_refs, refs = refs[:part_count], refs[part_count:]
-    split_ref, gate_hbm, up_hbm, out_ref, gate_ref, up_ref, gate_sem, up_sem = refs
-    width = x_refs[0].shape[1]
-    copies = []
-    for j in range(part_count):
-        at = pl.ds(pl.multiple_of((index_ref[0] ^ j) * width, width), width)
-        copies.append(
-            (
-                pltpu.make_async_copy(gate_hbm.at[at, :], gate_ref.at[j], gate_sem.at[j]),
-                pltpu.make_async_copy(up_hbm.at[at, :], up_ref.at[j], up_sem.at[j]),
-            )
-        )
-        copies[j][0].start()
-        copies[j][1].start()
-    gate = up = square = None
-    for j in range(part_count):
-        wide = x_refs[j][...].astype(jnp.float32)
-        rows = (wide * gain_refs[j][...]).astype(jnp.bfloat16)
-        part = jnp.sum(wide * wide, axis=1, keepdims=True)
-        square = part if j == 0 else square + part
-        copies[j][0].wait()
-        part = jnp.dot(rows, gate_ref[j], preferred_element_type=jnp.float32)
-        gate = part if j == 0 else gate + part
-        copies[j][1].wait()
-        part = jnp.dot(rows, up_ref[j], preferred_element_type=jnp.float32)
-        up = part if j == 0 else up + part
-    scale = lax.rsqrt(square / full_width + 1e-05) * (1.0 / math.sqrt(full_width))
-    gate = gate * scale
-    act = (gate / (1.0 + jnp.exp(-gate))) * (up * scale)
-    out_ref[...] = jnp.dot(
-        act.astype(jnp.bfloat16), split_ref[...], preferred_element_type=jnp.float32
-    ).astype(jnp.bfloat16)
-
-
-def hidden_units(index, parts, gains, gate_w, up_w, split):
-    part_count = len(parts)
-    row_count, width = parts[0].shape
-    full_width, hidden = gate_w.shape
-    vmem = pl.BlockSpec(memory_space=pltpu.VMEM)
-    hbm = pl.BlockSpec(memory_space=pltpu.HBM)
-    return pl.pallas_call(
-        functools.partial(hidden_kernel, part_count, full_width),
-        in_specs=[pl.BlockSpec(memory_space=pltpu.SMEM)]
-        + [vmem] * (2 * part_count + 1)
-        + [hbm] * 2,
-        out_specs=vmem,
-        out_shape=jax.ShapeDtypeStruct((row_count, hidden), jnp.bfloat16),
-        scratch_shapes=[
-            pltpu.VMEM((part_count, width, hidden), jnp.bfloat16),
-            pltpu.VMEM((part_count, width, hidden), jnp.bfloat16),
-            pltpu.SemaphoreType.DMA((part_count,)),
-            pltpu.SemaphoreType.DMA((part_count,)),
-        ],
-        compiler_params=pltpu.CompilerParams(vmem_limit_bytes=24 * MIB),
-        cost_estimate=SHORT,
-        name="hidden_units",
-    )(index, *parts, *gains, split, gate_w, up_w)
-
-
-def columns_kernel(array_count, *refs):
-    act_refs, down_ref, out_refs = refs[:array_count], refs[array_count], refs[array_count + 1 :]
-    total = None
-    source = 0
-    for acts in act_refs:
-        for i in range(acts.shape[0]):
-            part = jnp.dot(acts[i], down_ref[source], preferred_element_type=jnp.float32)
-            total = part if source == 0 else total + part
-            source += 1
-    at = 0
-    for out in out_refs:
-        rows = out.shape[0]
-        out[...] = total[at : at + rows].astype(jnp.bfloat16)
-        at += rows
-
-
-def columns(acts, down_w, piece_rows):
-    row_count = acts[0].shape[1]
-    width = down_w.shape[2]
-    vmem = pl.BlockSpec(memory_space=pltpu.VMEM)
-    count = row_count // piece_rows
-    return pl.pallas_call(
-        functools.partial(columns_kernel, len(acts)),
-        in_specs=[vmem] * (len(acts) + 1),
-        out_specs=[vmem] * count,
-        out_shape=[jax.ShapeDtypeStruct((piece_rows, width), jnp.bfloat16)] * count,
-        compiler_params=pltpu.CompilerParams(vmem_limit_bytes=24 * MIB),
-        cost_estimate=SHORT,
-        name="columns",
-    )(*acts, down_w)
-
-
 def make_stats(stream, gain, router):
     scaled = (stream * gain).astype(jnp.bfloat16)
     logits = lax.dot_general(router, scaled, NT, preferred_element_type=jnp.float32)
@@ -601,48 +479,14 @@
             returned[k] = piece if k == 0 else exchange(piece, "expert", k)
         return pieces
 
-    word_rows = down_codes.shape[2]
-    scale_rows = down_scales.shape[2]
-
-    def word_block(layer_idx, j):
-        at = (index[0] ^ j) * width
-        words = lax.dynamic_slice_in_dim(down_codes[layer_idx, 0], at, width, 1)
-        scales = lax.dynamic_slice_in_dim(down_scales[layer_idx, 0], at, width, 1)
-        spare = jnp.zeros((8 - scale_rows % 8, width), jnp.int32)
-        return jnp.concatenate([words, scales, spare], axis=0)
-
-    top = 1 << bits - 1
-    moved = {}
-
-    def swap_first(part, wait):
-        going = [j for j in range(part_count) if j & top]
-        going = going[part * len(going) // 2 : (part + 1) * len(going) // 2]
-        payload = wait(jnp.stack([word_block(LAYERS - 1, j) for j in going]))
-        arrived = exchange(payload, "tensor", top)
-        for i, j in enumerate(going):
-            moved[j ^ top] = [(0, word_block(LAYERS - 1, j ^ top)), (top, arrived[i])]
-        return payload
-
-    def swap_rest(wait):
-        held, payload = dict(moved), None
-        for bit in reversed(range(bits - 1)):
-            going = [(j, *item) for j in sorted(held) if j >> bit & 1 for item in held[j]]
-            payload = wait(jnp.stack([block for _, _, block in going]))
-            arrived = exchange(payload, "tensor", 1 << bit)
-            held = {j: list(items) for j, items in held.items() if not j >> bit & 1}
-            for i, (j, source, _) in enumerate(going):
-                held[j ^ 1 << bit].append((source ^ 1 << bit, arrived[i]))
-        return payload, [block for _, block in sorted(held[0], key=lambda item: item[0])]
-
-    final = None
+    unit = max(1, expert_count // 8)
+    groups = {
+        name: [k for u in units for k in range(u * unit, (u + 1) * unit)]
+        for name, units in GROUPS
+    }
     prepared = {}
     whole_gain = None
     for layer_idx in range(LAYERS):
-        unit = max(1, expert_count // 8)
-        groups = {
-            name: [k for u in units for k in range(u * unit, (u + 1) * unit)]
-            for name, units in GROUPS[layer_idx]
-        }
         arrived = {0: slots[0]}
 
         def sent(name, slots=slots):
@@ -652,8 +496,7 @@
             return [arrived[k] for k in groups[name]]
 
         returned = [None] * expert_count
-        rows, parts, outs, terms, acts = {}, {}, {}, {}, {}
-        by_words = layer_idx == LAYERS - 1
+        rows, parts, outs, terms = {}, {}, {}, {}
         token = None
         for step, chained in ORDERS[layer_idx]:
             kind, name = step[0], step[1:]
@@ -675,29 +518,6 @@
                 token = [held[j] for j in sorted(held) if j > 0]
                 held[0] = ordered(held[0], token)
                 parts[name] = gather_parts(held, core_bits)
-            elif kind == "E" and by_words:
-                token = hidden_units(
-                    wait(index),
-                    [parts[name][j] for j in range(part_count)],
-                    [whole_gain[j][layer_idx : layer_idx + 1] for j in range(part_count)],
-                    prepared["g", layer_idx],
-                    prepared["u", layer_idx],
-                    split,
-                )
-                acts[name] = [token[None], exchange(token, "tensor", 1)[None]]
-            elif kind == "X" and by_words:
-                for bit in range(1, bits):
-                    held = jnp.concatenate(wait(acts[name]), axis=0)
-                    token = held
-                    acts[name] = [held, exchange(held, "tensor", 1 << bit)]
-            elif kind == "P" and by_words:
-                token = columns(wait(acts[name]), prepared["d", layer_idx], capacity)
-                for k, piece in zip(groups[name], token):
-                    returned[k] = piece if k == 0 else exchange(piece, "expert", k)
-            elif kind == "V":
-                token = swap_first(int(name), wait)
-            elif kind == "v":
-                token, final = swap_rest(wait)
             elif kind == "E":
                 outs[name] = expert_parts(
                     wait(index),
@@ -721,10 +541,8 @@
                 token = rows[name]
             elif kind == "W":
                 at = int(name[1:])
-                if name[0] == "d" and at == LAYERS - 1:
-                    prepared["d", at] = out_weights(wait(final), word_rows)
-                elif name[0] == "d":
-                    prepared["d", at] = down_rows(down_codes, wait(down_scales), at)
+                if name[0] == "d":
+                    prepared["d", at] = out_weights(down_codes, wait(down_scales), at)
                 else:
                     codes, scales = {"g": (gate_codes, gate_scales), "u": (up_codes, up_scales)}[name[0]]
                     prepared[name[0], at] = in_weights(codes, scales, wait(table), at)
@@ -741,7 +559,8 @@
         if layer_idx + 1 < LAYERS:
             following = [norm_gain[layer_idx + 1 : layer_idx + 2], router_rows[layer_idx + 1]]
             ready = [value for (_, at), value in prepared.items() if at > layer_idx]
-            me = ordered(me, ready)
+            if ready:
+                me = ordered(me, ready)
         results = combine(
             me, routes_rows, picks, stats, stream, returned, full_width, following
         )

time: 348 us -> 285 us (0.82); the launches traced: 343 us -> 284 us
  waiting for transfers between devices: 152 us -> 126 us
  local copies, waits for them, and re-layouts: 33 us -> 10.2 us
  Pallas kernels: 84 us -> 74.5 us
  other arithmetic: 6.28 us -> 1.09 us
  starting transfers between devices: 67.3 us -> 71.7 us
    ppermute x68 -> x55, waiting for transfers between devices: 152 us -> 126 us  [exchange(): lax.ppermute(shard, axis, [(i, i ^ mask) for i in range(lax.axis_size(axi...]
    pallas_call x8 -> x2, Pallas kernels: 22.7 us -> 8.93 us  [out_weights(): pl.pallas_call(out_weights_kernel, grid=(width // tile,), in_specs=[pl.Bl...]
    unnamed x99 -> x32, local copies, waits for them, and re-layouts: 17.7 us -> 8.48 us
    pallas_call x3 -> x4, Pallas kernels: 21.1 us -> 29 us  [expert_parts(): pl.pallas_call(functools.partial(expert_kernel, part_count, full_width),...]
    slice x3 -> x0, local copies, waits for them, and re-layouts: 4.63 us -> none  [the longest x1 4.62 us: word_block(): words = lax.dynamic_slice_in_dim(down_codes[layer_idx, 0], at, width, 1)]
    ppermute x68 -> x55, starting transfers between devices: 67.3 us -> 71.7 us  [exchange(): lax.ppermute(shard, axis, [(i, i ^ mask) for i in range(lax.axis_size(axi...]
    another operation x2 -> x0, other arithmetic: 3.64 us -> none  [swap_rest(): payload = wait(jnp.stack([block for _, _, block in going]))]
  transfers between devices with their start and end apart: 68 -> 55, of which waited for: 23 -> 28; matrix products, arithmetic and copies ran while one was open for 6% -> 0% of each run, Pallas kernels for 24% -> 22%
where the time goes in v1:
time: 285 us; the launch traced here: 284 us
  waiting for transfers between devices  126 us (44%)
  Pallas kernels  74.5 us (26%)
  starting transfers between devices  71.7 us (25%)
  local copies, waits for them, and re-layouts  10.2 us (4%)
    ppermute x55, waiting for transfers between devices, exchange(): lax.ppermute(shard, axis, [(i, i ^ mask) for i in range(lax.axis_size(axi...  126 us
    ppermute x55, starting transfers between devices, exchange(): lax.ppermute(shard, axis, [(i, i ^ mask) for i in range(lax.axis_size(axi...  71.7 us
    pallas_call x4, Pallas kernels, in_weights(): pl.pallas_call(functools.partial(in_weights_kernel, first_steps), grid=(f...  31.2 us
    pallas_call x4, Pallas kernels, expert_parts(): pl.pallas_call(functools.partial(expert_kernel, part_count, full_width),...  29 us
    pallas_call x2, Pallas kernels, out_weights(): pl.pallas_call(out_weights_kernel, grid=(width // tile,), in_specs=[pl.Bl...  8.93 us
    unnamed x32, local copies, waits for them, and re-layouts  8.48 us
  transfers between devices with their start and end apart: 55, of which 28 were waited for; matrix products, arithmetic and copies ran while one was open for 0% of the time, Pallas kernels for 22%

profile of v1, /device:TPU:0, one launch (start us, length us, event | category | flops | bytes accessed | tf_op | source)
XLA Modules:
  0.0 284.0 jit_solution(3118389066934859390)
XLA Ops:
  4.4 3.0 %collective-permute-start.4 = (bf16[48,2048]{1,0:T(8,128)(2,1)S(1)}, bf16[48,2048]{1,0:T(8,128)(2,1)S(1)}, u32[]{:S(2)}, u32[]{:S(2)}) collective-permute-start(bf16[48,2048]{1,0:T(8,128)(2,1)S(1)} %get-tuple-element.92), channel_id=1, source_target_pairs={{0,4},{4,0},{8,12},{12,8},{16,20},{20,16},{24,28},{28,24},{1,5},{5... | collective-permute-start | bytes 589832 | tf_op jit(solution)/shard_map/ppermute | solution.py:38
  10.1 1.9 collective-permute-start.8
  12.0 2.6 collective-permute-start
  14.6 3.1 %collective-permute-start.1 = (bf16[48,2048]{1,0:T(8,128)(2,1)S(1)}, bf16[48,2048]{1,0:T(8,128)(2,1)S(1)}, u32[]{:S(2)}, u32[]{:S(2)}) collective-permute-start(bf16[48,2048]{1,0:T(8,128)(2,1)S(1)} %get-tuple-element.88), channel_id=1, source_target_pairs={{0,20},{4,16},{8,28},{12,24},{16,4},{20,0},{24,12},{28,8},{1,21},{... | collective-permute-start | bytes 589832 | tf_op jit(solution)/shard_map/ppermute | solution.py:38
  17.7 1.8 collective-permute-start.2
  19.5 2.0 collective-permute-start.3
  21.6 2.5 collective-permute-start.10
  24.1 7.7 %in_weights.4 = bf16[32,256,256]{2,1,0:T(8,128)(2,1)} custom-call(s32[2,1,4096,256]{3,2,1,0:T(8,128)} %words_ref.10, s32[2,1,64,256]{3,2,1,0:T(8,128)} %scales_ref.8, bf16[256,256]{1,0:T(8,128)(2,1)} %constant.13.clone.table_ref), custom_call_target="tpu_custom_call" | custom-call | flops 1000 | bytes 1000 | tf_op jit(solution)/shard_map/in_weights/pallas_call | solution.py:121
  31.8 4.5 %out_weights.2.refs_11_ = bf16[256,8192]{1,0:T(8,128)(2,1)} custom-call(s32[2,1,128,8192]{3,2,1,0:T(8,128)} %words_ref.9, s32[2,1,2,8192]{3,2,1,0:T(2,128)} %scales_ref.7), custom_call_target="tpu_custom_call" | custom-call | flops 1000 | bytes 1000 | tf_op jit(solution)/shard_map/out_weights/pallas_call | solution.py:164
  37.5 5.2 %collective-permute-done.1 = bf16[48,2048]{1,0:T(8,128)(2,1)S(1)} collective-permute-done((bf16[48,2048]{1,0:T(8,128)(2,1)S(1)}, bf16[48,2048]{1,0:T(8,128)(2,1)S(1)}, u32[]{:S(2)}, u32[]{:S(2)}) %collective-permute-start.1) | collective-permute-done | bytes 196640 | tf_op jit(solution)/shard_map/ppermute | solution.py:38
  44.9 7.8 %in_weights.5 = bf16[32,256,256]{2,1,0:T(8,128)(2,1)} custom-call(s32[2,1,4096,256]{3,2,1,0:T(8,128)} %words_ref.11, s32[2,1,64,256]{3,2,1,0:T(8,128)} %scales_ref.9, bf16[256,256]{1,0:T(8,128)(2,1)} %constant.13.clone.table_ref), custom_call_target="tpu_custom_call" | custom-call | flops 1000 | bytes 1000 | tf_op jit(solution)/shard_map/in_weights/pallas_call | solution.py:121
  52.7 8.0 %collective-permute-done.14 = f32[2,2048]{1,0:T(2,128)S(1)} collective-permute-done((f32[2,2048]{1,0:T(2,128)S(1)}, f32[2,2048]{1,0:T(2,128)S(1)}, u32[]{:S(2)}, u32[]{:S(2)}) %collective-permute-start.14) | collective-permute-done | bytes 16416 | tf_op jit(solution)/shard_map/ppermute | solution.py:38
  62.0 2.3 collective-permute-done.11.refs_1_
  64.3 2.2 copy-done.2
  66.5 2.2 copy-done.3
  68.7 7.2 %expert_parts.4 = (bf16[2,192,2048]{2,1,0:T(8,128)(2,1)S(1)}, bf16[2,192,2048]{2,1,0:T(8,128)(2,1)S(1)}) custom-call(s32[1]{0:T(128)} %bitcast.1.index_ref, bf16[192,2048]{1,0:T(8,128)(2,1)S(1)} %constant_dynamic-update-slice_fusion.4.refs_0_, bf16[192,2048]{1,0:T(8,128)(2,1)S(1)} %collective-permute-done.11.refs_1_, ...), custom_call_target="tpu_custom_call" | custom-call | flops 1000 | bytes 1000 | tf_op jit(solution)/shard_map/expert_parts/pallas_call | solution.py:232
  76.3 7.3 %expert_parts.5 = (bf16[2,192,2048]{2,1,0:T(8,128)(2,1)S(1)}, bf16[2,192,2048]{2,1,0:T(8,128)(2,1)S(1)}) custom-call(s32[1]{0:T(128)} %bitcast.1.index_ref, bf16[192,2048]{1,0:T(8,128)(2,1)S(1)} %constant_dynamic-update-slice_fusion.refs_0_, bf16[192,2048]{1,0:T(8,128)(2,1)S(1)} %collective-permute-done.18.refs_1_, ...), custom_call_target="tpu_custom_call" | custom-call | flops 1000 | bytes 1000 | tf_op jit(solution)/shard_map/expert_parts/pallas_call | solution.py:232
  84.7 2.4 collective-permute-done.20.refs_1_
  88.0 16.6 %collective-permute-done.17.refs_2_ = bf16[1,192,2048]{2,1,0:T(8,128)(2,1)S(1)} collective-permute-done((bf16[1,192,2048]{2,1,0:T(8,128)(2,1)S(1)}, bf16[1,192,2048]{2,1,0:T(8,128)(2,1)S(1)}, u32[]{:S(2)}, u32[]{:S(2)}) %collective-permute-start.17) | collective-permute-done | bytes 786464 | tf_op jit(solution)/shard_map/ppermute | solution.py:38
  104.9 11.6 %collective-permute-start.25 = (bf16[48,2048]{1,0:T(8,128)(2,1)S(1)}, bf16[48,2048]{1,0:T(8,128)(2,1)S(1)}, u32[]{:S(2)}, u32[]{:S(2)}) collective-permute-start(bf16[48,2048]{1,0:T(8,128)(2,1)S(1)} %get-tuple-element.115), channel_id=1, source_target_pairs={{0,16},{4,20},{8,24},{12,28},{16,0},{20,4},{24,8},{28,12},{1,17},{... | collective-permute-start | bytes 589832 | tf_op jit(solution)/shard_map/ppermute | solution.py:38
  117.0 4.3 %collective-permute-start.28 = (bf16[48,2048]{1,0:T(8,128)(2,1)S(1)}, bf16[48,2048]{1,0:T(8,128)(2,1)S(1)}, u32[]{:S(2)}, u32[]{:S(2)}) collective-permute-start(bf16[48,2048]{1,0:T(8,128)(2,1)S(1)} %get-tuple-element.118), channel_id=1, source_target_pairs={{0,28},{4,24},{8,20},{12,16},{16,12},{20,8},{24,4},{28,0},{1,29},{... | collective-permute-start | bytes 589832 | tf_op jit(solution)/shard_map/ppermute | solution.py:38
  121.3 4.5 %out_weights.3.refs_11_ = bf16[256,8192]{1,0:T(8,128)(2,1)} custom-call(s32[2,1,128,8192]{3,2,1,0:T(8,128)} %words_ref.9, s32[2,1,2,8192]{3,2,1,0:T(2,128)} %scales_ref.7), custom_call_target="tpu_custom_call" | custom-call | flops 1000 | bytes 1000 | tf_op jit(solution)/shard_map/out_weights/pallas_call | solution.py:164
  125.7 7.8 %in_weights.6 = bf16[32,256,256]{2,1,0:T(8,128)(2,1)} custom-call(s32[2,1,4096,256]{3,2,1,0:T(8,128)} %words_ref.10, s32[2,1,64,256]{3,2,1,0:T(8,128)} %scales_ref.8, bf16[256,256]{1,0:T(8,128)(2,1)} %constant.13.clone.table_ref), custom_call_target="tpu_custom_call" | custom-call | flops 1000 | bytes 1000 | tf_op jit(solution)/shard_map/in_weights/pallas_call | solution.py:121
  134.4 2.6 collective-permute-done.25.refs_8_
  137.0 5.0 %collective-permute-done.26.refs_9_ = bf16[48,2048]{1,0:T(8,128)(2,1)S(1)} collective-permute-done((bf16[48,2048]{1,0:T(8,128)(2,1)S(1)}, bf16[48,2048]{1,0:T(8,128)(2,1)S(1)}, u32[]{:S(2)}, u32[]{:S(2)}) %collective-permute-start.26) | collective-permute-done | bytes 196640 | tf_op jit(solution)/shard_map/ppermute | solution.py:38
  142.0 7.8 %in_weights.7 = bf16[32,256,256]{2,1,0:T(8,128)(2,1)} custom-call(s32[2,1,4096,256]{3,2,1,0:T(8,128)} %words_ref.11, s32[2,1,64,256]{3,2,1,0:T(8,128)} %scales_ref.9, bf16[256,256]{1,0:T(8,128)(2,1)} %constant.13.clone.table_ref), custom_call_target="tpu_custom_call" | custom-call | flops 1000 | bytes 1000 | tf_op jit(solution)/shard_map/in_weights/pallas_call | solution.py:121
  152.6 2.9 %collective-permute-start.32 = (bf16[48,2048]{1,0:T(8,128)(2,1)S(1)}, bf16[48,2048]{1,0:T(8,128)(2,1)S(1)}, u32[]{:S(2)}, u32[]{:S(2)}) collective-permute-start(bf16[48,2048]{1,0:T(8,128)(2,1)S(1)} %get-tuple-element.139), channel_id=1, source_target_pairs={{0,8},{4,12},{8,0},{12,4},{16,24},{20,28},{24,16},{28,20},{1,9},{5... | collective-permute-start | bytes 589832 | tf_op jit(solution)/shard_map/ppermute | solution.py:38
  157.6 1.9 collective-permute-start.36
  161.0 4.9 %collective-permute-done.32 = bf16[48,2048]{1,0:T(8,128)(2,1)S(1)} collective-permute-done((bf16[48,2048]{1,0:T(8,128)(2,1)S(1)}, bf16[48,2048]{1,0:T(8,128)(2,1)S(1)}, u32[]{:S(2)}, u32[]{:S(2)}) %collective-permute-start.32) | collective-permute-done | bytes 196640 | tf_op jit(solution)/shard_map/ppermute | solution.py:38
  165.9 3.8 %collective-permute-start.38 = (bf16[48,2048]{1,0:T(8,128)(2,1)S(1)}, bf16[48,2048]{1,0:T(8,128)(2,1)S(1)}, u32[]{:S(2)}, u32[]{:S(2)}) collective-permute-start(bf16[48,2048]{1,0:T(8,128)(2,1)S(1)} %get-tuple-element.144), channel_id=1, source_target_pairs={{0,28},{4,24},{8,20},{12,16},{16,12},{20,8},{24,4},{28,0},{1,29},{... | collective-permute-start | bytes 589832 | tf_op jit(solution)/shard_map/ppermute | solution.py:38
  170.7 11.0 %collective-permute-done.35 = bf16[48,2048]{1,0:T(8,128)(2,1)S(1)} collective-permute-done((bf16[48,2048]{1,0:T(8,128)(2,1)S(1)}, bf16[48,2048]{1,0:T(8,128)(2,1)S(1)}, u32[]{:S(2)}, u32[]{:S(2)}) %collective-permute-start.35) | collective-permute-done | bytes 196640 | tf_op jit(solution)/shard_map/ppermute | solution.py:38
  181.8 4.5 %collective-permute-done.36 = bf16[48,2048]{1,0:T(8,128)(2,1)S(1)} collective-permute-done((bf16[48,2048]{1,0:T(8,128)(2,1)S(1)}, bf16[48,2048]{1,0:T(8,128)(2,1)S(1)}, u32[]{:S(2)}, u32[]{:S(2)}) %collective-permute-start.36) | collective-permute-done | bytes 196640 | tf_op jit(solution)/shard_map/ppermute | solution.py:38
  191.1 2.2 copy-done.1
  193.3 7.4 %expert_parts.6 = (bf16[2,192,2048]{2,1,0:T(8,128)(2,1)S(1)}, bf16[2,192,2048]{2,1,0:T(8,128)(2,1)S(1)}) custom-call(s32[1]{0:T(128)} %bitcast.1.index_ref, bf16[192,2048]{1,0:T(8,128)(2,1)S(1)} %constant_dynamic-update-slice_fusion.8.refs_0_, bf16[192,2048]{1,0:T(8,128)(2,1)S(1)} %collective-permute-done.39.refs_1_, ...), custom_call_target="tpu_custom_call" | custom-call | flops 1000 | bytes 1000 | tf_op jit(solution)/shard_map/expert_parts/pallas_call | solution.py:232
  200.7 7.0 %collective-permute-done.42.refs_2_ = bf16[192,2048]{1,0:T(8,128)(2,1)S(1)} collective-permute-done((bf16[192,2048]{1,0:T(8,128)(2,1)S(1)}, bf16[192,2048]{1,0:T(8,128)(2,1)S(1)}, u32[]{:S(2)}, u32[]{:S(2)}) %collective-permute-start.42) | collective-permute-done | bytes 786464 | tf_op jit(solution)/shard_map/ppermute | solution.py:38
  208.1 1.8 collective-permute-done.43.refs_1_
  211.0 7.2 %expert_parts.7 = (bf16[2,192,2048]{2,1,0:T(8,128)(2,1)S(1)}, bf16[2,192,2048]{2,1,0:T(8,128)(2,1)S(1)}) custom-call(s32[1]{0:T(128)} %bitcast.1.index_ref, bf16[192,2048]{1,0:T(8,128)(2,1)S(1)} %constant_dynamic-update-slice_fusion.12.refs_0_, bf16[192,2048]{1,0:T(8,128)(2,1)S(1)} %collective-permute-done.43.refs_1_, ...), custom_call_target="tpu_custom_call" | custom-call | flops 1000 | bytes 1000 | tf_op jit(solution)/shard_map/expert_parts/pallas_call | solution.py:232
  218.8 2.9 %collective-permute-done.45.refs_1_ = bf16[2,192,2048]{2,1,0:T(8,128)(2,1)S(1)} collective-permute-done((bf16[2,192,2048]{2,1,0:T(8,128)(2,1)S(1)}, bf16[2,192,2048]{2,1,0:T(8,128)(2,1)S(1)}, u32[]{:S(2)}, u32[]{:S(2)}) %collective-permute-start.45) | collective-permute-done | bytes 1572896 | tf_op jit(solution)/shard_map/ppermute | solution.py:38
  225.1 17.3 %collective-permute-done.50.refs_2_ = bf16[1,192,2048]{2,1,0:T(8,128)(2,1)S(1)} collective-permute-done((bf16[1,192,2048]{2,1,0:T(8,128)(2,1)S(1)}, bf16[1,192,2048]{2,1,0:T(8,128)(2,1)S(1)}, u32[]{:S(2)}, u32[]{:S(2)}) %collective-permute-start.50) | collective-permute-done | bytes 786464 | tf_op jit(solution)/shard_map/ppermute | solution.py:38
  242.7 6.2 %collective-permute-start.51 = (bf16[48,2048]{1,0:T(8,128)(2,1)S(1)}, bf16[48,2048]{1,0:T(8,128)(2,1)S(1)}, u32[]{:S(2)}, u32[]{:S(2)}) collective-permute-start(bf16[48,2048]{1,0:T(8,128)(2,1)S(1)} %get-tuple-element.165), channel_id=1, source_target_pairs={{0,16},{4,20},{8,24},{12,28},{16,0},{20,4},{24,8},{28,12},{1,17},{... | collective-permute-start | bytes 589832 | tf_op jit(solution)/shard_map/ppermute | solution.py:38
  251.1 2.2 collective-permute-start.53
  253.3 5.2 %collective-permute-done.46.refs_2_ = bf16[1,192,2048]{2,1,0:T(8,128)(2,1)S(1)} collective-permute-done((bf16[1,192,2048]{2,1,0:T(8,128)(2,1)S(1)}, bf16[1,192,2048]{2,1,0:T(8,128)(2,1)S(1)}, u32[]{:S(2)}, u32[]{:S(2)}) %collective-permute-start.46) | collective-permute-done | bytes 786464 | tf_op jit(solution)/shard_map/ppermute | solution.py:38
  258.5 2.2 collective-permute-start.54
  262.1 9.4 %collective-permute-done.51.refs_8_ = bf16[48,2048]{1,0:T(8,128)(2,1)S(1)} collective-permute-done((bf16[48,2048]{1,0:T(8,128)(2,1)S(1)}, bf16[48,2048]{1,0:T(8,128)(2,1)S(1)}, u32[]{:S(2)}, u32[]{:S(2)}) %collective-permute-start.51) | collective-permute-done | bytes 196640 | tf_op jit(solution)/shard_map/ppermute | solution.py:38
  271.5 4.4 %collective-permute-done.52.refs_9_ = bf16[48,2048]{1,0:T(8,128)(2,1)S(1)} collective-permute-done((bf16[48,2048]{1,0:T(8,128)(2,1)S(1)}, bf16[48,2048]{1,0:T(8,128)(2,1)S(1)}, u32[]{:S(2)}, u32[]{:S(2)}) %collective-permute-start.52) | collective-permute-done | bytes 196640 | tf_op jit(solution)/shard_map/ppermute | solution.py:38
  275.9 3.7 %collective-permute-done.48.refs_6_ = bf16[48,2048]{1,0:T(8,128)(2,1)S(1)} collective-permute-done((bf16[48,2048]{1,0:T(8,128)(2,1)S(1)}, bf16[48,2048]{1,0:T(8,128)(2,1)S(1)}, u32[]{:S(2)}, u32[]{:S(2)}) %collective-permute-start.48) | collective-permute-done | bytes 196640 | tf_op jit(solution)/shard_map/ppermute | solution.py:38
  279.6 2.8 collective-permute-done.49.refs_7_
  282.4 1.6 combine.3
  (128 shorter events, 37.5 us)
Async XLA Ops:
  4.4 13.3 %collective-permute-start.4 = (bf16[48,2048]{1,0:T(8,128)(2,1)S(1)}, bf16[48,2048]{1,0:T(8,128)(2,1)S(1)}, u32[]{:S(2)}, u32[]{:S(2)}) collective-permute-start(bf16[48,2048]{1,0:T(8,128)(2,1)S(1)} %get-tuple-element.92), channel_id=1, source_target_pairs={{0,4},{4,0},{8,12},{12,8},{16,20},{20,16},{24,28},{28,24},{1,5},{5... | collective-permute-start | bytes 589832 | tf_op jit(solution)/shard_map/ppermute | solution.py:38
  7.3 12.1 %collective-permute-start.5 = (bf16[48,2048]{1,0:T(8,128)(2,1)S(1)}, bf16[48,2048]{1,0:T(8,128)(2,1)S(1)}, u32[]{:S(2)}, u32[]{:S(2)}) collective-permute-start(bf16[48,2048]{1,0:T(8,128)(2,1)S(1)} %get-tuple-element.93), channel_id=1, source_target_pairs={{0,8},{4,12},{8,0},{12,4},{16,24},{20,28},{24,16},{28,20},{1,9},{5... | collective-permute-start | bytes 589832 | tf_op jit(solution)/shard_map/ppermute | solution.py:38
  8.9 12.5 %collective-permute-start.6 = (bf16[48,2048]{1,0:T(8,128)(2,1)S(1)}, bf16[48,2048]{1,0:T(8,128)(2,1)S(1)}, u32[]{:S(2)}, u32[]{:S(2)}) collective-permute-start(bf16[48,2048]{1,0:T(8,128)(2,1)S(1)} %get-tuple-element.94), channel_id=1, source_target_pairs={{0,12},{4,8},{8,4},{12,0},{16,28},{20,24},{24,20},{28,16},{1,13},{... | collective-permute-start | bytes 589832 | tf_op jit(solution)/shard_map/ppermute | solution.py:38
  10.1 4.5 %collective-permute-start.8 = (f32[16,128]{1,0:T(8,128)S(1)}, f32[16,128]{1,0:T(8,128)S(1)}, u32[]{:S(2)}, u32[]{:S(2)}) collective-permute-start(f32[16,128]{1,0:T(8,128)S(1)} %add.24), channel_id=1, source_target_pairs={{0,2},{1,3},{2,0},{3,1},{4,6},{5,7},{6,4},{7,5},{8,10},{9,11},{10,... | collective-permute-start | bytes 24584 | tf_op jit(solution)/shard_map/ppermute | solution.py:38
  12.0 25.5 %collective-permute-start = (bf16[48,2048]{1,0:T(8,128)(2,1)S(1)}, bf16[48,2048]{1,0:T(8,128)(2,1)S(1)}, u32[]{:S(2)}, u32[]{:S(2)}) collective-permute-start(bf16[48,2048]{1,0:T(8,128)(2,1)S(1)} %get-tuple-element.87), channel_id=1, source_target_pairs={{0,16},{4,20},{8,24},{12,28},{16,0},{20,4},{24,8},{28,12},{1,17},{... | collective-permute-start | bytes 589832 | tf_op jit(solution)/shard_map/ppermute | solution.py:38
  14.6 28.1 %collective-permute-start.1 = (bf16[48,2048]{1,0:T(8,128)(2,1)S(1)}, bf16[48,2048]{1,0:T(8,128)(2,1)S(1)}, u32[]{:S(2)}, u32[]{:S(2)}) collective-permute-start(bf16[48,2048]{1,0:T(8,128)(2,1)S(1)} %get-tuple-element.88), channel_id=1, source_target_pairs={{0,20},{4,16},{8,28},{12,24},{16,4},{20,0},{24,12},{28,8},{1,21},{... | collective-permute-start | bytes 589832 | tf_op jit(solution)/shard_map/ppermute | solution.py:38
  17.7 25.0 %collective-permute-start.2 = (bf16[48,2048]{1,0:T(8,128)(2,1)S(1)}, bf16[48,2048]{1,0:T(8,128)(2,1)S(1)}, u32[]{:S(2)}, u32[]{:S(2)}) collective-permute-start(bf16[48,2048]{1,0:T(8,128)(2,1)S(1)} %get-tuple-element.89), channel_id=1, source_target_pairs={{0,24},{4,28},{8,16},{12,20},{16,8},{20,12},{24,0},{28,4},{1,25},{... | collective-permute-start | bytes 589832 | tf_op jit(solution)/shard_map/ppermute | solution.py:38
  19.5 23.2 %collective-permute-start.3 = (bf16[48,2048]{1,0:T(8,128)(2,1)S(1)}, bf16[48,2048]{1,0:T(8,128)(2,1)S(1)}, u32[]{:S(2)}, u32[]{:S(2)}) collective-permute-start(bf16[48,2048]{1,0:T(8,128)(2,1)S(1)} %get-tuple-element.90), channel_id=1, source_target_pairs={{0,28},{4,24},{8,20},{12,16},{16,12},{20,8},{24,4},{28,0},{1,29},{... | collective-permute-start | bytes 589832 | tf_op jit(solution)/shard_map/ppermute | solution.py:38
  21.6 39.2 %collective-permute-start.10 = (bf16[192,2048]{1,0:T(8,128)(2,1)S(1)}, bf16[192,2048]{1,0:T(8,128)(2,1)S(1)}, u32[]{:S(2)}, u32[]{:S(2)}) collective-permute-start(bf16[192,2048]{1,0:T(8,128)(2,1)S(1)} %constant_dynamic-update-slice_fusion.refs_0_), channel_id=1, source_target_pairs={{0,2},{1,3},{2,0},{3,1},{4,6},{5,7},{6,4},{7,5},{8,10},{9,11},{10,... | collective-permute-start | bytes 2359304 | tf_op jit(solution)/shard_map/ppermute | solution.py:38
  42.8 18.0 %collective-permute-start.9 = (bf16[192,2048]{1,0:T(8,128)(2,1)S(1)}, bf16[192,2048]{1,0:T(8,128)(2,1)S(1)}, u32[]{:S(2)}, u32[]{:S(2)}) collective-permute-start(bf16[192,2048]{1,0:T(8,128)(2,1)S(1)} %constant_dynamic-update-slice_fusion.4.refs_0_), channel_id=1, source_target_pairs={{0,2},{1,3},{2,0},{3,1},{4,6},{5,7},{6,4},{7,5},{8,10},{9,11},{10,... | collective-permute-start | bytes 2359304 | tf_op jit(solution)/shard_map/ppermute | solution.py:38
  43.4 17.3 %collective-permute-start.14 = (f32[2,2048]{1,0:T(2,128)S(1)}, f32[2,2048]{1,0:T(2,128)S(1)}, u32[]{:S(2)}, u32[]{:S(2)}) collective-permute-start(f32[2,2048]{1,0:T(2,128)S(1)} %copy-done.9), channel_id=1, source_target_pairs={{0,2},{1,3},{2,0},{3,1},{4,6},{5,7},{6,4},{7,5},{8,10},{9,11},{10,... | collective-permute-start | bytes 49160 | tf_op jit(solution)/shard_map/ppermute | solution.py:38
  44.9 16.5 %collective-permute-start.13 = (f32[2,2048]{1,0:T(2,128)S(1)}, f32[2,2048]{1,0:T(2,128)S(1)}, u32[]{:S(2)}, u32[]{:S(2)}) collective-permute-start(f32[2,2048]{1,0:T(2,128)S(1)} %copy-done.9), channel_id=1, source_target_pairs={{0,1},{1,0},{2,3},{3,2},{4,5},{5,4},{6,7},{7,6},{8,9},{9,8},{10,11... | collective-permute-start | bytes 49160 | tf_op jit(solution)/shard_map/ppermute | solution.py:38
  60.8 3.5 %collective-permute-start.12 = (bf16[192,2048]{1,0:T(8,128)(2,1)S(1)}, bf16[192,2048]{1,0:T(8,128)(2,1)S(1)}, u32[]{:S(2)}, u32[]{:S(2)}) collective-permute-start(bf16[192,2048]{1,0:T(8,128)(2,1)S(1)} %collective-permute-done.9.refs_2_), channel_id=1, source_target_pairs={{0,1},{1,0},{2,3},{3,2},{4,5},{5,4},{6,7},{7,6},{8,9},{9,8},{10,11... | collective-permute-start | bytes 2359304 | tf_op jit(solution)/shard_map/ppermute | solution.py:38
  61.4 14.9 %collective-permute-start.18 = (bf16[192,2048]{1,0:T(8,128)(2,1)S(1)}, bf16[192,2048]{1,0:T(8,128)(2,1)S(1)}, u32[]{:S(2)}, u32[]{:S(2)}) collective-permute-start(bf16[192,2048]{1,0:T(8,128)(2,1)S(1)} %constant_dynamic-update-slice_fusion.refs_0_), channel_id=1, source_target_pairs={{0,1},{1,0},{2,3},{3,2},{4,5},{5,4},{6,7},{7,6},{8,9},{9,8},{10,11... | collective-permute-start | bytes 2359304 | tf_op jit(solution)/shard_map/ppermute | solution.py:38
  61.9 14.4 %collective-permute-start.19 = (bf16[192,2048]{1,0:T(8,128)(2,1)S(1)}, bf16[192,2048]{1,0:T(8,128)(2,1)S(1)}, u32[]{:S(2)}, u32[]{:S(2)}) collective-permute-start(bf16[192,2048]{1,0:T(8,128)(2,1)S(1)} %collective-permute-done.10.refs_2_), channel_id=1, source_target_pairs={{0,1},{1,0},{2,3},{3,2},{4,5},{5,4},{6,7},{7,6},{8,9},{9,8},{10,11... | collective-permute-start | bytes 2359304 | tf_op jit(solution)/shard_map/ppermute | solution.py:38
  75.9 8.0 %collective-permute-start.16 = (bf16[2,192,2048]{2,1,0:T(8,128)(2,1)S(1)}, bf16[2,192,2048]{2,1,0:T(8,128)(2,1)S(1)}, u32[]{:S(2)}, u32[]{:S(2)}) collective-permute-start(bf16[2,192,2048]{2,1,0:T(8,128)(2,1)S(1)} %get-tuple-element.110), channel_id=1, source_target_pairs={{0,1},{1,0},{2,3},{3,2},{4,5},{5,4},{6,7},{7,6},{8,9},{9,8},{10,11... | collective-permute-start | bytes 4718600 | tf_op jit(solution)/shard_map/ppermute | solution.py:38
  83.6 3.5 %collective-permute-start.20 = (bf16[2,192,2048]{2,1,0:T(8,128)(2,1)S(1)}, bf16[2,192,2048]{2,1,0:T(8,128)(2,1)S(1)}, u32[]{:S(2)}, u32[]{:S(2)}) collective-permute-start(bf16[2,192,2048]{2,1,0:T(8,128)(2,1)S(1)} %get-tuple-element.123), channel_id=1, source_target_pairs={{0,1},{1,0},{2,3},{3,2},{4,5},{5,4},{6,7},{7,6},{8,9},{9,8},{10,11... | collective-permute-start | bytes 4718600 | tf_op jit(solution)/shard_map/ppermute | solution.py:38
  84.1 20.4 %collective-permute-start.17 = (bf16[1,192,2048]{2,1,0:T(8,128)(2,1)S(1)}, bf16[1,192,2048]{2,1,0:T(8,128)(2,1)S(1)}, u32[]{:S(2)}, u32[]{:S(2)}) collective-permute-start(bf16[1,192,2048]{2,1,0:T(8,128)(2,1)S(1)} %add_convert_fusion.3), channel_id=1, source_target_pairs={{0,2},{1,3},{2,0},{3,1},{4,6},{5,7},{6,4},{7,5},{8,10},{9,11},{10,... | collective-permute-start | bytes 2359304 | tf_op jit(solution)/shard_map/ppermute | solution.py:38
  87.4 46.2 %collective-permute-start.21 = (bf16[1,192,2048]{2,1,0:T(8,128)(2,1)S(1)}, bf16[1,192,2048]{2,1,0:T(8,128)(2,1)S(1)}, u32[]{:S(2)}, u32[]{:S(2)}) collective-permute-start(bf16[1,192,2048]{2,1,0:T(8,128)(2,1)S(1)} %add_convert_fusion.2), channel_id=1, source_target_pairs={{0,2},{1,3},{2,0},{3,1},{4,6},{5,7},{6,4},{7,5},{8,10},{9,11},{10,... | collective-permute-start | bytes 2359304 | tf_op jit(solution)/shard_map/ppermute | solution.py:38
  104.9 32.1 %collective-permute-start.25 = (bf16[48,2048]{1,0:T(8,128)(2,1)S(1)}, bf16[48,2048]{1,0:T(8,128)(2,1)S(1)}, u32[]{:S(2)}, u32[]{:S(2)}) collective-permute-start(bf16[48,2048]{1,0:T(8,128)(2,1)S(1)} %get-tuple-element.115), channel_id=1, source_target_pairs={{0,16},{4,20},{8,24},{12,28},{16,0},{20,4},{24,8},{28,12},{1,17},{... | collective-permute-start | bytes 589832 | tf_op jit(solution)/shard_map/ppermute | solution.py:38
  116.5 25.5 %collective-permute-start.26 = (bf16[48,2048]{1,0:T(8,128)(2,1)S(1)}, bf16[48,2048]{1,0:T(8,128)(2,1)S(1)}, u32[]{:S(2)}, u32[]{:S(2)}) collective-permute-start(bf16[48,2048]{1,0:T(8,128)(2,1)S(1)} %get-tuple-element.116), channel_id=1, source_target_pairs={{0,20},{4,16},{8,28},{12,24},{16,4},{20,0},{24,12},{28,8},{1,21},{... | collective-permute-start | bytes 589832 | tf_op jit(solution)/shard_map/ppermute | solution.py:38
  116.5 33.3 %collective-permute-start.27 = (bf16[48,2048]{1,0:T(8,128)(2,1)S(1)}, bf16[48,2048]{1,0:T(8,128)(2,1)S(1)}, u32[]{:S(2)}, u32[]{:S(2)}) collective-permute-start(bf16[48,2048]{1,0:T(8,128)(2,1)S(1)} %get-tuple-element.117), channel_id=1, source_target_pairs={{0,24},{4,28},{8,16},{12,20},{16,8},{20,12},{24,0},{28,4},{1,25},{... | collective-permute-start | bytes 589832 | tf_op jit(solution)/shard_map/ppermute | solution.py:38
  117.0 32.8 %collective-permute-start.28 = (bf16[48,2048]{1,0:T(8,128)(2,1)S(1)}, bf16[48,2048]{1,0:T(8,128)(2,1)S(1)}, u32[]{:S(2)}, u32[]{:S(2)}) collective-permute-start(bf16[48,2048]{1,0:T(8,128)(2,1)S(1)} %get-tuple-element.118), channel_id=1, source_target_pairs={{0,28},{4,24},{8,20},{12,16},{16,12},{20,8},{24,4},{28,0},{1,29},{... | collective-permute-start | bytes 589832 | tf_op jit(solution)/shard_map/ppermute | solution.py:38
  133.8 16.0 %collective-permute-start.22 = (bf16[48,2048]{1,0:T(8,128)(2,1)S(1)}, bf16[48,2048]{1,0:T(8,128)(2,1)S(1)}, u32[]{:S(2)}, u32[]{:S(2)}) collective-permute-start(bf16[48,2048]{1,0:T(8,128)(2,1)S(1)} %get-tuple-element.129), channel_id=1, source_target_pairs={{0,4},{4,0},{8,12},{12,8},{16,20},{20,16},{24,28},{28,24},{1,5},{5... | collective-permute-start | bytes 589832 | tf_op jit(solution)/shard_map/ppermute | solution.py:38
  137.0 12.8 %collective-permute-start.23 = (bf16[48,2048]{1,0:T(8,128)(2,1)S(1)}, bf16[48,2048]{1,0:T(8,128)(2,1)S(1)}, u32[]{:S(2)}, u32[]{:S(2)}) collective-permute-start(bf16[48,2048]{1,0:T(8,128)(2,1)S(1)} %get-tuple-element.130), channel_id=1, source_target_pairs={{0,8},{4,12},{8,0},{12,4},{16,24},{20,28},{24,16},{28,20},{1,9},{5... | collective-permute-start | bytes 589832 | tf_op jit(solution)/shard_map/ppermute | solution.py:38
  142.0 7.8 %collective-permute-start.24 = (bf16[48,2048]{1,0:T(8,128)(2,1)S(1)}, bf16[48,2048]{1,0:T(8,128)(2,1)S(1)}, u32[]{:S(2)}, u32[]{:S(2)}) collective-permute-start(bf16[48,2048]{1,0:T(8,128)(2,1)S(1)} %get-tuple-element.131), channel_id=1, source_target_pairs={{0,12},{4,8},{8,4},{12,0},{16,28},{20,24},{24,20},{28,16},{1,13},{... | collective-permute-start | bytes 589832 | tf_op jit(solution)/shard_map/ppermute | solution.py:38
  151.4 8.0 %collective-permute-start.31 = (bf16[48,2048]{1,0:T(8,128)(2,1)S(1)}, bf16[48,2048]{1,0:T(8,128)(2,1)S(1)}, u32[]{:S(2)}, u32[]{:S(2)}) collective-permute-start(bf16[48,2048]{1,0:T(8,128)(2,1)S(1)} %get-tuple-element.138), channel_id=1, source_target_pairs={{0,4},{4,0},{8,12},{12,8},{16,20},{20,16},{24,28},{28,24},{1,5},{5... | collective-permute-start | bytes 589832 | tf_op jit(solution)/shard_map/ppermute | solution.py:38
  152.6 13.3 %collective-permute-start.32 = (bf16[48,2048]{1,0:T(8,128)(2,1)S(1)}, bf16[48,2048]{1,0:T(8,128)(2,1)S(1)}, u32[]{:S(2)}, u32[]{:S(2)}) collective-permute-start(bf16[48,2048]{1,0:T(8,128)(2,1)S(1)} %get-tuple-element.139), channel_id=1, source_target_pairs={{0,8},{4,12},{8,0},{12,4},{16,24},{20,28},{24,16},{28,20},{1,9},{5... | collective-permute-start | bytes 589832 | tf_op jit(solution)/shard_map/ppermute | solution.py:38
  155.5 14.4 %collective-permute-start.33 = (bf16[48,2048]{1,0:T(8,128)(2,1)S(1)}, bf16[48,2048]{1,0:T(8,128)(2,1)S(1)}, u32[]{:S(2)}, u32[]{:S(2)}) collective-permute-start(bf16[48,2048]{1,0:T(8,128)(2,1)S(1)} %get-tuple-element.140), channel_id=1, source_target_pairs={{0,12},{4,8},{8,4},{12,0},{16,28},{20,24},{24,20},{28,16},{1,13},{... | collective-permute-start | bytes 589832 | tf_op jit(solution)/shard_map/ppermute | solution.py:38
  156.5 25.3 %collective-permute-start.35 = (bf16[48,2048]{1,0:T(8,128)(2,1)S(1)}, bf16[48,2048]{1,0:T(8,128)(2,1)S(1)}, u32[]{:S(2)}, u32[]{:S(2)}) collective-permute-start(bf16[48,2048]{1,0:T(8,128)(2,1)S(1)} %get-tuple-element.141), channel_id=1, source_target_pairs={{0,16},{4,20},{8,24},{12,28},{16,0},{20,4},{24,8},{28,12},{1,17},{... | collective-permute-start | bytes 589832 | tf_op jit(solution)/shard_map/ppermute | solution.py:38
  157.6 28.7 %collective-permute-start.36 = (bf16[48,2048]{1,0:T(8,128)(2,1)S(1)}, bf16[48,2048]{1,0:T(8,128)(2,1)S(1)}, u32[]{:S(2)}, u32[]{:S(2)}) collective-permute-start(bf16[48,2048]{1,0:T(8,128)(2,1)S(1)} %get-tuple-element.142), channel_id=1, source_target_pairs={{0,20},{4,16},{8,28},{12,24},{16,4},{20,0},{24,12},{28,8},{1,21},{... | collective-permute-start | bytes 589832 | tf_op jit(solution)/shard_map/ppermute | solution.py:38
  159.4 26.9 %collective-permute-start.37 = (bf16[48,2048]{1,0:T(8,128)(2,1)S(1)}, bf16[48,2048]{1,0:T(8,128)(2,1)S(1)}, u32[]{:S(2)}, u32[]{:S(2)}) collective-permute-start(bf16[48,2048]{1,0:T(8,128)(2,1)S(1)} %get-tuple-element.143), channel_id=1, source_target_pairs={{0,24},{4,28},{8,16},{12,20},{16,8},{20,12},{24,0},{28,4},{1,25},{... | collective-permute-start | bytes 589832 | tf_op jit(solution)/shard_map/ppermute | solution.py:38
  165.9 20.4 %collective-permute-start.38 = (bf16[48,2048]{1,0:T(8,128)(2,1)S(1)}, bf16[48,2048]{1,0:T(8,128)(2,1)S(1)}, u32[]{:S(2)}, u32[]{:S(2)}) collective-permute-start(bf16[48,2048]{1,0:T(8,128)(2,1)S(1)} %get-tuple-element.144), channel_id=1, source_target_pairs={{0,28},{4,24},{8,20},{12,16},{16,12},{20,8},{24,4},{28,0},{1,29},{... | collective-permute-start | bytes 589832 | tf_op jit(solution)/shard_map/ppermute | solution.py:38
  169.9 17.8 %collective-permute-start.34 = (bf16[192,2048]{1,0:T(8,128)(2,1)S(1)}, bf16[192,2048]{1,0:T(8,128)(2,1)S(1)}, u32[]{:S(2)}, u32[]{:S(2)}) collective-permute-start(bf16[192,2048]{1,0:T(8,128)(2,1)S(1)} %constant_dynamic-update-slice_fusion.8.refs_0_), channel_id=1, source_target_pairs={{0,2},{1,3},{2,0},{3,1},{4,6},{5,7},{6,4},{7,5},{8,10},{9,11},{10,... | collective-permute-start | bytes 2359304 | tf_op jit(solution)/shard_map/ppermute | solution.py:38
  187.7 3.4 %collective-permute-start.40 = (bf16[192,2048]{1,0:T(8,128)(2,1)S(1)}, bf16[192,2048]{1,0:T(8,128)(2,1)S(1)}, u32[]{:S(2)}, u32[]{:S(2)}) collective-permute-start(bf16[192,2048]{1,0:T(8,128)(2,1)S(1)} %collective-permute-done.34.refs_2_), channel_id=1, source_target_pairs={{0,1},{1,0},{2,3},{3,2},{4,5},{5,4},{6,7},{7,6},{8,9},{9,8},{10,11... | collective-permute-start | bytes 2359304 | tf_op jit(solution)/shard_map/ppermute | solution.py:38
  188.2 19.4 %collective-permute-start.42 = (bf16[192,2048]{1,0:T(8,128)(2,1)S(1)}, bf16[192,2048]{1,0:T(8,128)(2,1)S(1)}, u32[]{:S(2)}, u32[]{:S(2)}) collective-permute-start(bf16[192,2048]{1,0:T(8,128)(2,1)S(1)} %constant_dynamic-update-slice_fusion.12.refs_0_), channel_id=1, source_target_pairs={{0,2},{1,3},{2,0},{3,1},{4,6},{5,7},{6,4},{7,5},{8,10},{9,11},{10,... | collective-permute-start | bytes 2359304 | tf_op jit(solution)/shard_map/ppermute | solution.py:38
  218.2 3.5 %collective-permute-start.45 = (bf16[2,192,2048]{2,1,0:T(8,128)(2,1)S(1)}, bf16[2,192,2048]{2,1,0:T(8,128)(2,1)S(1)}, u32[]{:S(2)}, u32[]{:S(2)}) collective-permute-start(bf16[2,192,2048]{2,1,0:T(8,128)(2,1)S(1)} %get-tuple-element.155), channel_id=1, source_target_pairs={{0,1},{1,0},{2,3},{3,2},{4,5},{5,4},{6,7},{7,6},{8,9},{9,8},{10,11... | collective-permute-start | bytes 4718600 | tf_op jit(solution)/shard_map/ppermute | solution.py:38
  218.4 5.5 %collective-permute-start.41 = (bf16[2,192,2048]{2,1,0:T(8,128)(2,1)S(1)}, bf16[2,192,2048]{2,1,0:T(8,128)(2,1)S(1)}, u32[]{:S(2)}, u32[]{:S(2)}) collective-permute-start(bf16[2,192,2048]{2,1,0:T(8,128)(2,1)S(1)} %get-tuple-element.150), channel_id=1, source_target_pairs={{0,1},{1,0},{2,3},{3,2},{4,5},{5,4},{6,7},{7,6},{8,9},{9,8},{10,11... | collective-permute-start | bytes 4718600 | tf_op jit(solution)/shard_map/ppermute | solution.py:38
  221.9 20.5 %collective-permute-start.50 = (bf16[1,192,2048]{2,1,0:T(8,128)(2,1)S(1)}, bf16[1,192,2048]{2,1,0:T(8,128)(2,1)S(1)}, u32[]{:S(2)}, u32[]{:S(2)}) collective-permute-start(bf16[1,192,2048]{2,1,0:T(8,128)(2,1)S(1)} %add_convert_fusion), channel_id=1, source_target_pairs={{0,2},{1,3},{2,0},{3,1},{4,6},{5,7},{6,4},{7,5},{8,10},{9,11},{10,... | collective-permute-start | bytes 2359304 | tf_op jit(solution)/shard_map/ppermute | solution.py:38
  224.2 34.3 %collective-permute-start.46 = (bf16[1,192,2048]{2,1,0:T(8,128)(2,1)S(1)}, bf16[1,192,2048]{2,1,0:T(8,128)(2,1)S(1)}, u32[]{:S(2)}, u32[]{:S(2)}) collective-permute-start(bf16[1,192,2048]{2,1,0:T(8,128)(2,1)S(1)} %add_convert_fusion.1), channel_id=1, source_target_pairs={{0,2},{1,3},{2,0},{3,1},{4,6},{5,7},{6,4},{7,5},{8,10},{9,11},{10,... | collective-permute-start | bytes 2359304 | tf_op jit(solution)/shard_map/ppermute | solution.py:38
  242.7 28.8 %collective-permute-start.51 = (bf16[48,2048]{1,0:T(8,128)(2,1)S(1)}, bf16[48,2048]{1,0:T(8,128)(2,1)S(1)}, u32[]{:S(2)}, u32[]{:S(2)}) collective-permute-start(bf16[48,2048]{1,0:T(8,128)(2,1)S(1)} %get-tuple-element.165), channel_id=1, source_target_pairs={{0,16},{4,20},{8,24},{12,28},{16,0},{20,4},{24,8},{28,12},{1,17},{... | collective-permute-start | bytes 589832 | tf_op jit(solution)/shard_map/ppermute | solution.py:38
  248.9 27.0 %collective-permute-start.52 = (bf16[48,2048]{1,0:T(8,128)(2,1)S(1)}, bf16[48,2048]{1,0:T(8,128)(2,1)S(1)}, u32[]{:S(2)}, u32[]{:S(2)}) collective-permute-start(bf16[48,2048]{1,0:T(8,128)(2,1)S(1)} %get-tuple-element.166), channel_id=1, source_target_pairs={{0,20},{4,16},{8,28},{12,24},{16,4},{20,0},{24,12},{28,8},{1,21},{... | collective-permute-start | bytes 589832 | tf_op jit(solution)/shard_map/ppermute | solution.py:38
  250.5 10.5 %collective-permute-start.30 = (f32[16,128]{1,0:T(8,128)S(1)}, f32[16,128]{1,0:T(8,128)S(1)}, u32[]{:S(2)}, u32[]{:S(2)}) collective-permute-start(f32[16,128]{1,0:T(8,128)S(1)} %add.28), channel_id=1, source_target_pairs={{0,2},{1,3},{2,0},{3,1},{4,6},{5,7},{6,4},{7,5},{8,10},{9,11},{10,... | collective-permute-start | bytes 24584 | tf_op jit(solution)/shard_map/ppermute | solution.py:38
  251.1 24.8 %collective-permute-start.53 = (bf16[48,2048]{1,0:T(8,128)(2,1)S(1)}, bf16[48,2048]{1,0:T(8,128)(2,1)S(1)}, u32[]{:S(2)}, u32[]{:S(2)}) collective-permute-start(bf16[48,2048]{1,0:T(8,128)(2,1)S(1)} %get-tuple-element.167), channel_id=1, source_target_pairs={{0,24},{4,28},{8,16},{12,20},{16,8},{20,12},{24,0},{28,4},{1,25},{... | collective-permute-start | bytes 589832 | tf_op jit(solution)/shard_map/ppermute | solution.py:38
  258.5 17.3 %collective-permute-start.54 = (bf16[48,2048]{1,0:T(8,128)(2,1)S(1)}, bf16[48,2048]{1,0:T(8,128)(2,1)S(1)}, u32[]{:S(2)}, u32[]{:S(2)}) collective-permute-start(bf16[48,2048]{1,0:T(8,128)(2,1)S(1)} %get-tuple-element.168), channel_id=1, source_target_pairs={{0,28},{4,24},{8,20},{12,16},{16,12},{20,8},{24,4},{28,0},{1,29},{... | collective-permute-start | bytes 589832 | tf_op jit(solution)/shard_map/ppermute | solution.py:38
  261.0 14.9 %collective-permute-start.47 = (bf16[48,2048]{1,0:T(8,128)(2,1)S(1)}, bf16[48,2048]{1,0:T(8,128)(2,1)S(1)}, u32[]{:S(2)}, u32[]{:S(2)}) collective-permute-start(bf16[48,2048]{1,0:T(8,128)(2,1)S(1)} %get-tuple-element.159), channel_id=1, source_target_pairs={{0,4},{4,0},{8,12},{12,8},{16,20},{20,16},{24,28},{28,24},{1,5},{5... | collective-permute-start | bytes 589832 | tf_op jit(solution)/shard_map/ppermute | solution.py:38
  271.5 8.1 %collective-permute-start.48 = (bf16[48,2048]{1,0:T(8,128)(2,1)S(1)}, bf16[48,2048]{1,0:T(8,128)(2,1)S(1)}, u32[]{:S(2)}, u32[]{:S(2)}) collective-permute-start(bf16[48,2048]{1,0:T(8,128)(2,1)S(1)} %get-tuple-element.160), channel_id=1, source_target_pairs={{0,8},{4,12},{8,0},{12,4},{16,24},{20,28},{24,16},{28,20},{1,9},{5... | collective-permute-start | bytes 589832 | tf_op jit(solution)/shard_map/ppermute | solution.py:38
  275.9 6.6 %collective-permute-start.49 = (bf16[48,2048]{1,0:T(8,128)(2,1)S(1)}, bf16[48,2048]{1,0:T(8,128)(2,1)S(1)}, u32[]{:S(2)}, u32[]{:S(2)}) collective-permute-start(bf16[48,2048]{1,0:T(8,128)(2,1)S(1)} %get-tuple-element.161), channel_id=1, source_target_pairs={{0,12},{4,8},{8,4},{12,0},{16,28},{20,24},{24,20},{28,16},{1,13},{... | collective-permute-start | bytes 589832 | tf_op jit(solution)/shard_map/ppermute | solution.py:38
  (17 other events, 113.0 us)

commit v2 on v1

--- a/solution.py
+++ b/solution.py
@@ -12,13 +12,13 @@
 LAYERS = 2
 ORDERS = (
     (
-        ("Wg0", 1), ("G", 0), ("S", 0), ("Ra", 1), ("Wu0", 1), ("Wd0", 1), ("Rb", 1),
-        ("Ca", 0), ("Cb", 1), ("Ea", 0), ("Xa", 1), ("Eb", 0), ("Xb", 1), ("Pb", 1),
-        ("Wd1", 1), ("Wu1", 1), ("Pa", 1), ("Wg1", 1),
+        ("S", 0), ("Ra", 1), ("Wg0", 1), ("Wd0", 1), ("Wu0", 1), ("Rb", 1), ("Ca", 0),
+        ("Ea", 0), ("Cb", 1), ("Xa", 0), ("Eb", 0), ("Xb", 1), ("Wg1", 1), ("Pb", 1),
+        ("Wu1", 1), ("Pa", 1), ("Wd1", 1),
     ),
     (
-        ("S", 1), ("Ra", 0), ("Rb", 0), ("Ca", 1), ("Ea", 1), ("Cb", 1), ("Eb", 0), ("Xb", 1),
-        ("Xa", 1), ("Pb", 1), ("Pa", 0),
+        ("S", 1), ("Ra", 0), ("Rb", 0), ("Ca", 1), ("Ea", 1), ("Cb", 1), ("Eb", 1), ("Xb", 1),
+        ("Xa", 0), ("Pb", 1), ("Pa", 1),
     ),
 )
 GROUPS = (
@@ -176,10 +176,10 @@
     )(words, scales)
 
 
-def expert_kernel(part_count, full_width, index_ref, *refs):
+def expert_kernel(part_count, full_width, layer_idx, index_ref, *refs):
     x_refs, refs = refs[:part_count], refs[part_count:]
-    gain_refs, refs = refs[:part_count], refs[part_count:]
-    split_ref, gate_hbm, up_hbm, down_hbm = refs[:4]
+    gains_ref, split_ref, gate_hbm, up_hbm, down_hbm = refs[:5]
+    refs = refs[1:]
     out_refs, refs = refs[4:6], refs[6:]
     gate_ref, up_ref, down_ref, gate_sem, up_sem, down_sem = refs
     width = x_refs[0].shape[1]
@@ -201,7 +201,8 @@
     gate = up = square = None
     for j in range(part_count):
         wide = x_refs[j][...].astype(jnp.float32)
-        rows = (wide * gain_refs[j][...]).astype(jnp.bfloat16)
+        gain = gains_ref[pl.ds((index_ref[0] ^ j) * LAYERS + layer_idx, 1), :]
+        rows = (wide * gain).astype(jnp.bfloat16)
         part = jnp.sum(wide * wide, axis=1, keepdims=True)
         square = part if j == 0 else square + part
         copies[0][j].wait()
@@ -223,16 +224,16 @@
         ).astype(jnp.bfloat16)
 
 
-def expert_parts(index, parts, gains, gate_w, up_w, down_w, split):
+def expert_parts(layer_idx, index, parts, gains, gate_w, up_w, down_w, split):
     part_count = len(parts)
     row_count, width = parts[0].shape
     full_width, hidden = gate_w.shape
     vmem = pl.BlockSpec(memory_space=pltpu.VMEM)
     hbm = pl.BlockSpec(memory_space=pltpu.HBM)
     return pl.pallas_call(
-        functools.partial(expert_kernel, part_count, full_width),
+        functools.partial(expert_kernel, part_count, full_width, layer_idx),
         in_specs=[pl.BlockSpec(memory_space=pltpu.SMEM)]
-        + [vmem] * (2 * part_count + 1)
+        + [vmem] * (part_count + 2)
         + [hbm] * 3,
         out_specs=[vmem] * 2,
         out_shape=[jax.ShapeDtypeStruct((part_count // 2, row_count, width), jnp.bfloat16)] * 2,
@@ -247,7 +248,7 @@
         compiler_params=pltpu.CompilerParams(vmem_limit_bytes=36 * MIB),
         cost_estimate=SHORT,
         name="expert_parts",
-    )(index, *parts, *gains, split, gate_w, up_w, down_w)
+    )(index, *parts, gains, split, gate_w, up_w, down_w)
 
 
 def add_split_kernel(term_count, *refs):
@@ -296,7 +297,7 @@
         out[...] = gathered[k * capacity : (k + 1) * capacity].astype(jnp.bfloat16)
 
 
-def enter_kernel(expert_count, me_ref, routes_ref, tokens_ref, gain_ref, router_ref, *refs):
+def enter_kernel(expert_count, part_count, me_ref, index_ref, routes_ref, tokens_ref, gain_ref, router_ref, *refs):
     picks_ref, stats_ref = refs[:2]
     slot_refs = refs[2:]
     token_count = tokens_ref.shape[0]
@@ -317,27 +318,32 @@
     picks_ref[...] = picks
     tokens = tokens_ref[...]
     fill_slots(picks, tokens, slot_refs)
-    logits, square = make_stats(tokens.astype(jnp.float32), gain_ref[...], router_ref[...])
-    stats_ref[0:expert_count, :] = logits
-    stats_ref[expert_count:, :] = square
-
-
-def enter(me, routes, tokens, gain, router, capacity):
+    logits, square = make_stats(tokens.astype(jnp.float32), gain_ref[0:1, :], router_ref[...])
+    stats_ref[...] = jnp.zeros_like(stats_ref)
+    stats_ref[0:expert_count, 0:token_count] = logits
+    stats_ref[expert_count : expert_count + 8, 0:token_count] = square
+    for part in range(part_count):
+        own = (index_ref[0] == part).astype(jnp.float32)
+        at = expert_count + 8 + part * LAYERS
+        stats_ref[at : at + LAYERS, :] = gain_ref[...] * own
+
+
+def enter(me, index, routes, tokens, gain, router, capacity, part_count):
     token_count, width = tokens.shape
     expert_count = router.shape[0]
     vmem = pl.BlockSpec(memory_space=pltpu.VMEM)
     return pl.pallas_call(
-        functools.partial(enter_kernel, expert_count),
-        in_specs=[pl.BlockSpec(memory_space=pltpu.SMEM)] + [vmem] * 4,
+        functools.partial(enter_kernel, expert_count, part_count),
+        in_specs=[pl.BlockSpec(memory_space=pltpu.SMEM)] * 2 + [vmem] * 4,
         out_shape=[
             jax.ShapeDtypeStruct((expert_count * capacity, token_count), jnp.bfloat16),
-            jax.ShapeDtypeStruct((expert_count + 8, token_count), jnp.float32),
+            jax.ShapeDtypeStruct((expert_count + 8 + part_count * LAYERS, width), jnp.float32),
         ]
         + [jax.ShapeDtypeStruct((capacity, width), jnp.bfloat16)] * expert_count,
         compiler_params=pltpu.CompilerParams(vmem_limit_bytes=32 * MIB),
         cost_estimate=SHORT,
         name="enter",
-    )(me, routes, tokens, gain, router)
+    )(me, index, routes, tokens, gain, router)
 
 
 def combine_kernel(expert_count, piece_count, full_width, last, me_ref, *refs):
@@ -452,7 +458,7 @@
     router_rows = jnp.swapaxes(router_weight, 1, 2)
 
     picks, stats, *slots = enter(
-        me, routes_rows, tokens, norm_gain[0:1], router_rows[0], capacity
+        me, index, routes_rows, tokens, norm_gain, router_rows[0], capacity, part_count
     )
     first_bits, core_bits = list(reversed(range(1, bits))), [0]
     stream = tokens
@@ -485,7 +491,7 @@
         for name, units in GROUPS
     }
     prepared = {}
-    whole_gain = None
+    gains = None
     for layer_idx in range(LAYERS):
         arrived = {0: slots[0]}
 
@@ -520,9 +526,10 @@
                 parts[name] = gather_parts(held, core_bits)
             elif kind == "E":
                 outs[name] = expert_parts(
+                    layer_idx,
                     wait(index),
                     [parts[name][j] for j in range(part_count)],
-                    [whole_gain[j][layer_idx : layer_idx + 1] for j in range(part_count)],
+                    gains,
                     *[prepared[w, layer_idx] for w in "gud"],
                     split,
                 )
@@ -551,10 +558,12 @@
                 stats = wait(stats)
                 for bit in range(bits):
                     stats = stats + exchange(stats, "tensor", 1 << bit)
+                if layer_idx == 0:
+                    gains = stats[expert_count + 8 :]
+                    stats = stats[: expert_count + 8, :token_count]
                 token = stats
-            elif kind == "G":
-                whole_gain = gather_parts({0: wait(norm_gain)}, first_bits + core_bits)
-                token = whole_gain
+            elif kind == "T":
+                token = stats
         following = None
         if layer_idx + 1 < LAYERS:
             following = [norm_gain[layer_idx + 1 : layer_idx + 2], router_rows[layer_idx + 1]]

time: 285 us -> 278 us (0.975)
  starting transfers between devices: 71.7 us -> 66.7 us
  local copies, waits for them, and re-layouts: 10.2 us -> 5.69 us
    ppermute x55 -> x52, starting transfers between devices: 71.7 us -> 66.7 us  [exchange(): lax.ppermute(shard, axis, [(i, i ^ mask) for i in range(lax.axis_size(axi...]
    unnamed x32 -> x34, local copies, waits for them, and re-layouts: 8.48 us -> 4.83 us
    ppermute x55 -> x52, waiting for transfers between devices: 126 us -> 128 us  [exchange(): lax.ppermute(shard, axis, [(i, i ^ mask) for i in range(lax.axis_size(axi...]
  transfers between devices with their start and end apart: 55 -> 52, of which waited for: 28 -> 32; matrix products, arithmetic and copies ran while one was open for 0% -> 1% of each run, Pallas kernels for 22% -> 20%
where the time goes in v2:
time: 278 us; the launch traced here: 277 us
  waiting for transfers between devices  128 us (46%)
  Pallas kernels  74.6 us (27%)
  starting transfers between devices  66.7 us (24%)
  local copies, waits for them, and re-layouts  5.69 us (2%)
    ppermute x52, waiting for transfers between devices, exchange(): lax.ppermute(shard, axis, [(i, i ^ mask) for i in range(lax.axis_size(axi...  128 us
    ppermute x52, starting transfers between devices, exchange(): lax.ppermute(shard, axis, [(i, i ^ mask) for i in range(lax.axis_size(axi...  66.7 us
    pallas_call x4, Pallas kernels, in_weights(): pl.pallas_call(functools.partial(in_weights_kernel, first_steps), grid=(f...  31.3 us
    pallas_call x4, Pallas kernels, expert_parts(): pl.pallas_call(functools.partial(expert_kernel, part_count, full_width, l...  29 us
    pallas_call x2, Pallas kernels, out_weights(): pl.pallas_call(out_weights_kernel, grid=(width // tile,), in_specs=[pl.Bl...  8.88 us
  transfers between devices with their start and end apart: 52, of which 32 were waited for; matrix products, arithmetic and copies ran while one was open for 1% of the time, Pallas kernels for 20%

profile of v2, /device:TPU:0, one launch (start us, length us, event | category | flops | bytes accessed | tf_op | source)
XLA Modules:
  0.0 277.0 jit_solution(17067111901987452312)
XLA Ops:
  5.8 2.9 %collective-permute-start.8 = (f32[24,2048]{1,0:T(8,128)S(1)}, f32[24,2048]{1,0:T(8,128)S(1)}, u32[]{:S(2)}, u32[]{:S(2)}) collective-permute-start(f32[24,2048]{1,0:T(8,128)S(1)} %add.24), channel_id=1, source_target_pairs={{0,2},{1,3},{2,0},{3,1},{4,6},{5,7},{6,4},{7,5},{8,10},{9,11},{10,... | collective-permute-start | bytes 589832 | tf_op jit(solution)/shard_map/ppermute | solution.py:38
  12.3 2.6 collective-permute-start
  14.9 2.9 %collective-permute-start.1 = (bf16[48,2048]{1,0:T(8,128)(2,1)S(1)}, bf16[48,2048]{1,0:T(8,128)(2,1)S(1)}, u32[]{:S(2)}, u32[]{:S(2)}) collective-permute-start(bf16[48,2048]{1,0:T(8,128)(2,1)S(1)} %get-tuple-element.91), channel_id=1, source_target_pairs={{0,20},{4,16},{8,28},{12,24},{16,4},{20,0},{24,12},{28,8},{1,21},{... | collective-permute-start | bytes 589832 | tf_op jit(solution)/shard_map/ppermute | solution.py:38
  17.8 2.0 collective-permute-start.2
  19.9 5.9 %collective-permute-done.5 = bf16[48,2048]{1,0:T(8,128)(2,1)S(1)} collective-permute-done((bf16[48,2048]{1,0:T(8,128)(2,1)S(1)}, bf16[48,2048]{1,0:T(8,128)(2,1)S(1)}, u32[]{:S(2)}, u32[]{:S(2)}) %collective-permute-start.5) | collective-permute-done | bytes 196640 | tf_op jit(solution)/shard_map/ppermute | solution.py:38
  28.5 7.8 %in_weights.4 = bf16[32,256,256]{2,1,0:T(8,128)(2,1)} custom-call(s32[2,1,4096,256]{3,2,1,0:T(8,128)} %words_ref.9, s32[2,1,64,256]{3,2,1,0:T(8,128)} %scales_ref.7, bf16[256,256]{1,0:T(8,128)(2,1)} %constant.13.clone.table_ref), custom_call_target="tpu_custom_call" | custom-call | flops 1000 | bytes 1000 | tf_op jit(solution)/shard_map/in_weights/pallas_call | solution.py:121
  36.3 4.4 %out_weights.2.refs_8_ = bf16[256,8192]{1,0:T(8,128)(2,1)} custom-call(s32[2,1,128,8192]{3,2,1,0:T(8,128)} %words_ref.11, s32[2,1,2,8192]{3,2,1,0:T(2,128)} %scales_ref.9), custom_call_target="tpu_custom_call" | custom-call | flops 1000 | bytes 1000 | tf_op jit(solution)/shard_map/out_weights/pallas_call | solution.py:164
  40.7 8.0 %in_weights.5 = bf16[32,256,256]{2,1,0:T(8,128)(2,1)} custom-call(s32[2,1,4096,256]{3,2,1,0:T(8,128)} %words_ref.10, s32[2,1,64,256]{3,2,1,0:T(8,128)} %scales_ref.8, bf16[256,256]{1,0:T(8,128)(2,1)} %constant.13.clone.table_ref), custom_call_target="tpu_custom_call" | custom-call | flops 1000 | bytes 1000 | tf_op jit(solution)/shard_map/in_weights/pallas_call | solution.py:121
  52.2 2.2 copy-done.3
  54.4 7.1 %expert_parts.4 = (bf16[2,192,2048]{2,1,0:T(8,128)(2,1)S(1)}, bf16[2,192,2048]{2,1,0:T(8,128)(2,1)S(1)}) custom-call(s32[1]{0:T(128)} %bitcast.1.index_ref, bf16[192,2048]{1,0:T(8,128)(2,1)S(1)} %constant_dynamic-update-slice_fusion.refs_0_, bf16[192,2048]{1,0:T(8,128)(2,1)S(1)} %collective-permute-done.11.refs_1_, ...), custom_call_target="tpu_custom_call" | custom-call | flops 1000 | bytes 1000 | tf_op jit(solution)/shard_map/expert_parts/pallas_call | solution.py:233
  61.6 7.4 %collective-permute-done.9.refs_2_ = bf16[192,2048]{1,0:T(8,128)(2,1)S(1)} collective-permute-done((bf16[192,2048]{1,0:T(8,128)(2,1)S(1)}, bf16[192,2048]{1,0:T(8,128)(2,1)S(1)}, u32[]{:S(2)}, u32[]{:S(2)}) %collective-permute-start.9) | collective-permute-done | bytes 786464 | tf_op jit(solution)/shard_map/ppermute | solution.py:38
  69.4 1.8 collective-permute-done.13.refs_1_
  72.3 7.3 %expert_parts.5 = (bf16[2,192,2048]{2,1,0:T(8,128)(2,1)S(1)}, bf16[2,192,2048]{2,1,0:T(8,128)(2,1)S(1)}) custom-call(s32[1]{0:T(128)} %bitcast.1.index_ref, bf16[192,2048]{1,0:T(8,128)(2,1)S(1)} %constant_dynamic-update-slice_fusion.4.refs_0_, bf16[192,2048]{1,0:T(8,128)(2,1)S(1)} %collective-permute-done.13.refs_1_, ...), custom_call_target="tpu_custom_call" | custom-call | flops 1000 | bytes 1000 | tf_op jit(solution)/shard_map/expert_parts/pallas_call | solution.py:233
  80.3 2.9 %collective-permute-done.15.refs_1_ = bf16[2,192,2048]{2,1,0:T(8,128)(2,1)S(1)} collective-permute-done((bf16[2,192,2048]{2,1,0:T(8,128)(2,1)S(1)}, bf16[2,192,2048]{2,1,0:T(8,128)(2,1)S(1)}, u32[]{:S(2)}, u32[]{:S(2)}) %collective-permute-start.15) | collective-permute-done | bytes 1572896 | tf_op jit(solution)/shard_map/ppermute | solution.py:38
  87.0 7.8 %in_weights.6 = bf16[32,256,256]{2,1,0:T(8,128)(2,1)} custom-call(s32[2,1,4096,256]{3,2,1,0:T(8,128)} %words_ref.9, s32[2,1,64,256]{3,2,1,0:T(8,128)} %scales_ref.7, bf16[256,256]{1,0:T(8,128)(2,1)} %constant.13.clone.table_ref), custom_call_target="tpu_custom_call" | custom-call | flops 1000 | bytes 1000 | tf_op jit(solution)/shard_map/in_weights/pallas_call | solution.py:121
  94.9 10.1 %collective-permute-done.16.refs_2_ = bf16[1,192,2048]{2,1,0:T(8,128)(2,1)S(1)} collective-permute-done((bf16[1,192,2048]{2,1,0:T(8,128)(2,1)}, bf16[1,192,2048]{2,1,0:T(8,128)(2,1)S(1)}, u32[]{:S(2)}, u32[]{:S(2)}) %collective-permute-start.16) | collective-permute-done | bytes 786464 | tf_op jit(solution)/shard_map/ppermute | solution.py:38
  105.2 3.6 %collective-permute-start.22 = (bf16[48,2048]{1,0:T(8,128)(2,1)S(1)}, bf16[48,2048]{1,0:T(8,128)(2,1)S(1)}, u32[]{:S(2)}, u32[]{:S(2)}) collective-permute-start(bf16[48,2048]{1,0:T(8,128)(2,1)S(1)} %get-tuple-element.123), channel_id=1, source_target_pairs={{0,16},{4,20},{8,24},{12,28},{16,0},{20,4},{24,8},{28,12},{1,17},{... | collective-permute-start | bytes 589832 | tf_op jit(solution)/shard_map/ppermute | solution.py:38
  109.6 2.1 collective-permute-start.24
  111.7 1.9 collective-permute-start.25
  113.6 7.8 %in_weights.7 = bf16[32,256,256]{2,1,0:T(8,128)(2,1)} custom-call(s32[2,1,4096,256]{3,2,1,0:T(8,128)} %words_ref.10, s32[2,1,64,256]{3,2,1,0:T(8,128)} %scales_ref.8, bf16[256,256]{1,0:T(8,128)(2,1)} %constant.13.clone.table_ref), custom_call_target="tpu_custom_call" | custom-call | flops 1000 | bytes 1000 | tf_op jit(solution)/shard_map/in_weights/pallas_call | solution.py:121
  123.3 6.0 %collective-permute-done.22.refs_8_ = bf16[48,2048]{1,0:T(8,128)(2,1)S(1)} collective-permute-done((bf16[48,2048]{1,0:T(8,128)(2,1)S(1)}, bf16[48,2048]{1,0:T(8,128)(2,1)S(1)}, u32[]{:S(2)}, u32[]{:S(2)}) %collective-permute-start.22) | collective-permute-done | bytes 196640 | tf_op jit(solution)/shard_map/ppermute | solution.py:38
  129.5 4.2 %collective-permute-done.23.refs_9_ = bf16[48,2048]{1,0:T(8,128)(2,1)S(1)} collective-permute-done((bf16[48,2048]{1,0:T(8,128)(2,1)S(1)}, bf16[48,2048]{1,0:T(8,128)(2,1)S(1)}, u32[]{:S(2)}, u32[]{:S(2)}) %collective-permute-start.23) | collective-permute-done | bytes 196640 | tf_op jit(solution)/shard_map/ppermute | solution.py:38
  134.4 4.5 %out_weights.3.refs_8_ = bf16[256,8192]{1,0:T(8,128)(2,1)} custom-call(s32[2,1,128,8192]{3,2,1,0:T(8,128)} %words_ref.11, s32[2,1,2,8192]{3,2,1,0:T(2,128)} %scales_ref.9), custom_call_target="tpu_custom_call" | custom-call | flops 1000 | bytes 1000 | tf_op jit(solution)/shard_map/out_weights/pallas_call | solution.py:164
  138.9 3.1 %collective-permute-done.21.refs_7_ = bf16[48,2048]{1,0:T(8,128)(2,1)S(1)} collective-permute-done((bf16[48,2048]{1,0:T(8,128)(2,1)S(1)}, bf16[48,2048]{1,0:T(8,128)(2,1)S(1)}, u32[]{:S(2)}, u32[]{:S(2)}) %collective-permute-start.21) | collective-permute-done | bytes 196640 | tf_op jit(solution)/shard_map/ppermute | solution.py:38
  144.9 3.2 %collective-permute-start.29 = (bf16[48,2048]{1,0:T(8,128)(2,1)S(1)}, bf16[48,2048]{1,0:T(8,128)(2,1)S(1)}, u32[]{:S(2)}, u32[]{:S(2)}) collective-permute-start(bf16[48,2048]{1,0:T(8,128)(2,1)S(1)} %get-tuple-element.142), channel_id=1, source_target_pairs={{0,8},{4,12},{8,0},{12,4},{16,24},{20,28},{24,16},{28,20},{1,9},{5... | collective-permute-start | bytes 589832 | tf_op jit(solution)/shard_map/ppermute | solution.py:38
  148.7 2.0 collective-permute-start.32
  153.5 5.7 %collective-permute-done.29 = bf16[48,2048]{1,0:T(8,128)(2,1)S(1)} collective-permute-done((bf16[48,2048]{1,0:T(8,128)(2,1)S(1)}, bf16[48,2048]{1,0:T(8,128)(2,1)S(1)}, u32[]{:S(2)}, u32[]{:S(2)}) %collective-permute-start.29) | collective-permute-done | bytes 196640 | tf_op jit(solution)/shard_map/ppermute | solution.py:38
  159.2 4.2 %collective-permute-start.35 = (bf16[48,2048]{1,0:T(8,128)(2,1)S(1)}, bf16[48,2048]{1,0:T(8,128)(2,1)S(1)}, u32[]{:S(2)}, u32[]{:S(2)}) collective-permute-start(bf16[48,2048]{1,0:T(8,128)(2,1)S(1)} %get-tuple-element.147), channel_id=1, source_target_pairs={{0,28},{4,24},{8,20},{12,16},{16,12},{20,8},{24,4},{28,0},{1,29},{... | collective-permute-start | bytes 589832 | tf_op jit(solution)/shard_map/ppermute | solution.py:38
  163.6 2.3 collective-permute-start.31
  165.9 8.5 %collective-permute-done.32 = bf16[48,2048]{1,0:T(8,128)(2,1)S(1)} collective-permute-done((bf16[48,2048]{1,0:T(8,128)(2,1)S(1)}, bf16[48,2048]{1,0:T(8,128)(2,1)S(1)}, u32[]{:S(2)}, u32[]{:S(2)}) %collective-permute-start.32) | collective-permute-done | bytes 196640 | tf_op jit(solution)/shard_map/ppermute | solution.py:38
  174.3 4.5 %collective-permute-done.33 = bf16[48,2048]{1,0:T(8,128)(2,1)S(1)} collective-permute-done((bf16[48,2048]{1,0:T(8,128)(2,1)S(1)}, bf16[48,2048]{1,0:T(8,128)(2,1)S(1)}, u32[]{:S(2)}, u32[]{:S(2)}) %collective-permute-start.33) | collective-permute-done | bytes 196640 | tf_op jit(solution)/shard_map/ppermute | solution.py:38
  178.9 3.8 %collective-permute-done.31.refs_2_ = bf16[192,2048]{1,0:T(8,128)(2,1)S(1)} collective-permute-done((bf16[192,2048]{1,0:T(8,128)(2,1)S(1)}, bf16[192,2048]{1,0:T(8,128)(2,1)S(1)}, u32[]{:S(2)}, u32[]{:S(2)}) %collective-permute-start.31) | collective-permute-done | bytes 786464 | tf_op jit(solution)/shard_map/ppermute | solution.py:38
  183.2 1.7 collective-permute-start.40
  186.1 7.4 %expert_parts.6 = (bf16[2,192,2048]{2,1,0:T(8,128)(2,1)S(1)}, bf16[2,192,2048]{2,1,0:T(8,128)(2,1)S(1)}) custom-call(s32[1]{0:T(128)} %bitcast.1.index_ref, bf16[192,2048]{1,0:T(8,128)(2,1)S(1)} %constant_dynamic-update-slice_fusion.8.refs_0_, bf16[192,2048]{1,0:T(8,128)(2,1)S(1)} %collective-permute-done.36.refs_1_, ...), custom_call_target="tpu_custom_call" | custom-call | flops 1000 | bytes 1000 | tf_op jit(solution)/shard_map/expert_parts/pallas_call | solution.py:233
  193.5 9.2 %collective-permute-done.40.refs_2_ = bf16[192,2048]{1,0:T(8,128)(2,1)S(1)} collective-permute-done((bf16[192,2048]{1,0:T(8,128)(2,1)S(1)}, bf16[192,2048]{1,0:T(8,128)(2,1)S(1)}, u32[]{:S(2)}, u32[]{:S(2)}) %collective-permute-start.40) | collective-permute-done | bytes 786464 | tf_op jit(solution)/shard_map/ppermute | solution.py:38
  203.1 1.8 collective-permute-done.41.refs_1_
  206.0 7.2 %expert_parts.7 = (bf16[2,192,2048]{2,1,0:T(8,128)(2,1)S(1)}, bf16[2,192,2048]{2,1,0:T(8,128)(2,1)S(1)}) custom-call(s32[1]{0:T(128)} %bitcast.1.index_ref, bf16[192,2048]{1,0:T(8,128)(2,1)S(1)} %constant_dynamic-update-slice_fusion.12.refs_0_, bf16[192,2048]{1,0:T(8,128)(2,1)S(1)} %collective-permute-done.41.refs_1_, ...), custom_call_target="tpu_custom_call" | custom-call | flops 1000 | bytes 1000 | tf_op jit(solution)/shard_map/expert_parts/pallas_call | solution.py:233
  213.8 2.9 %collective-permute-done.43.refs_1_ = bf16[2,192,2048]{2,1,0:T(8,128)(2,1)S(1)} collective-permute-done((bf16[2,192,2048]{2,1,0:T(8,128)(2,1)S(1)}, bf16[2,192,2048]{2,1,0:T(8,128)(2,1)S(1)}, u32[]{:S(2)}, u32[]{:S(2)}) %collective-permute-start.43) | collective-permute-done | bytes 1572896 | tf_op jit(solution)/shard_map/ppermute | solution.py:38
  216.9 1.8 collective-permute-start.44
  219.2 1.8 collective-permute-start.39
  221.0 16.4 %collective-permute-done.44.refs_2_ = bf16[1,192,2048]{2,1,0:T(8,128)(2,1)S(1)} collective-permute-done((bf16[1,192,2048]{2,1,0:T(8,128)(2,1)S(1)}, bf16[1,192,2048]{2,1,0:T(8,128)(2,1)S(1)}, u32[]{:S(2)}, u32[]{:S(2)}) %collective-permute-start.44) | collective-permute-done | bytes 786464 | tf_op jit(solution)/shard_map/ppermute | solution.py:38
  237.7 3.7 %collective-permute-start.48 = (bf16[48,2048]{1,0:T(8,128)(2,1)S(1)}, bf16[48,2048]{1,0:T(8,128)(2,1)S(1)}, u32[]{:S(2)}, u32[]{:S(2)}) collective-permute-start(bf16[48,2048]{1,0:T(8,128)(2,1)S(1)} %get-tuple-element.164), channel_id=1, source_target_pairs={{0,16},{4,20},{8,24},{12,28},{16,0},{20,4},{24,8},{28,12},{1,17},{... | collective-permute-start | bytes 589832 | tf_op jit(solution)/shard_map/ppermute | solution.py:38
  246.5 7.0 %collective-permute-done.39.refs_2_ = bf16[1,192,2048]{2,1,0:T(8,128)(2,1)S(1)} collective-permute-done((bf16[1,192,2048]{2,1,0:T(8,128)(2,1)S(1)}, bf16[1,192,2048]{2,1,0:T(8,128)(2,1)S(1)}, u32[]{:S(2)}, u32[]{:S(2)}) %collective-permute-start.39) | collective-permute-done | bytes 786464 | tf_op jit(solution)/shard_map/ppermute | solution.py:38
  255.3 2.2 collective-permute-start.45
  257.4 6.6 %collective-permute-done.48.refs_8_ = bf16[48,2048]{1,0:T(8,128)(2,1)S(1)} collective-permute-done((bf16[48,2048]{1,0:T(8,128)(2,1)S(1)}, bf16[48,2048]{1,0:T(8,128)(2,1)S(1)}, u32[]{:S(2)}, u32[]{:S(2)}) %collective-permute-start.48) | collective-permute-done | bytes 196640 | tf_op jit(solution)/shard_map/ppermute | solution.py:38
  264.0 4.9 %collective-permute-done.49.refs_9_ = bf16[48,2048]{1,0:T(8,128)(2,1)S(1)} collective-permute-done((bf16[48,2048]{1,0:T(8,128)(2,1)S(1)}, bf16[48,2048]{1,0:T(8,128)(2,1)S(1)}, u32[]{:S(2)}, u32[]{:S(2)}) %collective-permute-start.49) | collective-permute-done | bytes 196640 | tf_op jit(solution)/shard_map/ppermute | solution.py:38
  269.7 2.4 collective-permute-done.46.refs_6_
  272.1 3.3 %collective-permute-done.47.refs_7_ = bf16[48,2048]{1,0:T(8,128)(2,1)S(1)} collective-permute-done((bf16[48,2048]{1,0:T(8,128)(2,1)S(1)}, bf16[48,2048]{1,0:T(8,128)(2,1)S(1)}, u32[]{:S(2)}, u32[]{:S(2)}) %collective-permute-start.47) | collective-permute-done | bytes 196640 | tf_op jit(solution)/shard_map/ppermute | solution.py:38
  (123 shorter events, 46.0 us)
Async XLA Ops:
  5.8 9.0 %collective-permute-start.8 = (f32[24,2048]{1,0:T(8,128)S(1)}, f32[24,2048]{1,0:T(8,128)S(1)}, u32[]{:S(2)}, u32[]{:S(2)}) collective-permute-start(f32[24,2048]{1,0:T(8,128)S(1)} %add.24), channel_id=1, source_target_pairs={{0,2},{1,3},{2,0},{3,1},{4,6},{5,7},{6,4},{7,5},{8,10},{9,11},{10,... | collective-permute-start | bytes 589832 | tf_op jit(solution)/shard_map/ppermute | solution.py:38
  8.8 9.0 %collective-permute-start.4 = (bf16[48,2048]{1,0:T(8,128)(2,1)S(1)}, bf16[48,2048]{1,0:T(8,128)(2,1)S(1)}, u32[]{:S(2)}, u32[]{:S(2)}) collective-permute-start(bf16[48,2048]{1,0:T(8,128)(2,1)S(1)} %get-tuple-element.95), channel_id=1, source_target_pairs={{0,4},{4,0},{8,12},{12,8},{16,20},{20,16},{24,28},{28,24},{1,5},{5... | collective-permute-start | bytes 589832 | tf_op jit(solution)/shard_map/ppermute | solution.py:38
  10.3 15.5 %collective-permute-start.5 = (bf16[48,2048]{1,0:T(8,128)(2,1)S(1)}, bf16[48,2048]{1,0:T(8,128)(2,1)S(1)}, u32[]{:S(2)}, u32[]{:S(2)}) collective-permute-start(bf16[48,2048]{1,0:T(8,128)(2,1)S(1)} %get-tuple-element.96), channel_id=1, source_target_pairs={{0,8},{4,12},{8,0},{12,4},{16,24},{20,28},{24,16},{28,20},{1,9},{5... | collective-permute-start | bytes 589832 | tf_op jit(solution)/shard_map/ppermute | solution.py:38
  11.9 15.8 %collective-permute-start.6 = (bf16[48,2048]{1,0:T(8,128)(2,1)S(1)}, bf16[48,2048]{1,0:T(8,128)(2,1)S(1)}, u32[]{:S(2)}, u32[]{:S(2)}) collective-permute-start(bf16[48,2048]{1,0:T(8,128)(2,1)S(1)} %get-tuple-element.97), channel_id=1, source_target_pairs={{0,12},{4,8},{8,4},{12,0},{16,28},{20,24},{24,20},{28,16},{1,13},{... | collective-permute-start | bytes 589832 | tf_op jit(solution)/shard_map/ppermute | solution.py:38
  12.3 36.4 %collective-permute-start = (bf16[48,2048]{1,0:T(8,128)(2,1)S(1)}, bf16[48,2048]{1,0:T(8,128)(2,1)S(1)}, u32[]{:S(2)}, u32[]{:S(2)}) collective-permute-start(bf16[48,2048]{1,0:T(8,128)(2,1)S(1)} %get-tuple-element.90), channel_id=1, source_target_pairs={{0,16},{4,20},{8,24},{12,28},{16,0},{20,4},{24,8},{28,12},{1,17},{... | collective-permute-start | bytes 589832 | tf_op jit(solution)/shard_map/ppermute | solution.py:38
  14.9 33.8 %collective-permute-start.1 = (bf16[48,2048]{1,0:T(8,128)(2,1)S(1)}, bf16[48,2048]{1,0:T(8,128)(2,1)S(1)}, u32[]{:S(2)}, u32[]{:S(2)}) collective-permute-start(bf16[48,2048]{1,0:T(8,128)(2,1)S(1)} %get-tuple-element.91), channel_id=1, source_target_pairs={{0,20},{4,16},{8,28},{12,24},{16,4},{20,0},{24,12},{28,8},{1,21},{... | collective-permute-start | bytes 589832 | tf_op jit(solution)/shard_map/ppermute | solution.py:38
  17.8 30.8 %collective-permute-start.2 = (bf16[48,2048]{1,0:T(8,128)(2,1)S(1)}, bf16[48,2048]{1,0:T(8,128)(2,1)S(1)}, u32[]{:S(2)}, u32[]{:S(2)}) collective-permute-start(bf16[48,2048]{1,0:T(8,128)(2,1)S(1)} %get-tuple-element.92), channel_id=1, source_target_pairs={{0,24},{4,28},{8,16},{12,20},{16,8},{20,12},{24,0},{28,4},{1,25},{... | collective-permute-start | bytes 589832 | tf_op jit(solution)/shard_map/ppermute | solution.py:38
  25.8 22.9 %collective-permute-start.3 = (bf16[48,2048]{1,0:T(8,128)(2,1)S(1)}, bf16[48,2048]{1,0:T(8,128)(2,1)S(1)}, u32[]{:S(2)}, u32[]{:S(2)}) collective-permute-start(bf16[48,2048]{1,0:T(8,128)(2,1)S(1)} %get-tuple-element.93), channel_id=1, source_target_pairs={{0,28},{4,24},{8,20},{12,16},{16,12},{20,8},{24,4},{28,0},{1,29},{... | collective-permute-start | bytes 589832 | tf_op jit(solution)/shard_map/ppermute | solution.py:38
  27.7 21.0 %collective-permute-start.10 = (bf16[192,2048]{1,0:T(8,128)(2,1)S(1)}, bf16[192,2048]{1,0:T(8,128)(2,1)S(1)}, u32[]{:S(2)}, u32[]{:S(2)}) collective-permute-start(bf16[192,2048]{1,0:T(8,128)(2,1)S(1)} %constant_dynamic-update-slice_fusion.refs_0_), channel_id=1, source_target_pairs={{0,2},{1,3},{2,0},{3,1},{4,6},{5,7},{6,4},{7,5},{8,10},{9,11},{10,... | collective-permute-start | bytes 2359304 | tf_op jit(solution)/shard_map/ppermute | solution.py:38
  48.7 2.4 collective-permute-start.11
  48.8 3.4 %collective-permute-start.12 = (bf16[192,2048]{1,0:T(8,128)(2,1)S(1)}, bf16[192,2048]{1,0:T(8,128)(2,1)S(1)}, u32[]{:S(2)}, u32[]{:S(2)}) collective-permute-start(bf16[192,2048]{1,0:T(8,128)(2,1)S(1)} %collective-permute-done.10.refs_2_), channel_id=1, source_target_pairs={{0,1},{1,0},{2,3},{3,2},{4,5},{5,4},{6,7},{7,6},{8,9},{9,8},{10,11... | collective-permute-start | bytes 2359304 | tf_op jit(solution)/shard_map/ppermute | solution.py:38
  49.3 19.6 %collective-permute-start.9 = (bf16[192,2048]{1,0:T(8,128)(2,1)S(1)}, bf16[192,2048]{1,0:T(8,128)(2,1)S(1)}, u32[]{:S(2)}, u32[]{:S(2)}) collective-permute-start(bf16[192,2048]{1,0:T(8,128)(2,1)S(1)} %constant_dynamic-update-slice_fusion.4.refs_0_), channel_id=1, source_target_pairs={{0,2},{1,3},{2,0},{3,1},{4,6},{5,7},{6,4},{7,5},{8,10},{9,11},{10,... | collective-permute-start | bytes 2359304 | tf_op jit(solution)/shard_map/ppermute | solution.py:38
  68.9 2.3 collective-permute-start.13
  68.9 3.4 %collective-permute-start.14 = (bf16[192,2048]{1,0:T(8,128)(2,1)S(1)}, bf16[192,2048]{1,0:T(8,128)(2,1)S(1)}, u32[]{:S(2)}, u32[]{:S(2)}) collective-permute-start(bf16[192,2048]{1,0:T(8,128)(2,1)S(1)} %collective-permute-done.9.refs_2_), channel_id=1, source_target_pairs={{0,1},{1,0},{2,3},{3,2},{4,5},{5,4},{6,7},{7,6},{8,9},{9,8},{10,11... | collective-permute-start | bytes 2359304 | tf_op jit(solution)/shard_map/ppermute | solution.py:38
  79.7 3.5 %collective-permute-start.15 = (bf16[2,192,2048]{2,1,0:T(8,128)(2,1)S(1)}, bf16[2,192,2048]{2,1,0:T(8,128)(2,1)S(1)}, u32[]{:S(2)}, u32[]{:S(2)}) collective-permute-start(bf16[2,192,2048]{2,1,0:T(8,128)(2,1)S(1)} %get-tuple-element.117), channel_id=1, source_target_pairs={{0,1},{1,0},{2,3},{3,2},{4,5},{5,4},{6,7},{7,6},{8,9},{9,8},{10,11... | collective-permute-start | bytes 4718600 | tf_op jit(solution)/shard_map/ppermute | solution.py:38
  79.9 5.7 %collective-permute-start.17 = (bf16[2,192,2048]{2,1,0:T(8,128)(2,1)S(1)}, bf16[2,192,2048]{2,1,0:T(8,128)(2,1)S(1)}, u32[]{:S(2)}, u32[]{:S(2)}) collective-permute-start(bf16[2,192,2048]{2,1,0:T(8,128)(2,1)S(1)} %get-tuple-element.112), channel_id=1, source_target_pairs={{0,1},{1,0},{2,3},{3,2},{4,5},{5,4},{6,7},{7,6},{8,9},{9,8},{10,11... | collective-permute-start | bytes 4718600 | tf_op jit(solution)/shard_map/ppermute | solution.py:38
  84.3 20.6 %collective-permute-start.16 = (bf16[1,192,2048]{2,1,0:T(8,128)(2,1)}, bf16[1,192,2048]{2,1,0:T(8,128)(2,1)S(1)}, u32[]{:S(2)}, u32[]{:S(2)}) collective-permute-start(bf16[1,192,2048]{2,1,0:T(8,128)(2,1)} %add_convert_fusion.3), channel_id=1, source_target_pairs={{0,2},{1,3},{2,0},{3,1},{4,6},{5,7},{6,4},{7,5},{8,10},{9,11},{10,... | collective-permute-start | bytes 2359304 | tf_op jit(solution)/shard_map/ppermute | solution.py:38
  85.9 35.5 %collective-permute-start.18 = (bf16[1,192,2048]{2,1,0:T(8,128)(2,1)S(1)}, bf16[1,192,2048]{2,1,0:T(8,128)(2,1)S(1)}, u32[]{:S(2)}, u32[]{:S(2)}) collective-permute-start(bf16[1,192,2048]{2,1,0:T(8,128)(2,1)S(1)} %add_convert_fusion.2), channel_id=1, source_target_pairs={{0,2},{1,3},{2,0},{3,1},{4,6},{5,7},{6,4},{7,5},{8,10},{9,11},{10,... | collective-permute-start | bytes 2359304 | tf_op jit(solution)/shard_map/ppermute | solution.py:38
  105.2 24.1 %collective-permute-start.22 = (bf16[48,2048]{1,0:T(8,128)(2,1)S(1)}, bf16[48,2048]{1,0:T(8,128)(2,1)S(1)}, u32[]{:S(2)}, u32[]{:S(2)}) collective-permute-start(bf16[48,2048]{1,0:T(8,128)(2,1)S(1)} %get-tuple-element.123), channel_id=1, source_target_pairs={{0,16},{4,20},{8,24},{12,28},{16,0},{20,4},{24,8},{28,12},{1,17},{... | collective-permute-start | bytes 589832 | tf_op jit(solution)/shard_map/ppermute | solution.py:38
  108.8 24.9 %collective-permute-start.23 = (bf16[48,2048]{1,0:T(8,128)(2,1)S(1)}, bf16[48,2048]{1,0:T(8,128)(2,1)S(1)}, u32[]{:S(2)}, u32[]{:S(2)}) collective-permute-start(bf16[48,2048]{1,0:T(8,128)(2,1)S(1)} %get-tuple-element.124), channel_id=1, source_target_pairs={{0,20},{4,16},{8,28},{12,24},{16,4},{20,0},{24,12},{28,8},{1,21},{... | collective-permute-start | bytes 589832 | tf_op jit(solution)/shard_map/ppermute | solution.py:38
  109.6 29.3 %collective-permute-start.24 = (bf16[48,2048]{1,0:T(8,128)(2,1)S(1)}, bf16[48,2048]{1,0:T(8,128)(2,1)S(1)}, u32[]{:S(2)}, u32[]{:S(2)}) collective-permute-start(bf16[48,2048]{1,0:T(8,128)(2,1)S(1)} %get-tuple-element.125), channel_id=1, source_target_pairs={{0,24},{4,28},{8,16},{12,20},{16,8},{20,12},{24,0},{28,4},{1,25},{... | collective-permute-start | bytes 589832 | tf_op jit(solution)/shard_map/ppermute | solution.py:38
  111.7 27.2 %collective-permute-start.25 = (bf16[48,2048]{1,0:T(8,128)(2,1)S(1)}, bf16[48,2048]{1,0:T(8,128)(2,1)S(1)}, u32[]{:S(2)}, u32[]{:S(2)}) collective-permute-start(bf16[48,2048]{1,0:T(8,128)(2,1)S(1)} %get-tuple-element.126), channel_id=1, source_target_pairs={{0,28},{4,24},{8,20},{12,16},{16,12},{20,8},{24,4},{28,0},{1,29},{... | collective-permute-start | bytes 589832 | tf_op jit(solution)/shard_map/ppermute | solution.py:38
  121.7 17.2 %collective-permute-start.19 = (bf16[48,2048]{1,0:T(8,128)(2,1)S(1)}, bf16[48,2048]{1,0:T(8,128)(2,1)S(1)}, u32[]{:S(2)}, u32[]{:S(2)}) collective-permute-start(bf16[48,2048]{1,0:T(8,128)(2,1)S(1)} %get-tuple-element.132), channel_id=1, source_target_pairs={{0,4},{4,0},{8,12},{12,8},{16,20},{20,16},{24,28},{28,24},{1,5},{5... | collective-permute-start | bytes 589832 | tf_op jit(solution)/shard_map/ppermute | solution.py:38
  129.3 9.6 %collective-permute-start.20 = (bf16[48,2048]{1,0:T(8,128)(2,1)S(1)}, bf16[48,2048]{1,0:T(8,128)(2,1)S(1)}, u32[]{:S(2)}, u32[]{:S(2)}) collective-permute-start(bf16[48,2048]{1,0:T(8,128)(2,1)S(1)} %get-tuple-element.133), channel_id=1, source_target_pairs={{0,8},{4,12},{8,0},{12,4},{16,24},{20,28},{24,16},{28,20},{1,9},{5... | collective-permute-start | bytes 589832 | tf_op jit(solution)/shard_map/ppermute | solution.py:38
  133.8 8.3 %collective-permute-start.21 = (bf16[48,2048]{1,0:T(8,128)(2,1)S(1)}, bf16[48,2048]{1,0:T(8,128)(2,1)S(1)}, u32[]{:S(2)}, u32[]{:S(2)}) collective-permute-start(bf16[48,2048]{1,0:T(8,128)(2,1)S(1)} %get-tuple-element.134), channel_id=1, source_target_pairs={{0,12},{4,8},{8,4},{12,0},{16,28},{20,24},{24,20},{28,16},{1,13},{... | collective-permute-start | bytes 589832 | tf_op jit(solution)/shard_map/ppermute | solution.py:38
  143.7 8.3 %collective-permute-start.28 = (bf16[48,2048]{1,0:T(8,128)(2,1)S(1)}, bf16[48,2048]{1,0:T(8,128)(2,1)S(1)}, u32[]{:S(2)}, u32[]{:S(2)}) collective-permute-start(bf16[48,2048]{1,0:T(8,128)(2,1)S(1)} %get-tuple-element.141), channel_id=1, source_target_pairs={{0,4},{4,0},{8,12},{12,8},{16,20},{20,16},{24,28},{28,24},{1,5},{5... | collective-permute-start | bytes 589832 | tf_op jit(solution)/shard_map/ppermute | solution.py:38
  144.9 14.3 %collective-permute-start.29 = (bf16[48,2048]{1,0:T(8,128)(2,1)S(1)}, bf16[48,2048]{1,0:T(8,128)(2,1)S(1)}, u32[]{:S(2)}, u32[]{:S(2)}) collective-permute-start(bf16[48,2048]{1,0:T(8,128)(2,1)S(1)} %get-tuple-element.142), channel_id=1, source_target_pairs={{0,8},{4,12},{8,0},{12,4},{16,24},{20,28},{24,16},{28,20},{1,9},{5... | collective-permute-start | bytes 589832 | tf_op jit(solution)/shard_map/ppermute | solution.py:38
  148.1 15.5 %collective-permute-start.30 = (bf16[48,2048]{1,0:T(8,128)(2,1)S(1)}, bf16[48,2048]{1,0:T(8,128)(2,1)S(1)}, u32[]{:S(2)}, u32[]{:S(2)}) collective-permute-start(bf16[48,2048]{1,0:T(8,128)(2,1)S(1)} %get-tuple-element.143), channel_id=1, source_target_pairs={{0,12},{4,8},{8,4},{12,0},{16,28},{20,24},{24,20},{28,16},{1,13},{... | collective-permute-start | bytes 589832 | tf_op jit(solution)/shard_map/ppermute | solution.py:38
  148.7 25.6 %collective-permute-start.32 = (bf16[48,2048]{1,0:T(8,128)(2,1)S(1)}, bf16[48,2048]{1,0:T(8,128)(2,1)S(1)}, u32[]{:S(2)}, u32[]{:S(2)}) collective-permute-start(bf16[48,2048]{1,0:T(8,128)(2,1)S(1)} %get-tuple-element.144), channel_id=1, source_target_pairs={{0,16},{4,20},{8,24},{12,28},{16,0},{20,4},{24,8},{28,12},{1,17},{... | collective-permute-start | bytes 589832 | tf_op jit(solution)/shard_map/ppermute | solution.py:38
  150.7 28.1 %collective-permute-start.33 = (bf16[48,2048]{1,0:T(8,128)(2,1)S(1)}, bf16[48,2048]{1,0:T(8,128)(2,1)S(1)}, u32[]{:S(2)}, u32[]{:S(2)}) collective-permute-start(bf16[48,2048]{1,0:T(8,128)(2,1)S(1)} %get-tuple-element.145), channel_id=1, source_target_pairs={{0,20},{4,16},{8,28},{12,24},{16,4},{20,0},{24,12},{28,8},{1,21},{... | collective-permute-start | bytes 589832 | tf_op jit(solution)/shard_map/ppermute | solution.py:38
  151.9 26.9 %collective-permute-start.34 = (bf16[48,2048]{1,0:T(8,128)(2,1)S(1)}, bf16[48,2048]{1,0:T(8,128)(2,1)S(1)}, u32[]{:S(2)}, u32[]{:S(2)}) collective-permute-start(bf16[48,2048]{1,0:T(8,128)(2,1)S(1)} %get-tuple-element.146), channel_id=1, source_target_pairs={{0,24},{4,28},{8,16},{12,20},{16,8},{20,12},{24,0},{28,4},{1,25},{... | collective-permute-start | bytes 589832 | tf_op jit(solution)/shard_map/ppermute | solution.py:38
  159.2 19.6 %collective-permute-start.35 = (bf16[48,2048]{1,0:T(8,128)(2,1)S(1)}, bf16[48,2048]{1,0:T(8,128)(2,1)S(1)}, u32[]{:S(2)}, u32[]{:S(2)}) collective-permute-start(bf16[48,2048]{1,0:T(8,128)(2,1)S(1)} %get-tuple-element.147), channel_id=1, source_target_pairs={{0,28},{4,24},{8,20},{12,16},{16,12},{20,8},{24,4},{28,0},{1,29},{... | collective-permute-start | bytes 589832 | tf_op jit(solution)/shard_map/ppermute | solution.py:38
  163.6 19.1 %collective-permute-start.31 = (bf16[192,2048]{1,0:T(8,128)(2,1)S(1)}, bf16[192,2048]{1,0:T(8,128)(2,1)S(1)}, u32[]{:S(2)}, u32[]{:S(2)}) collective-permute-start(bf16[192,2048]{1,0:T(8,128)(2,1)S(1)} %constant_dynamic-update-slice_fusion.8.refs_0_), channel_id=1, source_target_pairs={{0,2},{1,3},{2,0},{3,1},{4,6},{5,7},{6,4},{7,5},{8,10},{9,11},{10,... | collective-permute-start | bytes 2359304 | tf_op jit(solution)/shard_map/ppermute | solution.py:38
  182.7 3.4 %collective-permute-start.37 = (bf16[192,2048]{1,0:T(8,128)(2,1)S(1)}, bf16[192,2048]{1,0:T(8,128)(2,1)S(1)}, u32[]{:S(2)}, u32[]{:S(2)}) collective-permute-start(bf16[192,2048]{1,0:T(8,128)(2,1)S(1)} %collective-permute-done.31.refs_2_), channel_id=1, source_target_pairs={{0,1},{1,0},{2,3},{3,2},{4,5},{5,4},{6,7},{7,6},{8,9},{9,8},{10,11... | collective-permute-start | bytes 2359304 | tf_op jit(solution)/shard_map/ppermute | solution.py:38
  183.2 19.4 %collective-permute-start.40 = (bf16[192,2048]{1,0:T(8,128)(2,1)S(1)}, bf16[192,2048]{1,0:T(8,128)(2,1)S(1)}, u32[]{:S(2)}, u32[]{:S(2)}) collective-permute-start(bf16[192,2048]{1,0:T(8,128)(2,1)S(1)} %constant_dynamic-update-slice_fusion.12.refs_0_), channel_id=1, source_target_pairs={{0,2},{1,3},{2,0},{3,1},{4,6},{5,7},{6,4},{7,5},{8,10},{9,11},{10,... | collective-permute-start | bytes 2359304 | tf_op jit(solution)/shard_map/ppermute | solution.py:38
  202.6 3.4 %collective-permute-start.42 = (bf16[192,2048]{1,0:T(8,128)(2,1)S(1)}, bf16[192,2048]{1,0:T(8,128)(2,1)S(1)}, u32[]{:S(2)}, u32[]{:S(2)}) collective-permute-start(bf16[192,2048]{1,0:T(8,128)(2,1)S(1)} %collective-permute-done.40.refs_2_), channel_id=1, source_target_pairs={{0,1},{1,0},{2,3},{3,2},{4,5},{5,4},{6,7},{7,6},{8,9},{9,8},{10,11... | collective-permute-start | bytes 2359304 | tf_op jit(solution)/shard_map/ppermute | solution.py:38
  213.2 3.5 %collective-permute-start.43 = (bf16[2,192,2048]{2,1,0:T(8,128)(2,1)S(1)}, bf16[2,192,2048]{2,1,0:T(8,128)(2,1)S(1)}, u32[]{:S(2)}, u32[]{:S(2)}) collective-permute-start(bf16[2,192,2048]{2,1,0:T(8,128)(2,1)S(1)} %get-tuple-element.159), channel_id=1, source_target_pairs={{0,1},{1,0},{2,3},{3,2},{4,5},{5,4},{6,7},{7,6},{8,9},{9,8},{10,11... | collective-permute-start | bytes 4718600 | tf_op jit(solution)/shard_map/ppermute | solution.py:38
  213.4 5.5 %collective-permute-start.38 = (bf16[2,192,2048]{2,1,0:T(8,128)(2,1)S(1)}, bf16[2,192,2048]{2,1,0:T(8,128)(2,1)S(1)}, u32[]{:S(2)}, u32[]{:S(2)}) collective-permute-start(bf16[2,192,2048]{2,1,0:T(8,128)(2,1)S(1)} %get-tuple-element.153), channel_id=1, source_target_pairs={{0,1},{1,0},{2,3},{3,2},{4,5},{5,4},{6,7},{7,6},{8,9},{9,8},{10,11... | collective-permute-start | bytes 4718600 | tf_op jit(solution)/shard_map/ppermute | solution.py:38
  216.9 20.5 %collective-permute-start.44 = (bf16[1,192,2048]{2,1,0:T(8,128)(2,1)S(1)}, bf16[1,192,2048]{2,1,0:T(8,128)(2,1)S(1)}, u32[]{:S(2)}, u32[]{:S(2)}) collective-permute-start(bf16[1,192,2048]{2,1,0:T(8,128)(2,1)S(1)} %add_convert_fusion), channel_id=1, source_target_pairs={{0,2},{1,3},{2,0},{3,1},{4,6},{5,7},{6,4},{7,5},{8,10},{9,11},{10,... | collective-permute-start | bytes 2359304 | tf_op jit(solution)/shard_map/ppermute | solution.py:38
  219.2 34.4 %collective-permute-start.39 = (bf16[1,192,2048]{2,1,0:T(8,128)(2,1)S(1)}, bf16[1,192,2048]{2,1,0:T(8,128)(2,1)S(1)}, u32[]{:S(2)}, u32[]{:S(2)}) collective-permute-start(bf16[1,192,2048]{2,1,0:T(8,128)(2,1)S(1)} %add_convert_fusion.1), channel_id=1, source_target_pairs={{0,2},{1,3},{2,0},{3,1},{4,6},{5,7},{6,4},{7,5},{8,10},{9,11},{10,... | collective-permute-start | bytes 2359304 | tf_op jit(solution)/shard_map/ppermute | solution.py:38
  237.7 26.3 %collective-permute-start.48 = (bf16[48,2048]{1,0:T(8,128)(2,1)S(1)}, bf16[48,2048]{1,0:T(8,128)(2,1)S(1)}, u32[]{:S(2)}, u32[]{:S(2)}) collective-permute-start(bf16[48,2048]{1,0:T(8,128)(2,1)S(1)} %get-tuple-element.164), channel_id=1, source_target_pairs={{0,16},{4,20},{8,24},{12,28},{16,0},{20,4},{24,8},{28,12},{1,17},{... | collective-permute-start | bytes 589832 | tf_op jit(solution)/shard_map/ppermute | solution.py:38
  241.4 27.5 %collective-permute-start.49 = (bf16[48,2048]{1,0:T(8,128)(2,1)S(1)}, bf16[48,2048]{1,0:T(8,128)(2,1)S(1)}, u32[]{:S(2)}, u32[]{:S(2)}) collective-permute-start(bf16[48,2048]{1,0:T(8,128)(2,1)S(1)} %get-tuple-element.165), channel_id=1, source_target_pairs={{0,20},{4,16},{8,28},{12,24},{16,4},{20,0},{24,12},{28,8},{1,21},{... | collective-permute-start | bytes 589832 | tf_op jit(solution)/shard_map/ppermute | solution.py:38
  243.3 11.9 %collective-permute-start.27 = (f32[16,128]{1,0:T(8,128)S(1)}, f32[16,128]{1,0:T(8,128)S(1)}, u32[]{:S(2)}, u32[]{:S(2)}) collective-permute-start(f32[16,128]{1,0:T(8,128)S(1)} %add.28), channel_id=1, source_target_pairs={{0,2},{1,3},{2,0},{3,1},{4,6},{5,7},{6,4},{7,5},{8,10},{9,11},{10,... | collective-permute-start | bytes 24584 | tf_op jit(solution)/shard_map/ppermute | solution.py:38
  245.1 23.8 %collective-permute-start.50 = (bf16[48,2048]{1,0:T(8,128)(2,1)S(1)}, bf16[48,2048]{1,0:T(8,128)(2,1)S(1)}, u32[]{:S(2)}, u32[]{:S(2)}) collective-permute-start(bf16[48,2048]{1,0:T(8,128)(2,1)S(1)} %get-tuple-element.166), channel_id=1, source_target_pairs={{0,24},{4,28},{8,16},{12,20},{16,8},{20,12},{24,0},{28,4},{1,25},{... | collective-permute-start | bytes 589832 | tf_op jit(solution)/shard_map/ppermute | solution.py:38
  253.6 15.3 %collective-permute-start.51 = (bf16[48,2048]{1,0:T(8,128)(2,1)S(1)}, bf16[48,2048]{1,0:T(8,128)(2,1)S(1)}, u32[]{:S(2)}, u32[]{:S(2)}) collective-permute-start(bf16[48,2048]{1,0:T(8,128)(2,1)S(1)} %get-tuple-element.167), channel_id=1, source_target_pairs={{0,28},{4,24},{8,20},{12,16},{16,12},{20,8},{24,4},{28,0},{1,29},{... | collective-permute-start | bytes 589832 | tf_op jit(solution)/shard_map/ppermute | solution.py:38
  255.3 14.4 %collective-permute-start.45 = (bf16[48,2048]{1,0:T(8,128)(2,1)S(1)}, bf16[48,2048]{1,0:T(8,128)(2,1)S(1)}, u32[]{:S(2)}, u32[]{:S(2)}) collective-permute-start(bf16[48,2048]{1,0:T(8,128)(2,1)S(1)} %get-tuple-element.172), channel_id=1, source_target_pairs={{0,4},{4,0},{8,12},{12,8},{16,20},{20,16},{24,28},{28,24},{1,5},{5... | collective-permute-start | bytes 589832 | tf_op jit(solution)/shard_map/ppermute | solution.py:38
  264.0 8.1 %collective-permute-start.46 = (bf16[48,2048]{1,0:T(8,128)(2,1)S(1)}, bf16[48,2048]{1,0:T(8,128)(2,1)S(1)}, u32[]{:S(2)}, u32[]{:S(2)}) collective-permute-start(bf16[48,2048]{1,0:T(8,128)(2,1)S(1)} %get-tuple-element.173), channel_id=1, source_target_pairs={{0,8},{4,12},{8,0},{12,4},{16,24},{20,28},{24,16},{28,20},{1,9},{5... | collective-permute-start | bytes 589832 | tf_op jit(solution)/shard_map/ppermute | solution.py:38
  268.9 6.6 %collective-permute-start.47 = (bf16[48,2048]{1,0:T(8,128)(2,1)S(1)}, bf16[48,2048]{1,0:T(8,128)(2,1)S(1)}, u32[]{:S(2)}, u32[]{:S(2)}) collective-permute-start(bf16[48,2048]{1,0:T(8,128)(2,1)S(1)} %get-tuple-element.174), channel_id=1, source_target_pairs={{0,12},{4,8},{8,4},{12,0},{16,28},{20,24},{24,20},{28,16},{1,13},{... | collective-permute-start | bytes 589832 | tf_op jit(solution)/shard_map/ppermute | solution.py:38
  (15 other events, 151.2 us)

commit v3 on v2

--- a/solution.py
+++ b/solution.py
@@ -178,26 +178,10 @@
 
 def expert_kernel(part_count, full_width, layer_idx, index_ref, *refs):
     x_refs, refs = refs[:part_count], refs[part_count:]
-    gains_ref, split_ref, gate_hbm, up_hbm, down_hbm = refs[:5]
+    gains_ref, split_ref, gate_ref, up_ref, down_ref = refs[:5]
     refs = refs[1:]
     out_refs, refs = refs[4:6], refs[6:]
-    gate_ref, up_ref, down_ref, gate_sem, up_sem, down_sem = refs
     width = x_refs[0].shape[1]
-    copies = [[], [], []]
-    for j in range(part_count):
-        at = pl.ds(pl.multiple_of((index_ref[0] ^ j) * width, width), width)
-        copies[0].append(
-            pltpu.make_async_copy(gate_hbm.at[at, :], gate_ref.at[j], gate_sem.at[j])
-        )
-        copies[1].append(pltpu.make_async_copy(up_hbm.at[at, :], up_ref.at[j], up_sem.at[j]))
-        copies[2].append(
-            pltpu.make_async_copy(down_hbm.at[:, at], down_ref.at[j], down_sem.at[j])
-        )
-    for j in range(part_count):
-        copies[0][j].start()
-        copies[1][j].start()
-    for j in range(part_count):
-        copies[2][j].start()
     gate = up = square = None
     for j in range(part_count):
         wide = x_refs[j][...].astype(jnp.float32)
@@ -205,11 +189,10 @@
         rows = (wide * gain).astype(jnp.bfloat16)
         part = jnp.sum(wide * wide, axis=1, keepdims=True)
         square = part if j == 0 else square + part
-        copies[0][j].wait()
-        part = jnp.dot(rows, gate_ref[j], preferred_element_type=jnp.float32)
+        at = pl.ds(pl.multiple_of((index_ref[0] ^ j) * width, width), width)
+        part = jnp.dot(rows, gate_ref[at, :], preferred_element_type=jnp.float32)
         gate = part if j == 0 else gate + part
-        copies[1][j].wait()
-        part = jnp.dot(rows, up_ref[j], preferred_element_type=jnp.float32)
+        part = jnp.dot(rows, up_ref[at, :], preferred_element_type=jnp.float32)
         up = part if j == 0 else up + part
     scale = lax.rsqrt(square / full_width + 1e-05) * (1.0 / math.sqrt(full_width))
     gate = gate * scale
@@ -218,9 +201,9 @@
         act.astype(jnp.bfloat16), split_ref[...], preferred_element_type=jnp.float32
     ).astype(jnp.bfloat16)
     for j in range(part_count):
-        copies[2][j].wait()
+        at = pl.ds(pl.multiple_of((index_ref[0] ^ j) * width, width), width)
         out_refs[j % 2][j // 2] = jnp.dot(
-            act, down_ref[j], preferred_element_type=jnp.float32
+            act, down_ref[:, at], preferred_element_type=jnp.float32
         ).astype(jnp.bfloat16)
 
 
@@ -229,23 +212,13 @@
     row_count, width = parts[0].shape
     full_width, hidden = gate_w.shape
     vmem = pl.BlockSpec(memory_space=pltpu.VMEM)
-    hbm = pl.BlockSpec(memory_space=pltpu.HBM)
     return pl.pallas_call(
         functools.partial(expert_kernel, part_count, full_width, layer_idx),
         in_specs=[pl.BlockSpec(memory_space=pltpu.SMEM)]
-        + [vmem] * (part_count + 2)
-        + [hbm] * 3,
+        + [vmem] * (part_count + 5),
         out_specs=[vmem] * 2,
         out_shape=[jax.ShapeDtypeStruct((part_count // 2, row_count, width), jnp.bfloat16)] * 2,
-        scratch_shapes=[
-            pltpu.VMEM((part_count, width, hidden), jnp.bfloat16),
-            pltpu.VMEM((part_count, width, hidden), jnp.bfloat16),
-            pltpu.VMEM((part_count, hidden, width), jnp.bfloat16),
-            pltpu.SemaphoreType.DMA((part_count,)),
-            pltpu.SemaphoreType.DMA((part_count,)),
-            pltpu.SemaphoreType.DMA((part_count,)),
-        ],
-        compiler_params=pltpu.CompilerParams(vmem_limit_bytes=36 * MIB),
+        compiler_params=pltpu.CompilerParams(vmem_limit_bytes=16 * MIB),
         cost_estimate=SHORT,
         name="expert_parts",
     )(index, *parts, gains, split, gate_w, up_w, down_w)

time: 278 us -> 274 us (0.986)
  Pallas kernels: 74.6 us -> 59.4 us
  local copies, waits for them, and re-layouts: 5.69 us -> 15.6 us
    pallas_call x4, Pallas kernels: 29 us -> 12.1 us  [expert_parts(): pl.pallas_call(functools.partial(expert_kernel, part_count, full_width, l...]
    unnamed x34 -> x52, local copies, waits for them, and re-layouts: 4.83 us -> 13 us
  transfers between devices with their start and end apart: 52 -> 52, of which waited for: 32 -> 31; matrix products, arithmetic and copies ran while one was open for 1% -> 2% of each run, Pallas kernels for 20% -> 18%
where the time goes in v3:
time: 274 us; the launch traced here: 273 us
  waiting for transfers between devices  130 us (47%)
  starting transfers between devices  65.4 us (24%)
  Pallas kernels  59.4 us (22%)
  local copies, waits for them, and re-layouts  15.6 us (6%)
    ppermute x52, waiting for transfers between devices, exchange(): lax.ppermute(shard, axis, [(i, i ^ mask) for i in range(lax.axis_size(axi...  130 us
    ppermute x52, starting transfers between devices, exchange(): lax.ppermute(shard, axis, [(i, i ^ mask) for i in range(lax.axis_size(axi...  65.4 us
    pallas_call x4, Pallas kernels, in_weights(): pl.pallas_call(functools.partial(in_weights_kernel, first_steps), grid=(f...  32.4 us
    unnamed x52, local copies, waits for them, and re-layouts  13 us
    pallas_call x4, Pallas kernels, expert_parts(): pl.pallas_call(functools.partial(expert_kernel, part_count, full_width, l...  12.1 us
    pallas_call x2, Pallas kernels, out_weights(): pl.pallas_call(out_weights_kernel, grid=(width // tile,), in_specs=[pl.Bl...  8.94 us
  transfers between devices with their start and end apart: 52, of which 31 were waited for; matrix products, arithmetic and copies ran while one was open for 2% of the time, Pallas kernels for 18%

profile of v3, /device:TPU:0, one launch (start us, length us, event | category | flops | bytes accessed | tf_op | source)
XLA Modules:
  0.0 273.0 jit_solution(3312116277660526066)
XLA Ops:
  3.2 1.7 enter.1
  6.5 2.9 %collective-permute-start.8 = (f32[24,2048]{1,0:T(8,128)S(1)}, f32[24,2048]{1,0:T(8,128)S(1)}, u32[]{:S(2)}, u32[]{:S(2)}) collective-permute-start(f32[24,2048]{1,0:T(8,128)S(1)} %add.24), channel_id=1, source_target_pairs={{0,2},{1,3},{2,0},{3,1},{4,6},{5,7},{6,4},{7,5},{8,10},{9,11},{10,... | collective-permute-start | bytes 589832 | tf_op jit(solution)/shard_map/ppermute | solution.py:38
  12.9 2.6 collective-permute-start
  15.5 2.9 %collective-permute-start.1 = (bf16[48,2048]{1,0:T(8,128)(2,1)}, bf16[48,2048]{1,0:T(8,128)(2,1)}, u32[]{:S(2)}, u32[]{:S(2)}) collective-permute-start(bf16[48,2048]{1,0:T(8,128)(2,1)} %get-tuple-element.91), channel_id=1, source_target_pairs={{0,20},{4,16},{8,28},{12,24},{16,4},{20,0},{24,12},{28,8},{1,21},{... | collective-permute-start | bytes 589832 | tf_op jit(solution)/shard_map/ppermute | solution.py:38
  18.5 2.0 collective-permute-start.2
  20.5 5.8 %collective-permute-done.5 = bf16[48,2048]{1,0:T(8,128)(2,1)S(1)} collective-permute-done((bf16[48,2048]{1,0:T(8,128)(2,1)S(1)}, bf16[48,2048]{1,0:T(8,128)(2,1)S(1)}, u32[]{:S(2)}, u32[]{:S(2)}) %collective-permute-start.5) | collective-permute-done | bytes 196640 | tf_op jit(solution)/shard_map/ppermute | solution.py:38
  29.0 7.8 %in_weights.4 = bf16[32,256,256]{2,1,0:T(8,128)(2,1)} custom-call(s32[2,1,4096,256]{3,2,1,0:T(8,128)} %words_ref.9, s32[2,1,64,256]{3,2,1,0:T(8,128)} %scales_ref.7, bf16[256,256]{1,0:T(8,128)(2,1)} %constant.13.clone.table_ref), custom_call_target="tpu_custom_call" | custom-call | flops 1000 | bytes 1000 | tf_op jit(solution)/shard_map/in_weights/pallas_call | solution.py:121
  36.8 4.4 %out_weights.2.refs_8_ = bf16[256,8192]{1,0:T(8,128)(2,1)} custom-call(s32[2,1,128,8192]{3,2,1,0:T(8,128)} %words_ref.11, s32[2,1,2,8192]{3,2,1,0:T(2,128)} %scales_ref.9), custom_call_target="tpu_custom_call" | custom-call | flops 1000 | bytes 1000 | tf_op jit(solution)/shard_map/out_weights/pallas_call | solution.py:164
  41.2 8.7 %in_weights.5 = bf16[32,256,256]{2,1,0:T(8,128)(2,1)} custom-call(s32[2,1,4096,256]{3,2,1,0:T(8,128)} %words_ref.10, s32[2,1,64,256]{3,2,1,0:T(8,128)} %scales_ref.8, bf16[256,256]{1,0:T(8,128)(2,1)} %constant.13.clone.table_ref), custom_call_target="tpu_custom_call" | custom-call | flops 1000 | bytes 1000 | tf_op jit(solution)/shard_map/in_weights/pallas_call | solution.py:121
  57.6 2.2 copy-done.5
  62.1 3.1 %expert_parts.4 = (bf16[2,192,2048]{2,1,0:T(8,128)(2,1)S(1)}, bf16[2,192,2048]{2,1,0:T(8,128)(2,1)S(1)}) custom-call(s32[1]{0:T(128)} %bitcast.1.index_ref, bf16[192,2048]{1,0:T(8,128)(2,1)S(1)} %copy-done.12, bf16[192,2048]{1,0:T(8,128)(2,1)S(1)} %collective-permute-done.11.refs_1_, bf16[192,2048]{1,0:T(8,128)(2,1)S(1)} %copy-done.14, ...), custom_call_target="tpu_custom_call" | custom-call | flops 1000 | bytes 1000 | tf_op jit(solution)/shard_map/expert_parts/pallas_call | solution.py:215
  65.1 9.7 %collective-permute-done.9.refs_2_ = bf16[192,2048]{1,0:T(8,128)(2,1)S(1)} collective-permute-done((bf16[192,2048]{1,0:T(8,128)(2,1)S(1)}, bf16[192,2048]{1,0:T(8,128)(2,1)S(1)}, u32[]{:S(2)}, u32[]{:S(2)}) %collective-permute-start.9) | collective-permute-done | bytes 786464 | tf_op jit(solution)/shard_map/ppermute | solution.py:38
  75.4 1.8 collective-permute-done.13.refs_1_
  78.3 3.1 %expert_parts.5 = (bf16[2,192,2048]{2,1,0:T(8,128)(2,1)S(1)}, bf16[2,192,2048]{2,1,0:T(8,128)(2,1)S(1)}) custom-call(s32[1]{0:T(128)} %bitcast.1.index_ref, bf16[192,2048]{1,0:T(8,128)(2,1)S(1)} %constant_dynamic-update-slice_fusion.4.refs_0_, bf16[192,2048]{1,0:T(8,128)(2,1)S(1)} %collective-permute-done.13.refs_1_, ...), custom_call_target="tpu_custom_call" | custom-call | flops 1000 | bytes 1000 | tf_op jit(solution)/shard_map/expert_parts/pallas_call | solution.py:215
  81.9 2.9 %collective-permute-done.15.refs_1_ = bf16[2,192,2048]{2,1,0:T(8,128)(2,1)S(1)} collective-permute-done((bf16[2,192,2048]{2,1,0:T(8,128)(2,1)S(1)}, bf16[2,192,2048]{2,1,0:T(8,128)(2,1)S(1)}, u32[]{:S(2)}, u32[]{:S(2)}) %collective-permute-start.15) | collective-permute-done | bytes 1572896 | tf_op jit(solution)/shard_map/ppermute | solution.py:38
  89.6 8.0 %in_weights.6 = bf16[32,256,256]{2,1,0:T(8,128)(2,1)} custom-call(s32[2,1,4096,256]{3,2,1,0:T(8,128)} %words_ref.9, s32[2,1,64,256]{3,2,1,0:T(8,128)} %scales_ref.7, bf16[256,256]{1,0:T(8,128)(2,1)} %constant.13.clone.table_ref), custom_call_target="tpu_custom_call" | custom-call | flops 1000 | bytes 1000 | tf_op jit(solution)/shard_map/in_weights/pallas_call | solution.py:121
  97.6 8.0 %collective-permute-done.16.refs_2_ = bf16[1,192,2048]{2,1,0:T(8,128)(2,1)S(1)} collective-permute-done((bf16[1,192,2048]{2,1,0:T(8,128)(2,1)S(1)}, bf16[1,192,2048]{2,1,0:T(8,128)(2,1)S(1)}, u32[]{:S(2)}, u32[]{:S(2)}) %collective-permute-start.16) | collective-permute-done | bytes 786464 | tf_op jit(solution)/shard_map/ppermute | solution.py:38
  105.8 3.2 %collective-permute-start.22 = (bf16[48,2048]{1,0:T(8,128)(2,1)S(1)}, bf16[48,2048]{1,0:T(8,128)(2,1)S(1)}, u32[]{:S(2)}, u32[]{:S(2)}) collective-permute-start(bf16[48,2048]{1,0:T(8,128)(2,1)S(1)} %get-tuple-element.123), channel_id=1, source_target_pairs={{0,16},{4,20},{8,24},{12,28},{16,0},{20,4},{24,8},{28,12},{1,17},{... | collective-permute-start | bytes 589832 | tf_op jit(solution)/shard_map/ppermute | solution.py:38
  110.4 1.9 collective-permute-start.24
  113.8 7.9 %in_weights.7 = bf16[32,256,256]{2,1,0:T(8,128)(2,1)} custom-call(s32[2,1,4096,256]{3,2,1,0:T(8,128)} %words_ref.10, s32[2,1,64,256]{3,2,1,0:T(8,128)} %scales_ref.8, bf16[256,256]{1,0:T(8,128)(2,1)} %constant.13.clone.table_ref), custom_call_target="tpu_custom_call" | custom-call | flops 1000 | bytes 1000 | tf_op jit(solution)/shard_map/in_weights/pallas_call | solution.py:121
  122.0 2.1 collective-permute-start.19
  124.1 5.5 %collective-permute-done.22.refs_8_ = bf16[48,2048]{1,0:T(8,128)(2,1)S(1)} collective-permute-done((bf16[48,2048]{1,0:T(8,128)(2,1)S(1)}, bf16[48,2048]{1,0:T(8,128)(2,1)S(1)}, u32[]{:S(2)}, u32[]{:S(2)}) %collective-permute-start.22) | collective-permute-done | bytes 196640 | tf_op jit(solution)/shard_map/ppermute | solution.py:38
  130.2 4.0 %collective-permute-done.23.refs_9_ = bf16[48,2048]{1,0:T(8,128)(2,1)S(1)} collective-permute-done((bf16[48,2048]{1,0:T(8,128)(2,1)S(1)}, bf16[48,2048]{1,0:T(8,128)(2,1)S(1)}, u32[]{:S(2)}, u32[]{:S(2)}) %collective-permute-start.23) | collective-permute-done | bytes 196640 | tf_op jit(solution)/shard_map/ppermute | solution.py:38
  134.6 4.5 %out_weights.3.refs_8_ = bf16[256,8192]{1,0:T(8,128)(2,1)} custom-call(s32[2,1,128,8192]{3,2,1,0:T(8,128)} %words_ref.11, s32[2,1,2,8192]{3,2,1,0:T(2,128)} %scales_ref.9), custom_call_target="tpu_custom_call" | custom-call | flops 1000 | bytes 1000 | tf_op jit(solution)/shard_map/out_weights/pallas_call | solution.py:164
  139.2 3.3 %collective-permute-done.21.refs_7_ = bf16[48,2048]{1,0:T(8,128)(2,1)S(1)} collective-permute-done((bf16[48,2048]{1,0:T(8,128)(2,1)S(1)}, bf16[48,2048]{1,0:T(8,128)(2,1)S(1)}, u32[]{:S(2)}, u32[]{:S(2)}) %collective-permute-start.21) | collective-permute-done | bytes 196640 | tf_op jit(solution)/shard_map/ppermute | solution.py:38
  145.1 3.4 %collective-permute-start.29 = (bf16[48,2048]{1,0:T(8,128)(2,1)S(1)}, bf16[48,2048]{1,0:T(8,128)(2,1)S(1)}, u32[]{:S(2)}, u32[]{:S(2)}) collective-permute-start(bf16[48,2048]{1,0:T(8,128)(2,1)S(1)} %get-tuple-element.142), channel_id=1, source_target_pairs={{0,8},{4,12},{8,0},{12,4},{16,24},{20,28},{24,16},{28,20},{1,9},{5... | collective-permute-start | bytes 589832 | tf_op jit(solution)/shard_map/ppermute | solution.py:38
  148.9 2.4 collective-permute-start.32
  153.9 6.3 %collective-permute-done.29 = bf16[48,2048]{1,0:T(8,128)(2,1)S(1)} collective-permute-done((bf16[48,2048]{1,0:T(8,128)(2,1)S(1)}, bf16[48,2048]{1,0:T(8,128)(2,1)S(1)}, u32[]{:S(2)}, u32[]{:S(2)}) %collective-permute-start.29) | collective-permute-done | bytes 196640 | tf_op jit(solution)/shard_map/ppermute | solution.py:38
  160.2 3.7 %collective-permute-start.35 = (bf16[48,2048]{1,0:T(8,128)(2,1)S(1)}, bf16[48,2048]{1,0:T(8,128)(2,1)S(1)}, u32[]{:S(2)}, u32[]{:S(2)}) collective-permute-start(bf16[48,2048]{1,0:T(8,128)(2,1)S(1)} %get-tuple-element.147), channel_id=1, source_target_pairs={{0,28},{4,24},{8,20},{12,16},{16,12},{20,8},{24,4},{28,0},{1,29},{... | collective-permute-start | bytes 589832 | tf_op jit(solution)/shard_map/ppermute | solution.py:38
  164.5 1.6 collective-permute-start.31
  166.2 13.0 %collective-permute-done.33 = bf16[48,2048]{1,0:T(8,128)(2,1)S(1)} collective-permute-done((bf16[48,2048]{1,0:T(8,128)(2,1)S(1)}, bf16[48,2048]{1,0:T(8,128)(2,1)S(1)}, u32[]{:S(2)}, u32[]{:S(2)}) %collective-permute-start.33) | collective-permute-done | bytes 196640 | tf_op jit(solution)/shard_map/ppermute | solution.py:38
  179.3 3.9 %collective-permute-done.31.refs_2_ = bf16[192,2048]{1,0:T(8,128)(2,1)S(1)} collective-permute-done((bf16[192,2048]{1,0:T(8,128)(2,1)S(1)}, bf16[192,2048]{1,0:T(8,128)(2,1)S(1)}, u32[]{:S(2)}, u32[]{:S(2)}) %collective-permute-start.31) | collective-permute-done | bytes 786464 | tf_op jit(solution)/shard_map/ppermute | solution.py:38
  186.6 2.2 copy-done.2
  188.8 3.0 %expert_parts.6 = (bf16[2,192,2048]{2,1,0:T(8,128)(2,1)S(1)}, bf16[2,192,2048]{2,1,0:T(8,128)(2,1)S(1)}) custom-call(s32[1]{0:T(128)} %bitcast.1.index_ref, bf16[192,2048]{1,0:T(8,128)(2,1)S(1)} %constant_dynamic-update-slice_fusion.8.refs_0_, bf16[192,2048]{1,0:T(8,128)(2,1)S(1)} %collective-permute-done.36.refs_1_, ...), custom_call_target="tpu_custom_call" | custom-call | flops 1000 | bytes 1000 | tf_op jit(solution)/shard_map/expert_parts/pallas_call | solution.py:215
  191.7 11.4 %collective-permute-done.40.refs_2_ = bf16[192,2048]{1,0:T(8,128)(2,1)S(1)} collective-permute-done((bf16[192,2048]{1,0:T(8,128)(2,1)S(1)}, bf16[192,2048]{1,0:T(8,128)(2,1)S(1)}, u32[]{:S(2)}, u32[]{:S(2)}) %collective-permute-start.40) | collective-permute-done | bytes 786464 | tf_op jit(solution)/shard_map/ppermute | solution.py:38
  203.6 1.8 collective-permute-done.41.refs_1_
  206.5 3.0 %expert_parts.7 = (bf16[2,192,2048]{2,1,0:T(8,128)(2,1)S(1)}, bf16[2,192,2048]{2,1,0:T(8,128)(2,1)S(1)}) custom-call(s32[1]{0:T(128)} %bitcast.1.index_ref, bf16[192,2048]{1,0:T(8,128)(2,1)S(1)} %constant_dynamic-update-slice_fusion.12.refs_0_, bf16[192,2048]{1,0:T(8,128)(2,1)S(1)} %collective-permute-done.41.refs_1_, ...), custom_call_target="tpu_custom_call" | custom-call | flops 1000 | bytes 1000 | tf_op jit(solution)/shard_map/expert_parts/pallas_call | solution.py:215
  210.1 2.9 %collective-permute-done.43.refs_1_ = bf16[2,192,2048]{2,1,0:T(8,128)(2,1)S(1)} collective-permute-done((bf16[2,192,2048]{2,1,0:T(8,128)(2,1)S(1)}, bf16[2,192,2048]{2,1,0:T(8,128)(2,1)S(1)}, u32[]{:S(2)}, u32[]{:S(2)}) %collective-permute-start.43) | collective-permute-done | bytes 1572896 | tf_op jit(solution)/shard_map/ppermute | solution.py:38
  217.1 16.6 %collective-permute-done.44.refs_2_ = bf16[1,192,2048]{2,1,0:T(8,128)(2,1)S(1)} collective-permute-done((bf16[1,192,2048]{2,1,0:T(8,128)(2,1)S(1)}, bf16[1,192,2048]{2,1,0:T(8,128)(2,1)S(1)}, u32[]{:S(2)}, u32[]{:S(2)}) %collective-permute-start.44) | collective-permute-done | bytes 786464 | tf_op jit(solution)/shard_map/ppermute | solution.py:38
  234.0 3.7 %collective-permute-start.48 = (bf16[48,2048]{1,0:T(8,128)(2,1)S(1)}, bf16[48,2048]{1,0:T(8,128)(2,1)S(1)}, u32[]{:S(2)}, u32[]{:S(2)}) collective-permute-start(bf16[48,2048]{1,0:T(8,128)(2,1)S(1)} %get-tuple-element.164), channel_id=1, source_target_pairs={{0,16},{4,20},{8,24},{12,28},{16,0},{20,4},{24,8},{28,12},{1,17},{... | collective-permute-start | bytes 589832 | tf_op jit(solution)/shard_map/ppermute | solution.py:38
  239.3 1.7 collective-permute-start.27
  241.1 1.7 collective-permute-start.50
  242.7 7.1 %collective-permute-done.39.refs_2_ = bf16[1,192,2048]{2,1,0:T(8,128)(2,1)S(1)} collective-permute-done((bf16[1,192,2048]{2,1,0:T(8,128)(2,1)S(1)}, bf16[1,192,2048]{2,1,0:T(8,128)(2,1)S(1)}, u32[]{:S(2)}, u32[]{:S(2)}) %collective-permute-start.39) | collective-permute-done | bytes 786464 | tf_op jit(solution)/shard_map/ppermute | solution.py:38
  251.3 2.3 collective-permute-start.45
  253.6 6.7 %collective-permute-done.48.refs_8_ = bf16[48,2048]{1,0:T(8,128)(2,1)S(1)} collective-permute-done((bf16[48,2048]{1,0:T(8,128)(2,1)S(1)}, bf16[48,2048]{1,0:T(8,128)(2,1)S(1)}, u32[]{:S(2)}, u32[]{:S(2)}) %collective-permute-start.48) | collective-permute-done | bytes 196640 | tf_op jit(solution)/shard_map/ppermute | solution.py:38
  260.2 4.6 %collective-permute-done.49.refs_9_ = bf16[48,2048]{1,0:T(8,128)(2,1)S(1)} collective-permute-done((bf16[48,2048]{1,0:T(8,128)(2,1)S(1)}, bf16[48,2048]{1,0:T(8,128)(2,1)S(1)}, u32[]{:S(2)}, u32[]{:S(2)}) %collective-permute-start.49) | collective-permute-done | bytes 196640 | tf_op jit(solution)/shard_map/ppermute | solution.py:38
  265.8 2.6 collective-permute-done.46.refs_6_
  268.4 3.0 %collective-permute-done.47.refs_7_ = bf16[48,2048]{1,0:T(8,128)(2,1)S(1)} collective-permute-done((bf16[48,2048]{1,0:T(8,128)(2,1)S(1)}, bf16[48,2048]{1,0:T(8,128)(2,1)S(1)}, u32[]{:S(2)}, u32[]{:S(2)}) %collective-permute-start.47) | collective-permute-done | bytes 196640 | tf_op jit(solution)/shard_map/ppermute | solution.py:38
  (141 shorter events, 54.3 us)
Async XLA Ops:
  6.5 9.0 %collective-permute-start.8 = (f32[24,2048]{1,0:T(8,128)S(1)}, f32[24,2048]{1,0:T(8,128)S(1)}, u32[]{:S(2)}, u32[]{:S(2)}) collective-permute-start(f32[24,2048]{1,0:T(8,128)S(1)} %add.24), channel_id=1, source_target_pairs={{0,2},{1,3},{2,0},{3,1},{4,6},{5,7},{6,4},{7,5},{8,10},{9,11},{10,... | collective-permute-start | bytes 589832 | tf_op jit(solution)/shard_map/ppermute | solution.py:38
  9.4 9.1 %collective-permute-start.4 = (bf16[48,2048]{1,0:T(8,128)(2,1)S(1)}, bf16[48,2048]{1,0:T(8,128)(2,1)S(1)}, u32[]{:S(2)}, u32[]{:S(2)}) collective-permute-start(bf16[48,2048]{1,0:T(8,128)(2,1)S(1)} %get-tuple-element.95), channel_id=1, source_target_pairs={{0,4},{4,0},{8,12},{12,8},{16,20},{20,16},{24,28},{28,24},{1,5},{5... | collective-permute-start | bytes 589832 | tf_op jit(solution)/shard_map/ppermute | solution.py:38
  10.9 15.4 %collective-permute-start.5 = (bf16[48,2048]{1,0:T(8,128)(2,1)S(1)}, bf16[48,2048]{1,0:T(8,128)(2,1)S(1)}, u32[]{:S(2)}, u32[]{:S(2)}) collective-permute-start(bf16[48,2048]{1,0:T(8,128)(2,1)S(1)} %get-tuple-element.96), channel_id=1, source_target_pairs={{0,8},{4,12},{8,0},{12,4},{16,24},{20,28},{24,16},{28,20},{1,9},{5... | collective-permute-start | bytes 589832 | tf_op jit(solution)/shard_map/ppermute | solution.py:38
  12.5 15.7 %collective-permute-start.6 = (bf16[48,2048]{1,0:T(8,128)(2,1)S(1)}, bf16[48,2048]{1,0:T(8,128)(2,1)S(1)}, u32[]{:S(2)}, u32[]{:S(2)}) collective-permute-start(bf16[48,2048]{1,0:T(8,128)(2,1)S(1)} %get-tuple-element.97), channel_id=1, source_target_pairs={{0,12},{4,8},{8,4},{12,0},{16,28},{20,24},{24,20},{28,16},{1,13},{... | collective-permute-start | bytes 589832 | tf_op jit(solution)/shard_map/ppermute | solution.py:38
  12.9 37.0 %collective-permute-start = (bf16[48,2048]{1,0:T(8,128)(2,1)}, bf16[48,2048]{1,0:T(8,128)(2,1)}, u32[]{:S(2)}, u32[]{:S(2)}) collective-permute-start(bf16[48,2048]{1,0:T(8,128)(2,1)} %get-tuple-element.90), channel_id=1, source_target_pairs={{0,16},{4,20},{8,24},{12,28},{16,0},{20,4},{24,8},{28,12},{1,17},{... | collective-permute-start | bytes 589832 | tf_op jit(solution)/shard_map/ppermute | solution.py:38
  15.5 34.5 %collective-permute-start.1 = (bf16[48,2048]{1,0:T(8,128)(2,1)}, bf16[48,2048]{1,0:T(8,128)(2,1)}, u32[]{:S(2)}, u32[]{:S(2)}) collective-permute-start(bf16[48,2048]{1,0:T(8,128)(2,1)} %get-tuple-element.91), channel_id=1, source_target_pairs={{0,20},{4,16},{8,28},{12,24},{16,4},{20,0},{24,12},{28,8},{1,21},{... | collective-permute-start | bytes 589832 | tf_op jit(solution)/shard_map/ppermute | solution.py:38
  18.5 31.5 %collective-permute-start.2 = (bf16[48,2048]{1,0:T(8,128)(2,1)}, bf16[48,2048]{1,0:T(8,128)(2,1)}, u32[]{:S(2)}, u32[]{:S(2)}) collective-permute-start(bf16[48,2048]{1,0:T(8,128)(2,1)} %get-tuple-element.92), channel_id=1, source_target_pairs={{0,24},{4,28},{8,16},{12,20},{16,8},{20,12},{24,0},{28,4},{1,25},{... | collective-permute-start | bytes 589832 | tf_op jit(solution)/shard_map/ppermute | solution.py:38
  26.3 23.7 %collective-permute-start.3 = (bf16[48,2048]{1,0:T(8,128)(2,1)}, bf16[48,2048]{1,0:T(8,128)(2,1)}, u32[]{:S(2)}, u32[]{:S(2)}) collective-permute-start(bf16[48,2048]{1,0:T(8,128)(2,1)} %get-tuple-element.93), channel_id=1, source_target_pairs={{0,28},{4,24},{8,20},{12,16},{16,12},{20,8},{24,4},{28,0},{1,29},{... | collective-permute-start | bytes 589832 | tf_op jit(solution)/shard_map/ppermute | solution.py:38
  28.3 24.6 %collective-permute-start.10 = (bf16[192,2048]{1,0:T(8,128)(2,1)S(1)}, bf16[192,2048]{1,0:T(8,128)(2,1)S(1)}, u32[]{:S(2)}, u32[]{:S(2)}) collective-permute-start(bf16[192,2048]{1,0:T(8,128)(2,1)S(1)} %constant_dynamic-update-slice_fusion.refs_0_), channel_id=1, source_target_pairs={{0,2},{1,3},{2,0},{3,1},{4,6},{5,7},{6,4},{7,5},{8,10},{9,11},{10,... | collective-permute-start | bytes 2359304 | tf_op jit(solution)/shard_map/ppermute | solution.py:38
  52.9 4.7 %collective-permute-start.11 = (bf16[192,2048]{1,0:T(8,128)(2,1)S(1)}, bf16[192,2048]{1,0:T(8,128)(2,1)S(1)}, u32[]{:S(2)}, u32[]{:S(2)}) collective-permute-start(bf16[192,2048]{1,0:T(8,128)(2,1)S(1)} %constant_dynamic-update-slice_fusion.refs_0_), channel_id=1, source_target_pairs={{0,1},{1,0},{2,3},{3,2},{4,5},{5,4},{6,7},{7,6},{8,9},{9,8},{10,11... | collective-permute-start | bytes 2359304 | tf_op jit(solution)/shard_map/ppermute | solution.py:38
  52.9 4.6 %collective-permute-start.12 = (bf16[192,2048]{1,0:T(8,128)(2,1)S(1)}, bf16[192,2048]{1,0:T(8,128)(2,1)S(1)}, u32[]{:S(2)}, u32[]{:S(2)}) collective-permute-start(bf16[192,2048]{1,0:T(8,128)(2,1)S(1)} %collective-permute-done.10.refs_2_), channel_id=1, source_target_pairs={{0,1},{1,0},{2,3},{3,2},{4,5},{5,4},{6,7},{7,6},{8,9},{9,8},{10,11... | collective-permute-start | bytes 2359304 | tf_op jit(solution)/shard_map/ppermute | solution.py:38
  55.3 19.6 %collective-permute-start.9 = (bf16[192,2048]{1,0:T(8,128)(2,1)S(1)}, bf16[192,2048]{1,0:T(8,128)(2,1)S(1)}, u32[]{:S(2)}, u32[]{:S(2)}) collective-permute-start(bf16[192,2048]{1,0:T(8,128)(2,1)S(1)} %constant_dynamic-update-slice_fusion.4.refs_0_), channel_id=1, source_target_pairs={{0,2},{1,3},{2,0},{3,1},{4,6},{5,7},{6,4},{7,5},{8,10},{9,11},{10,... | collective-permute-start | bytes 2359304 | tf_op jit(solution)/shard_map/ppermute | solution.py:38
  74.8 2.3 collective-permute-start.13
  74.9 3.4 %collective-permute-start.14 = (bf16[192,2048]{1,0:T(8,128)(2,1)S(1)}, bf16[192,2048]{1,0:T(8,128)(2,1)S(1)}, u32[]{:S(2)}, u32[]{:S(2)}) collective-permute-start(bf16[192,2048]{1,0:T(8,128)(2,1)S(1)} %collective-permute-done.9.refs_2_), channel_id=1, source_target_pairs={{0,1},{1,0},{2,3},{3,2},{4,5},{5,4},{6,7},{7,6},{8,9},{9,8},{10,11... | collective-permute-start | bytes 2359304 | tf_op jit(solution)/shard_map/ppermute | solution.py:38
  81.3 3.5 %collective-permute-start.15 = (bf16[2,192,2048]{2,1,0:T(8,128)(2,1)S(1)}, bf16[2,192,2048]{2,1,0:T(8,128)(2,1)S(1)}, u32[]{:S(2)}, u32[]{:S(2)}) collective-permute-start(bf16[2,192,2048]{2,1,0:T(8,128)(2,1)S(1)} %get-tuple-element.117), channel_id=1, source_target_pairs={{0,1},{1,0},{2,3},{3,2},{4,5},{5,4},{6,7},{7,6},{8,9},{9,8},{10,11... | collective-permute-start | bytes 4718600 | tf_op jit(solution)/shard_map/ppermute | solution.py:38
  81.6 5.5 %collective-permute-start.17 = (bf16[2,192,2048]{2,1,0:T(8,128)(2,1)S(1)}, bf16[2,192,2048]{2,1,0:T(8,128)(2,1)S(1)}, u32[]{:S(2)}, u32[]{:S(2)}) collective-permute-start(bf16[2,192,2048]{2,1,0:T(8,128)(2,1)S(1)} %get-tuple-element.112), channel_id=1, source_target_pairs={{0,1},{1,0},{2,3},{3,2},{4,5},{5,4},{6,7},{7,6},{8,9},{9,8},{10,11... | collective-permute-start | bytes 4718600 | tf_op jit(solution)/shard_map/ppermute | solution.py:38
  85.1 20.4 %collective-permute-start.16 = (bf16[1,192,2048]{2,1,0:T(8,128)(2,1)S(1)}, bf16[1,192,2048]{2,1,0:T(8,128)(2,1)S(1)}, u32[]{:S(2)}, u32[]{:S(2)}) collective-permute-start(bf16[1,192,2048]{2,1,0:T(8,128)(2,1)S(1)} %add_convert_fusion.3), channel_id=1, source_target_pairs={{0,2},{1,3},{2,0},{3,1},{4,6},{5,7},{6,4},{7,5},{8,10},{9,11},{10,... | collective-permute-start | bytes 2359304 | tf_op jit(solution)/shard_map/ppermute | solution.py:38
  88.2 33.5 %collective-permute-start.18 = (bf16[1,192,2048]{2,1,0:T(8,128)(2,1)}, bf16[1,192,2048]{2,1,0:T(8,128)(2,1)S(1)}, u32[]{:S(2)}, u32[]{:S(2)}) collective-permute-start(bf16[1,192,2048]{2,1,0:T(8,128)(2,1)} %add_convert_fusion.2), channel_id=1, source_target_pairs={{0,2},{1,3},{2,0},{3,1},{4,6},{5,7},{6,4},{7,5},{8,10},{9,11},{10,... | collective-permute-start | bytes 2359304 | tf_op jit(solution)/shard_map/ppermute | solution.py:38
  105.8 23.7 %collective-permute-start.22 = (bf16[48,2048]{1,0:T(8,128)(2,1)S(1)}, bf16[48,2048]{1,0:T(8,128)(2,1)S(1)}, u32[]{:S(2)}, u32[]{:S(2)}) collective-permute-start(bf16[48,2048]{1,0:T(8,128)(2,1)S(1)} %get-tuple-element.123), channel_id=1, source_target_pairs={{0,16},{4,20},{8,24},{12,28},{16,0},{20,4},{24,8},{28,12},{1,17},{... | collective-permute-start | bytes 589832 | tf_op jit(solution)/shard_map/ppermute | solution.py:38
  109.0 25.2 %collective-permute-start.23 = (bf16[48,2048]{1,0:T(8,128)(2,1)S(1)}, bf16[48,2048]{1,0:T(8,128)(2,1)S(1)}, u32[]{:S(2)}, u32[]{:S(2)}) collective-permute-start(bf16[48,2048]{1,0:T(8,128)(2,1)S(1)} %get-tuple-element.124), channel_id=1, source_target_pairs={{0,20},{4,16},{8,28},{12,24},{16,4},{20,0},{24,12},{28,8},{1,21},{... | collective-permute-start | bytes 589832 | tf_op jit(solution)/shard_map/ppermute | solution.py:38
  110.4 28.8 %collective-permute-start.24 = (bf16[48,2048]{1,0:T(8,128)(2,1)S(1)}, bf16[48,2048]{1,0:T(8,128)(2,1)S(1)}, u32[]{:S(2)}, u32[]{:S(2)}) collective-permute-start(bf16[48,2048]{1,0:T(8,128)(2,1)S(1)} %get-tuple-element.125), channel_id=1, source_target_pairs={{0,24},{4,28},{8,16},{12,20},{16,8},{20,12},{24,0},{28,4},{1,25},{... | collective-permute-start | bytes 589832 | tf_op jit(solution)/shard_map/ppermute | solution.py:38
  112.3 26.9 %collective-permute-start.25 = (bf16[48,2048]{1,0:T(8,128)(2,1)S(1)}, bf16[48,2048]{1,0:T(8,128)(2,1)S(1)}, u32[]{:S(2)}, u32[]{:S(2)}) collective-permute-start(bf16[48,2048]{1,0:T(8,128)(2,1)S(1)} %get-tuple-element.126), channel_id=1, source_target_pairs={{0,28},{4,24},{8,20},{12,16},{16,12},{20,8},{24,4},{28,0},{1,29},{... | collective-permute-start | bytes 589832 | tf_op jit(solution)/shard_map/ppermute | solution.py:38
  122.0 17.2 %collective-permute-start.19 = (bf16[48,2048]{1,0:T(8,128)(2,1)S(1)}, bf16[48,2048]{1,0:T(8,128)(2,1)S(1)}, u32[]{:S(2)}, u32[]{:S(2)}) collective-permute-start(bf16[48,2048]{1,0:T(8,128)(2,1)S(1)} %get-tuple-element.132), channel_id=1, source_target_pairs={{0,4},{4,0},{8,12},{12,8},{16,20},{20,16},{24,28},{28,24},{1,5},{5... | collective-permute-start | bytes 589832 | tf_op jit(solution)/shard_map/ppermute | solution.py:38
  129.5 9.7 %collective-permute-start.20 = (bf16[48,2048]{1,0:T(8,128)(2,1)S(1)}, bf16[48,2048]{1,0:T(8,128)(2,1)S(1)}, u32[]{:S(2)}, u32[]{:S(2)}) collective-permute-start(bf16[48,2048]{1,0:T(8,128)(2,1)S(1)} %get-tuple-element.133), channel_id=1, source_target_pairs={{0,8},{4,12},{8,0},{12,4},{16,24},{20,28},{24,16},{28,20},{1,9},{5... | collective-permute-start | bytes 589832 | tf_op jit(solution)/shard_map/ppermute | solution.py:38
  134.2 8.3 %collective-permute-start.21 = (bf16[48,2048]{1,0:T(8,128)(2,1)S(1)}, bf16[48,2048]{1,0:T(8,128)(2,1)S(1)}, u32[]{:S(2)}, u32[]{:S(2)}) collective-permute-start(bf16[48,2048]{1,0:T(8,128)(2,1)S(1)} %get-tuple-element.134), channel_id=1, source_target_pairs={{0,12},{4,8},{8,4},{12,0},{16,28},{20,24},{24,20},{28,16},{1,13},{... | collective-permute-start | bytes 589832 | tf_op jit(solution)/shard_map/ppermute | solution.py:38
  144.1 8.3 %collective-permute-start.28 = (bf16[48,2048]{1,0:T(8,128)(2,1)S(1)}, bf16[48,2048]{1,0:T(8,128)(2,1)S(1)}, u32[]{:S(2)}, u32[]{:S(2)}) collective-permute-start(bf16[48,2048]{1,0:T(8,128)(2,1)S(1)} %get-tuple-element.141), channel_id=1, source_target_pairs={{0,4},{4,0},{8,12},{12,8},{16,20},{20,16},{24,28},{28,24},{1,5},{5... | collective-permute-start | bytes 589832 | tf_op jit(solution)/shard_map/ppermute | solution.py:38
  145.1 15.1 %collective-permute-start.29 = (bf16[48,2048]{1,0:T(8,128)(2,1)S(1)}, bf16[48,2048]{1,0:T(8,128)(2,1)S(1)}, u32[]{:S(2)}, u32[]{:S(2)}) collective-permute-start(bf16[48,2048]{1,0:T(8,128)(2,1)S(1)} %get-tuple-element.142), channel_id=1, source_target_pairs={{0,8},{4,12},{8,0},{12,4},{16,24},{20,28},{24,16},{28,20},{1,9},{5... | collective-permute-start | bytes 589832 | tf_op jit(solution)/shard_map/ppermute | solution.py:38
  148.5 16.0 %collective-permute-start.30 = (bf16[48,2048]{1,0:T(8,128)(2,1)S(1)}, bf16[48,2048]{1,0:T(8,128)(2,1)S(1)}, u32[]{:S(2)}, u32[]{:S(2)}) collective-permute-start(bf16[48,2048]{1,0:T(8,128)(2,1)S(1)} %get-tuple-element.143), channel_id=1, source_target_pairs={{0,12},{4,8},{8,4},{12,0},{16,28},{20,24},{24,20},{28,16},{1,13},{... | collective-permute-start | bytes 589832 | tf_op jit(solution)/shard_map/ppermute | solution.py:38
  148.9 17.3 %collective-permute-start.32 = (bf16[48,2048]{1,0:T(8,128)(2,1)S(1)}, bf16[48,2048]{1,0:T(8,128)(2,1)S(1)}, u32[]{:S(2)}, u32[]{:S(2)}) collective-permute-start(bf16[48,2048]{1,0:T(8,128)(2,1)S(1)} %get-tuple-element.144), channel_id=1, source_target_pairs={{0,16},{4,20},{8,24},{12,28},{16,0},{20,4},{24,8},{28,12},{1,17},{... | collective-permute-start | bytes 589832 | tf_op jit(solution)/shard_map/ppermute | solution.py:38
  151.3 27.9 %collective-permute-start.33 = (bf16[48,2048]{1,0:T(8,128)(2,1)S(1)}, bf16[48,2048]{1,0:T(8,128)(2,1)S(1)}, u32[]{:S(2)}, u32[]{:S(2)}) collective-permute-start(bf16[48,2048]{1,0:T(8,128)(2,1)S(1)} %get-tuple-element.145), channel_id=1, source_target_pairs={{0,20},{4,16},{8,28},{12,24},{16,4},{20,0},{24,12},{28,8},{1,21},{... | collective-permute-start | bytes 589832 | tf_op jit(solution)/shard_map/ppermute | solution.py:38
  152.4 26.9 %collective-permute-start.34 = (bf16[48,2048]{1,0:T(8,128)(2,1)S(1)}, bf16[48,2048]{1,0:T(8,128)(2,1)S(1)}, u32[]{:S(2)}, u32[]{:S(2)}) collective-permute-start(bf16[48,2048]{1,0:T(8,128)(2,1)S(1)} %get-tuple-element.146), channel_id=1, source_target_pairs={{0,24},{4,28},{8,16},{12,20},{16,8},{20,12},{24,0},{28,4},{1,25},{... | collective-permute-start | bytes 589832 | tf_op jit(solution)/shard_map/ppermute | solution.py:38
  160.2 19.1 %collective-permute-start.35 = (bf16[48,2048]{1,0:T(8,128)(2,1)S(1)}, bf16[48,2048]{1,0:T(8,128)(2,1)S(1)}, u32[]{:S(2)}, u32[]{:S(2)}) collective-permute-start(bf16[48,2048]{1,0:T(8,128)(2,1)S(1)} %get-tuple-element.147), channel_id=1, source_target_pairs={{0,28},{4,24},{8,20},{12,16},{16,12},{20,8},{24,4},{28,0},{1,29},{... | collective-permute-start | bytes 589832 | tf_op jit(solution)/shard_map/ppermute | solution.py:38
  164.5 18.6 %collective-permute-start.31 = (bf16[192,2048]{1,0:T(8,128)(2,1)S(1)}, bf16[192,2048]{1,0:T(8,128)(2,1)S(1)}, u32[]{:S(2)}, u32[]{:S(2)}) collective-permute-start(bf16[192,2048]{1,0:T(8,128)(2,1)S(1)} %constant_dynamic-update-slice_fusion.8.refs_0_), channel_id=1, source_target_pairs={{0,2},{1,3},{2,0},{3,1},{4,6},{5,7},{6,4},{7,5},{8,10},{9,11},{10,... | collective-permute-start | bytes 2359304 | tf_op jit(solution)/shard_map/ppermute | solution.py:38
  183.1 3.4 %collective-permute-start.37 = (bf16[192,2048]{1,0:T(8,128)(2,1)S(1)}, bf16[192,2048]{1,0:T(8,128)(2,1)S(1)}, u32[]{:S(2)}, u32[]{:S(2)}) collective-permute-start(bf16[192,2048]{1,0:T(8,128)(2,1)S(1)} %collective-permute-done.31.refs_2_), channel_id=1, source_target_pairs={{0,1},{1,0},{2,3},{3,2},{4,5},{5,4},{6,7},{7,6},{8,9},{9,8},{10,11... | collective-permute-start | bytes 2359304 | tf_op jit(solution)/shard_map/ppermute | solution.py:38
  183.7 19.4 %collective-permute-start.40 = (bf16[192,2048]{1,0:T(8,128)(2,1)S(1)}, bf16[192,2048]{1,0:T(8,128)(2,1)S(1)}, u32[]{:S(2)}, u32[]{:S(2)}) collective-permute-start(bf16[192,2048]{1,0:T(8,128)(2,1)S(1)} %constant_dynamic-update-slice_fusion.12.refs_0_), channel_id=1, source_target_pairs={{0,2},{1,3},{2,0},{3,1},{4,6},{5,7},{6,4},{7,5},{8,10},{9,11},{10,... | collective-permute-start | bytes 2359304 | tf_op jit(solution)/shard_map/ppermute | solution.py:38
  203.1 3.4 %collective-permute-start.42 = (bf16[192,2048]{1,0:T(8,128)(2,1)S(1)}, bf16[192,2048]{1,0:T(8,128)(2,1)S(1)}, u32[]{:S(2)}, u32[]{:S(2)}) collective-permute-start(bf16[192,2048]{1,0:T(8,128)(2,1)S(1)} %collective-permute-done.40.refs_2_), channel_id=1, source_target_pairs={{0,1},{1,0},{2,3},{3,2},{4,5},{5,4},{6,7},{7,6},{8,9},{9,8},{10,11... | collective-permute-start | bytes 2359304 | tf_op jit(solution)/shard_map/ppermute | solution.py:38
  209.5 3.5 %collective-permute-start.43 = (bf16[2,192,2048]{2,1,0:T(8,128)(2,1)S(1)}, bf16[2,192,2048]{2,1,0:T(8,128)(2,1)S(1)}, u32[]{:S(2)}, u32[]{:S(2)}) collective-permute-start(bf16[2,192,2048]{2,1,0:T(8,128)(2,1)S(1)} %get-tuple-element.159), channel_id=1, source_target_pairs={{0,1},{1,0},{2,3},{3,2},{4,5},{5,4},{6,7},{7,6},{8,9},{9,8},{10,11... | collective-permute-start | bytes 4718600 | tf_op jit(solution)/shard_map/ppermute | solution.py:38
  209.7 5.5 %collective-permute-start.38 = (bf16[2,192,2048]{2,1,0:T(8,128)(2,1)S(1)}, bf16[2,192,2048]{2,1,0:T(8,128)(2,1)S(1)}, u32[]{:S(2)}, u32[]{:S(2)}) collective-permute-start(bf16[2,192,2048]{2,1,0:T(8,128)(2,1)S(1)} %get-tuple-element.153), channel_id=1, source_target_pairs={{0,1},{1,0},{2,3},{3,2},{4,5},{5,4},{6,7},{7,6},{8,9},{9,8},{10,11... | collective-permute-start | bytes 4718600 | tf_op jit(solution)/shard_map/ppermute | solution.py:38
  213.3 20.4 %collective-permute-start.44 = (bf16[1,192,2048]{2,1,0:T(8,128)(2,1)S(1)}, bf16[1,192,2048]{2,1,0:T(8,128)(2,1)S(1)}, u32[]{:S(2)}, u32[]{:S(2)}) collective-permute-start(bf16[1,192,2048]{2,1,0:T(8,128)(2,1)S(1)} %add_convert_fusion), channel_id=1, source_target_pairs={{0,2},{1,3},{2,0},{3,1},{4,6},{5,7},{6,4},{7,5},{8,10},{9,11},{10,... | collective-permute-start | bytes 2359304 | tf_op jit(solution)/shard_map/ppermute | solution.py:38
  215.5 34.3 %collective-permute-start.39 = (bf16[1,192,2048]{2,1,0:T(8,128)(2,1)S(1)}, bf16[1,192,2048]{2,1,0:T(8,128)(2,1)S(1)}, u32[]{:S(2)}, u32[]{:S(2)}) collective-permute-start(bf16[1,192,2048]{2,1,0:T(8,128)(2,1)S(1)} %add_convert_fusion.1), channel_id=1, source_target_pairs={{0,2},{1,3},{2,0},{3,1},{4,6},{5,7},{6,4},{7,5},{8,10},{9,11},{10,... | collective-permute-start | bytes 2359304 | tf_op jit(solution)/shard_map/ppermute | solution.py:38
  234.0 26.2 %collective-permute-start.48 = (bf16[48,2048]{1,0:T(8,128)(2,1)S(1)}, bf16[48,2048]{1,0:T(8,128)(2,1)S(1)}, u32[]{:S(2)}, u32[]{:S(2)}) collective-permute-start(bf16[48,2048]{1,0:T(8,128)(2,1)S(1)} %get-tuple-element.164), channel_id=1, source_target_pairs={{0,16},{4,20},{8,24},{12,28},{16,0},{20,4},{24,8},{28,12},{1,17},{... | collective-permute-start | bytes 589832 | tf_op jit(solution)/shard_map/ppermute | solution.py:38
  237.6 27.2 %collective-permute-start.49 = (bf16[48,2048]{1,0:T(8,128)(2,1)S(1)}, bf16[48,2048]{1,0:T(8,128)(2,1)S(1)}, u32[]{:S(2)}, u32[]{:S(2)}) collective-permute-start(bf16[48,2048]{1,0:T(8,128)(2,1)S(1)} %get-tuple-element.165), channel_id=1, source_target_pairs={{0,20},{4,16},{8,28},{12,24},{16,4},{20,0},{24,12},{28,8},{1,21},{... | collective-permute-start | bytes 589832 | tf_op jit(solution)/shard_map/ppermute | solution.py:38
  239.3 11.9 %collective-permute-start.27 = (f32[16,128]{1,0:T(8,128)S(1)}, f32[16,128]{1,0:T(8,128)S(1)}, u32[]{:S(2)}, u32[]{:S(2)}) collective-permute-start(f32[16,128]{1,0:T(8,128)S(1)} %add.28), channel_id=1, source_target_pairs={{0,2},{1,3},{2,0},{3,1},{4,6},{5,7},{6,4},{7,5},{8,10},{9,11},{10,... | collective-permute-start | bytes 24584 | tf_op jit(solution)/shard_map/ppermute | solution.py:38
  241.1 23.8 %collective-permute-start.50 = (bf16[48,2048]{1,0:T(8,128)(2,1)S(1)}, bf16[48,2048]{1,0:T(8,128)(2,1)S(1)}, u32[]{:S(2)}, u32[]{:S(2)}) collective-permute-start(bf16[48,2048]{1,0:T(8,128)(2,1)S(1)} %get-tuple-element.166), channel_id=1, source_target_pairs={{0,24},{4,28},{8,16},{12,20},{16,8},{20,12},{24,0},{28,4},{1,25},{... | collective-permute-start | bytes 589832 | tf_op jit(solution)/shard_map/ppermute | solution.py:38
  249.8 15.0 %collective-permute-start.51 = (bf16[48,2048]{1,0:T(8,128)(2,1)S(1)}, bf16[48,2048]{1,0:T(8,128)(2,1)S(1)}, u32[]{:S(2)}, u32[]{:S(2)}) collective-permute-start(bf16[48,2048]{1,0:T(8,128)(2,1)S(1)} %get-tuple-element.167), channel_id=1, source_target_pairs={{0,28},{4,24},{8,20},{12,16},{16,12},{20,8},{24,4},{28,0},{1,29},{... | collective-permute-start | bytes 589832 | tf_op jit(solution)/shard_map/ppermute | solution.py:38
  251.3 14.5 %collective-permute-start.45 = (bf16[48,2048]{1,0:T(8,128)(2,1)S(1)}, bf16[48,2048]{1,0:T(8,128)(2,1)S(1)}, u32[]{:S(2)}, u32[]{:S(2)}) collective-permute-start(bf16[48,2048]{1,0:T(8,128)(2,1)S(1)} %get-tuple-element.172), channel_id=1, source_target_pairs={{0,4},{4,0},{8,12},{12,8},{16,20},{20,16},{24,28},{28,24},{1,5},{5... | collective-permute-start | bytes 589832 | tf_op jit(solution)/shard_map/ppermute | solution.py:38
  260.2 8.1 %collective-permute-start.46 = (bf16[48,2048]{1,0:T(8,128)(2,1)S(1)}, bf16[48,2048]{1,0:T(8,128)(2,1)S(1)}, u32[]{:S(2)}, u32[]{:S(2)}) collective-permute-start(bf16[48,2048]{1,0:T(8,128)(2,1)S(1)} %get-tuple-element.173), channel_id=1, source_target_pairs={{0,8},{4,12},{8,0},{12,4},{16,24},{20,28},{24,16},{28,20},{1,9},{5... | collective-permute-start | bytes 589832 | tf_op jit(solution)/shard_map/ppermute | solution.py:38
  264.8 6.6 %collective-permute-start.47 = (bf16[48,2048]{1,0:T(8,128)(2,1)S(1)}, bf16[48,2048]{1,0:T(8,128)(2,1)S(1)}, u32[]{:S(2)}, u32[]{:S(2)}) collective-permute-start(bf16[48,2048]{1,0:T(8,128)(2,1)S(1)} %get-tuple-element.174), channel_id=1, source_target_pairs={{0,12},{4,8},{8,4},{12,0},{16,28},{20,24},{24,20},{28,16},{1,13},{... | collective-permute-start | bytes 589832 | tf_op jit(solution)/shard_map/ppermute | solution.py:38
  (24 other events, 239.6 us)
